TPU v7x, 32 devices: a whole 2x2x4 slice. The times are simulated.
32 devices in a mesh: island: 2 (over y), fsdp: 16 (over z, x, core).
Axes of the slice: x: 2, y: 2, z: 4, core: 2. Of those that a mesh axis runs over, the one named last changes fastest.
Arguments:
- tokens: bfloat16 [4096, 8192], P(('island', 'fsdp')), may hold values from -6 to 6
- norm_gain: float32 [8192], replicated, may hold values from 0.1 to 1.9
- master: float32 [8192, 512], P('fsdp'), may hold values from -6 to 6
- momentum: float32 [8192, 512], P('fsdp'), may hold values from -4 to 4
- pseudo_grad: float32 [2, 8192, 512], P('island', 'fsdp'), may hold values from -20 to 20
Outputs:
- keys: bfloat16 [4096, 512], P(('island', 'fsdp'))
- master_new: float32 [8192, 512], P('fsdp')
- momentum_new: float32 [8192, 512], P('fsdp')
All inputs are finite; a program needn't handle non-finite values.
Results may differ from a plain program's by a relative error of at most 0.008.
Values may be sent and summed in bfloat16 or wider, within the bound.
No kernel may reach another device: no remote copies, remote signals or barrier semaphores. Data moves between devices by JAX's collectives and lax.ppermute only.
A program may use at most 64 MiB of HBM per device.

v0:
```python
import jax
import jax.numpy as jnp
from jax import lax
from jax.sharding import PartitionSpec as P

BLOCK = 128


outer_rate = 0.7
outer_mu = 0.9


def on_device(tokens, norm_gain, master, momentum, pseudo_grad):
    islands = lax.axis_size("island")
    island_grad = pseudo_grad[0]
    row_total, col_total = island_grad.shape
    every_island = lax.all_gather(
        pseudo_grad.astype(jnp.bfloat16), "island", axis=0, tiled=True
    ).astype(pseudo_grad.dtype)
    grouped_all = every_island.reshape(islands, row_total, col_total // BLOCK, BLOCK)
    peaks_all = jnp.max(jnp.abs(grouped_all), axis=3)
    shared = jnp.sum(peaks_all, axis=0) / islands + 1e-06
    quantized_all = jnp.clip(grouped_all / shared[None, :, :, None], -1.0, 1.0).astype(jnp.bfloat16)
    summed = jnp.sum(quantized_all.astype(jnp.float32), axis=0)
    outer_grad = (shared[:, :, None] * summed / islands).reshape(row_total, col_total)
    momentum_new = outer_mu * momentum + outer_grad
    master_new = master - outer_rate * (outer_grad + outer_mu * momentum_new)
    weight = master_new.astype(jnp.bfloat16)
    features = tokens.astype(jnp.float32)
    inverse = lax.rsqrt(jnp.mean(features * features, axis=1, keepdims=True) + 1e-05)
    normed = (features * inverse * norm_gain[None, :]).astype(jnp.bfloat16)
    scale = 1.0 / jnp.sqrt(jnp.float32(normed.shape[1]))
    gathered = lax.all_gather(weight, "fsdp", axis=0, tiled=True)
    product = jnp.dot(normed, gathered, preferred_element_type=jnp.float32)
    keys = (product * scale).astype(jnp.bfloat16)
    return (keys, master_new, momentum_new)


def solution(mesh):
    placed = (
        P(("island", "fsdp"), None),
        P(),
        P("fsdp", None),
        P("fsdp", None),
        P("island", "fsdp", None),
    )
    return jax.shard_map(
        on_device,
        mesh=mesh,
        in_specs=placed,
        out_specs=(P(("island", "fsdp"), None), P("fsdp", None), P("fsdp", None)),
        check_vma=False,
    )
```

profile of v0, /device:TPU:0, one launch (start us, length us, event | category | flops | bytes accessed | tf_op | source)
XLA Modules:
  0.0 131.9 jit_solution(16106397895837396728)
XLA Ops:
  7.2 0.0 all-gather.3.cloned.1.call-start
  7.2 2.1 %convert_element_type.28 = bf16[1,512,512]{2,1,0:T(8,128)(2,1)} convert(f32[1,512,512]{2,1,0:T(8,128)} %param.9) | non-fusion elementwise | flops 262144 | bytes 1572864 | tf_op jit(solution)/shard_map/convert_element_type | solution.py:18
  9.3 0.0 all-gather.3.cloned.1.call-update
  9.3 0.0 all-gather.5.cloned.1.call-start
  9.4 24.8 %all-gather.3.cloned.1.call-done = bf16[2,512,512]{2,1,0:T(8,128)(2,1)} async-done(((bf16[1,512,512]{2,1,0:T(8,128)(2,1)}), bf16[2,512,512]{2,1,0:T(8,128)(2,1)}) %all-gather.3.cloned.1.call-update) | async-done | bytes 1048592 | tf_op jit(solution)/shard_map/all_gather | solution.py:17
  34.2 2.9 %convert_abs_fusion = f32[2,512,512]{2,1,0:T(8,128)} fusion(bf16[2,512,512]{2,1,0:T(8,128)(2,1)} %all-gather.3.cloned.1.call-done), kind=kLoop, calls=%fused_computation.6 | loop fusion | flops 1048576 | bytes 3145728 | tf_op jit(solution)/shard_map/abs | solution.py:21
  37.0 1.9 %abs.7 = f32[2,512,4,128]{3,2,1,0:T(4,128)S(1)} reshape(f32[2,512,512]{2,1,0:T(8,128)} %convert_abs_fusion) | data formatting | bytes 4194304 | tf_op jit(solution)/shard_map/abs | solution.py:21
  39.0 1.1 reduce_max.9
  40.2 0.0 copy-start
  40.2 0.6 mul.53
  40.8 0.1 copy.21
  40.9 0.0 copy-start.2
  40.9 0.0 copy-start.3
  40.9 0.5 copy-done
  41.4 0.4 convert_reduce_fusion
  41.8 0.4 copy-done.2
  42.2 0.3 copy-done.3
  42.5 0.0 copy-start.1
  42.5 2.1 %fusion.15 = (bf16[512,512]{1,0:T(8,128)(2,1)}, f32[512,512]{1,0:T(8,128)}, f32[512,512]{1,0:T(8,128)}) fusion(f32[512,512]{1,0:T(8,128)S(1)} %copy-done.2, f32[512,512]{1,0:T(8,128)S(1)} %convert_reduce_fusion, f32[64,8,4,128]{3,2,1,0:T(4,128)S(1)} %bitcast.12, f32[512,512]{1,0:T(8,128)S(1)} %copy-done.3), kind=kLoop, calls=%fused_computation.21 | loop fusion | flops 2359296 | bytes 6815744 | tf_op jit(solution)/shard_map/convert_element_type | solution.py:28
  44.6 0.0 copy-start.4
  44.6 0.0 all-gather.5.cloned.1.call-update
  44.7 0.0 copy-done.1
  44.7 0.5 fusion
  45.2 74.5 %all-gather.5.cloned.1.call-done = bf16[8192,512]{1,0:T(8,128)(2,1)} async-done(((bf16[512,512]{1,0:T(8,128)(2,1)}), bf16[8192,512]{1,0:T(8,128)(2,1)}) %all-gather.5.cloned.1.call-update) | async-done | bytes 8388624 | tf_op jit(solution)/shard_map/all_gather | solution.py:33
  119.7 0.0 copy-done.4
  119.7 5.3 %fusion.12 = bf16[128,512]{1,0:T(8,128)(2,1)} fusion(bf16[8192,512]{1,0:T(8,128)(2,1)} %all-gather.5.cloned.1.call-done, bf16[128,8192]{1,0:T(8,128)(2,1)S(1)} %copy-done.1, f32[8192]{0:T(1024)S(1)} %copy-done.4, f32[128]{0:T(128)S(1)} %add_rsqrt_fusion), kind=kOutput, calls=%fused_computation.14 | convolution fusion | flops 1078067200 | bytes 10650112 | tf_op jit(solution)/shard_map/dot_general | solution.py:34
  (3 shorter events, 0.1 us)
Async XLA Ops:
  7.2 27.0 %all-gather.3.cloned.1.call-start = ((), (), s32[]{:S(2)}) async-start(), calls=%async_computation | async-start | bytes 1572864 | tf_op jit(solution)/shard_map/all_gather | solution.py:17
  9.3 110.4 %all-gather.5.cloned.1.call-start = ((), (), s32[]{:S(2)}) async-start(), calls=%async_computation.1 | async-start | bytes 8912896 | tf_op jit(solution)/shard_map/all_gather | solution.py:33
  40.2 1.2 copy-start
  40.9 1.3 copy-start.2
  40.9 1.6 %copy-start.3 = (f32[512,512]{1,0:T(8,128)S(1)}, f32[512,512]{1,0:T(8,128)}, u32[]{:S(2)}) copy-start(f32[512,512]{1,0:T(8,128)} %param.8) | copy-start | bytes 3145732
  42.5 2.1 %copy-start.1 = (bf16[128,8192]{1,0:T(8,128)(2,1)S(1)}, bf16[128,8192]{1,0:T(8,128)(2,1)}, u32[]{:S(2)}) copy-start(bf16[128,8192]{1,0:T(8,128)(2,1)} %param.5) | copy-start | bytes 6291460
  44.6 75.1 %copy-start.4 = (f32[8192]{0:T(1024)S(1)}, f32[8192]{0:T(1024)}, u32[]{:S(2)}) copy-start(f32[8192]{0:T(1024)} %param.6) | copy-start | bytes 98308
Sparse Core Ops, SparseCore 0:
  10.1 23.9 all-gather.2
  44.8 74.8 all-gather.4
where the time goes:
time: 132 us
  waiting for transfers between devices  99.4 us (75%)
  between operations  14.1 us (11%)
  other arithmetic  9.2 us (7%)
  matrix products  5.34 us (4%)
  local copies, waits for them, and re-layouts  3.79 us (3%)
    all_gather x1, waiting for transfers between devices, on_device(): gathered = lax.all_gather(weight, 'fsdp', axis=0, tiled=True)  74.5 us
    all_gather x1, waiting for transfers between devices, on_device(): lax.all_gather(pseudo_grad.astype(jnp.bfloat16), 'island', axis=0, tiled=...  24.8 us
    dot_general x1, matrix products, on_device(): product = jnp.dot(normed, gathered, preferred_element_type=jnp.float32)  5.34 us
    abs x1, other arithmetic, on_device(): peaks_all = jnp.max(jnp.abs(grouped_all), axis=3)  2.86 us
  transfers between devices with their start and end apart: 2, of which 2 were waited for; matrix products, arithmetic and copies ran while one was open for 0% of the time, Pallas kernels for 0%

commit v1 on v0

--- a/solution.py
+++ b/solution.py
@@ -1,16 +1,261 @@
+import functools
+
 import jax
 import jax.numpy as jnp
 from jax import lax
+from jax.experimental import pallas as pl
+from jax.experimental.pallas import tpu as pltpu
 from jax.sharding import PartitionSpec as P
 
 BLOCK = 128
-
+CORES = 2
+RING_LIMIT = 16
 
 outer_rate = 0.7
 outer_mu = 0.9
-
-
-def on_device(tokens, norm_gain, master, momentum, pseudo_grad):
+VMEM = pl.BlockSpec(memory_space=pltpu.VMEM)
+VMEM_LIMIT = 40 * 1024 * 1024
+
+
+def params():
+    return pltpu.CompilerParams(vmem_limit_bytes=VMEM_LIMIT)
+
+
+def chip_at(place, chips):
+    up = 2 * place
+    down = 2 * (chips - 1 - place) + 1
+    if isinstance(place, int):
+        return up if place < chips // 2 else down
+    return jnp.where(place < chips // 2, up, down)
+
+
+def place_of(chip, chips):
+    if isinstance(chip, int):
+        return chip // 2 if chip % 2 == 0 else chips - 1 - chip // 2
+    return jnp.where(chip % 2 == 0, chip // 2, chips - 1 - chip // 2)
+
+
+def ring_pairs(chips):
+    pairs = []
+    for chip in range(chips):
+        for core in range(CORES):
+            step = 1 if core == 0 else -1
+            target = chip_at((place_of(chip, chips) + step) % chips, chips)
+            pairs.append((chip * CORES + core, target * CORES + core))
+    return pairs
+
+
+def swap_pairs(chips):
+    return [(f, f ^ 1) for f in range(CORES * chips)]
+
+
+def slots(chips):
+    order = [(0, 0), (0, 1)]
+    for step in range(1, chips // 2):
+        order += [(step, 0), (step, 1), (-step, 1), (-step, 0)]
+    return order + [(chips // 2, 0), (chips // 2, 1)]
+
+
+def shard_of(slot, chips):
+    back, other = slot
+    me = lax.axis_index("fsdp")
+    core = me % CORES
+    direction = jnp.where(core == 0, -1, 1)
+    place = (place_of(me // CORES, chips) + direction * back + chips) % chips
+    return chip_at(place, chips) * CORES + (1 - core if other else core)
+
+
+def cast_kernel(grad, out):
+    out[...] = grad[...].astype(out.dtype)
+
+
+def cast_half(grad, which):
+    rows, cols = grad.shape
+    half = rows // 2
+    steps = 2
+    tall = half // steps
+    return pl.pallas_call(
+        cast_kernel,
+        grid=(steps,),
+        in_specs=[pl.BlockSpec((tall, cols), lambda g: (which() * steps + g, 0))],
+        out_specs=pl.BlockSpec((tall, cols), lambda g: (g, 0)),
+        out_shape=jax.ShapeDtypeStruct((half, cols), jnp.bfloat16),
+        compiler_params=params(),
+        cost_estimate=pl.CostEstimate(flops=half * cols, bytes_accessed=6 * half * cols, transcendentals=0),
+    )(grad)
+
+
+def mine():
+    return lax.axis_index("island")
+
+
+def others():
+    return 1 - lax.axis_index("island")
+
+
+def token_kernel(chips, half, tokens, own, sent, inverse):
+    rows, width = tokens.shape
+    for k, slot in enumerate(slots(chips)):
+        start = shard_of(slot, chips) * 2 * half
+        own[k] = tokens[:, pl.ds(pl.multiple_of(start + mine() * half, half), half)]
+        sent[k] = tokens[:, pl.ds(pl.multiple_of(start + others() * half, half), half)]
+    total = jnp.zeros((rows, BLOCK), jnp.float32)
+    for k in range(width // BLOCK):
+        part = tokens[:, k * BLOCK : (k + 1) * BLOCK].astype(jnp.float32)
+        total += part * part
+    mean = jnp.sum(total, axis=1, keepdims=True) / width
+    inverse[...] = lax.rsqrt(mean + 1e-05) / jnp.sqrt(jnp.float32(width))
+
+
+def split_tokens(tokens, chips):
+    rows, width = tokens.shape
+    half = width // (chips * CORES * 2)
+    shape = (chips * CORES, rows, half)
+    return pl.pallas_call(
+        functools.partial(token_kernel, chips, half),
+        in_specs=[VMEM],
+        out_specs=[VMEM] * 3,
+        out_shape=[
+            jax.ShapeDtypeStruct(shape, tokens.dtype),
+            jax.ShapeDtypeStruct(shape, tokens.dtype),
+            jax.ShapeDtypeStruct((rows, 1), jnp.float32),
+        ],
+        compiler_params=params(),
+        cost_estimate=pl.CostEstimate(flops=2 * rows * width, bytes_accessed=4 * rows * width, transcendentals=0),
+    )(tokens)
+
+
+def sync_kernel(which, kept, first, second, master, momentum, gain, *refs):
+    weight, master_new, momentum_new = refs[-3:]
+    tall, cols = first.shape
+    row = lax.axis_index("fsdp") * (2 * pl.num_programs(0)) + which() * pl.num_programs(0) + pl.program_id(0)
+    gains = jnp.transpose(jnp.broadcast_to(gain[pl.ds(row, 1), :], (tall, tall)))
+    for k in range(cols // BLOCK):
+        at = slice(k * BLOCK, (k + 1) * BLOCK)
+        a = first[:, at].astype(jnp.float32)
+        b = second[:, at].astype(jnp.float32)
+        peak_a = jnp.max(jnp.abs(a), axis=1, keepdims=True)
+        peak_b = jnp.max(jnp.abs(b), axis=1, keepdims=True)
+        shared = (peak_a + peak_b) / 2 + 1e-06
+        over = 1.0 / shared
+        low_a = jnp.clip(a * over, -1.0, 1.0).astype(jnp.bfloat16).astype(jnp.float32)
+        low_b = jnp.clip(b * over, -1.0, 1.0).astype(jnp.bfloat16).astype(jnp.float32)
+        outer_grad = shared * (low_a + low_b) / 2
+        moved = outer_mu * momentum[:, at] + outer_grad
+        fresh = master[:, at] - outer_rate * (outer_grad + outer_mu * moved)
+        momentum_new[:, at] = moved
+        master_new[:, at] = fresh
+        if weight is not None:
+            weight[:, at] = (gains * fresh).astype(weight.dtype)
+
+
+def sync_half(which, first, second, master, momentum, gain, kept=()):
+    rows, cols = master.shape
+    half = rows // 2
+    tall = BLOCK
+    steps = half // tall
+    here = pl.BlockSpec((tall, cols), lambda g: (g, 0))
+    there = pl.BlockSpec((tall, cols), lambda g: (which() * steps + g, 0))
+    full = jax.ShapeDtypeStruct(master.shape, jnp.float32)
+    return pl.pallas_call(
+        functools.partial(sync_kernel, which, len(kept)),
+        grid=(steps,),
+        in_specs=[here, here, there, there, VMEM] + [pl.BlockSpec(memory_space=pl.ANY)] * len(kept),
+        out_specs=[here, there, there],
+        out_shape=[jax.ShapeDtypeStruct((half, cols), jnp.bfloat16), full, full],
+        input_output_aliases={5 + k: 1 + k for k in range(len(kept))},
+        compiler_params=params(),
+        cost_estimate=pl.CostEstimate(flops=30 * half * cols, bytes_accessed=22 * half * cols, transcendentals=0),
+    )(first, second, master, momentum, gain, *kept)
+
+
+def dot_kernel(slot_from, count, own, other, *refs):
+    blocks, more = refs[:count], refs[count:]
+    rows = own.shape[1]
+    total = more[0][...] if slot_from else None
+    for k in range(count):
+        left = jnp.concatenate([own[slot_from + k], other[slot_from + k]], axis=0)
+        term = jnp.dot(left, blocks[k][...], preferred_element_type=jnp.float32)
+        total = term if total is None else total + term
+    if slot_from:
+        more[1][...] = total[:rows]
+        more[2][...] = total[rows:].astype(jnp.bfloat16)
+    else:
+        more[0][...] = total
+
+
+def dot_blocks(slot_from, own, other, blocks, total=None):
+    rows = own.shape[1]
+    cols = blocks[0].shape[1]
+    count = len(blocks)
+    if total is None:
+        outs = jax.ShapeDtypeStruct((2 * rows, cols), jnp.float32)
+        out_specs = VMEM
+        given = (own, other, *blocks)
+    else:
+        outs = [jax.ShapeDtypeStruct((rows, cols), jnp.float32), jax.ShapeDtypeStruct((rows, cols), jnp.bfloat16)]
+        out_specs = [VMEM, VMEM]
+        given = (own, other, *blocks, total)
+    return pl.pallas_call(
+        functools.partial(dot_kernel, slot_from, count),
+        in_specs=[VMEM] * len(given),
+        out_specs=out_specs,
+        out_shape=outs,
+        compiler_params=params(),
+        cost_estimate=pl.CostEstimate(
+            flops=4 * rows * cols * count * own.shape[2], bytes_accessed=2 * count * own.shape[2] * (cols + 2 * rows), transcendentals=0
+        ),
+    )(*given)
+
+
+def close_kernel(mine_part, other_part, inverse, keys):
+    keys[...] = ((mine_part[...] + other_part[...].astype(jnp.float32)) * inverse[...]).astype(keys.dtype)
+
+
+def by_permutes(tokens, norm_gain, master, momentum, pseudo_grad):
+    chips = lax.axis_size("fsdp") // CORES
+    gain = norm_gain.reshape(-1, BLOCK)
+    ring = functools.partial(lax.ppermute, axis_name="fsdp", perm=ring_pairs(chips))
+    swap = functools.partial(lax.ppermute, axis_name="fsdp", perm=swap_pairs(chips))
+    cross = functools.partial(lax.ppermute, axis_name="island", perm=[(0, 1), (1, 0)])
+
+    grad_sent = cast_half(pseudo_grad[0], others)
+    grad_here = cross(grad_sent)
+    grad_own = cast_half(pseudo_grad[0], mine)
+    own, sent, inverse = split_tokens(tokens, chips)
+
+    weight, master_new, momentum_new = sync_half(mine, grad_own, grad_here, master, momentum, gain)
+    sent, weight = lax.optimization_barrier((sent, weight))
+    other = cross(sent)
+    a = weight
+    b = swap(weight)
+    blocks = [a, b]
+    for step in range(1, chips // 2):
+        a, b = ring(a), ring(b)
+        blocks += [a, b, swap(a), swap(b)]
+    a = ring(a)
+    blocks += [a, swap(a)]
+
+    other, grad_own = lax.optimization_barrier((other, grad_own))
+    grad_there = cross(grad_own)
+    _, master_new, momentum_new = sync_half(
+        others, grad_sent, grad_there, master, momentum, gain, (master_new, momentum_new)
+    )
+    early = len(blocks) - 6
+    total = dot_blocks(0, own, other, blocks[:early])
+    mine_part, sent_part = dot_blocks(early, own, other, blocks[early:], total)
+    other_part = cross(sent_part)
+    keys = pl.pallas_call(
+        close_kernel,
+        in_specs=[VMEM] * 3,
+        out_specs=VMEM,
+        out_shape=jax.ShapeDtypeStruct(mine_part.shape, jnp.bfloat16),
+        compiler_params=params(),
+    )(mine_part, other_part, inverse)
+    return (keys, master_new, momentum_new)
+
+
+def by_gathers(tokens, norm_gain, master, momentum, pseudo_grad):
     islands = lax.axis_size("island")
     island_grad = pseudo_grad[0]
     row_total, col_total = island_grad.shape
@@ -36,6 +281,15 @@
     return (keys, master_new, momentum_new)
 
 
+def on_device(tokens, norm_gain, master, momentum, pseudo_grad):
+    shards = lax.axis_size("fsdp")
+    rows = master.shape[0]
+    ringed = shards % (2 * CORES) == 0 and 4 * CORES <= shards <= RING_LIMIT * CORES
+    if lax.axis_size("island") == 2 and ringed and rows % (2 * BLOCK) == 0:
+        return by_permutes(tokens, norm_gain, master, momentum, pseudo_grad)
+    return by_gathers(tokens, norm_gain, master, momentum, pseudo_grad)
+
+
 def solution(mesh):
     placed = (
         P(("island", "fsdp"), None),

time: 132 us -> 53.6 us (0.41)
  waiting for transfers between devices: 99.4 us -> 23 us
  starting transfers between devices: 0.08 us -> 20.9 us
  between operations: 14.1 us -> 0.73 us
  other arithmetic: 9.2 us -> 0 us
  Pallas kernels: 0 us -> 6.02 us
  matrix products: 5.34 us -> 0 us
    all_gather x2 -> x0, waiting for transfers between devices: 99.3 us -> none  [the longest x1 74.5 us: on_device(): gathered = lax.all_gather(weight, 'fsdp', axis=0, tiled=True)]
    ppermute x0 -> x19, waiting for transfers between devices: none -> 23 us  [the longest x6 11.6 us: by_permutes(): a, b = (ring(a), ring(b))]
    ppermute x0 -> x19, starting transfers between devices: none -> 20.9 us  [the longest x6 10.6 us: by_permutes(): a, b = (ring(a), ring(b))]
    pallas_call x0 -> x8, Pallas kernels: none -> 6.02 us  [the longest x2 3.07 us: sync_half(): pl.pallas_call(functools.partial(sync_kernel, which, len(kept)), grid=(st...]
    dot_general x1 -> x0, matrix products: 5.34 us -> none  [on_device(): product = jnp.dot(normed, gathered, preferred_element_type=jnp.float32)]
    convert_element_type x2 -> x0, other arithmetic: 4.19 us -> none  [the longest x1 2.11 us: on_device(): weight = master_new.astype(jnp.bfloat16)]
    abs x1 -> x0, other arithmetic: 2.86 us -> none  [on_device(): peaks_all = jnp.max(jnp.abs(grouped_all), axis=3)]
    abs x1 -> x0, local copies, waits for them, and re-layouts: 1.93 us -> none  [on_device(): peaks_all = jnp.max(jnp.abs(grouped_all), axis=3)]
  transfers between devices with their start and end apart: 2 -> 19, of which waited for: 2 -> 10; matrix products, arithmetic and copies ran while one was open for 0% -> 0% of each run, Pallas kernels for 0% -> 7%
where the time goes in v1:
time: 53.6 us; the launch traced here: 53.4 us
  waiting for transfers between devices  23 us (43%)
  starting transfers between devices  20.9 us (39%)
  Pallas kernels  6.02 us (11%)
  local copies, waits for them, and re-layouts  2.82 us (5%)
  between operations  0.73 us (1%)
    ppermute x6, waiting for transfers between devices, by_permutes(): a, b = (ring(a), ring(b))  11.6 us
    ppermute x6, starting transfers between devices, by_permutes(): a, b = (ring(a), ring(b))  10.6 us
    ppermute x1, waiting for transfers between devices, by_permutes(): grad_there = cross(grad_own)  5.19 us
    ppermute x1, waiting for transfers between devices, by_permutes(): grad_here = cross(grad_sent)  3.96 us
    pallas_call x2, Pallas kernels, sync_half(): pl.pallas_call(functools.partial(sync_kernel, which, len(kept)), grid=(st...  3.07 us
    ppermute x1, starting transfers between devices, by_permutes(): grad_here = cross(grad_sent)  3.03 us
    unnamed x10, local copies, waits for them, and re-layouts  2.82 us
    ppermute x1, starting transfers between devices, by_permutes(): a = ring(a)  1.8 us
  transfers between devices with their start and end apart: 19, of which 10 were waited for; matrix products, arithmetic and copies ran while one was open for 0% of the time, Pallas kernels for 7%

profile of v1, /device:TPU:0, one launch (start us, length us, event | category | flops | bytes accessed | tf_op | source)
XLA Modules:
  0.0 53.4 jit_solution(3091006248727579926)
XLA Ops:
  0.6 1.2 %copy-done = f32[1,512,512]{2,1,0:T(8,128)S(1)} copy-done((f32[1,512,512]{2,1,0:T(8,128)S(1)}, f32[1,512,512]{2,1,0:T(8,128)}, u32[]{:S(2)}) %copy-start) | copy-done | bytes 1048600
  1.9 3.0 %collective-permute-start = (bf16[256,512]{1,0:T(8,128)(2,1)S(1)}, bf16[256,512]{1,0:T(8,128)(2,1)S(1)}, u32[]{:S(2)}, u32[]{:S(2)}) collective-permute-start(bf16[256,512]{1,0:T(8,128)(2,1)S(1)} %shard_map.78.first), channel_id=1, source_target_pairs={{0,16},{16,0},{1,17},{17,1},{2,18},{18,2},{3,19},{19,3},{4,20},{20... | collective-permute-start | bytes 786440 | tf_op jit(solution)/shard_map/ppermute | solution.py:223
  5.0 1.6 %copy-done.3 = bf16[128,8192]{1,0:T(8,128)(2,1)S(1)} copy-done((bf16[128,8192]{1,0:T(8,128)(2,1)S(1)}, bf16[128,8192]{1,0:T(8,128)(2,1)}, u32[]{:S(2)}) %copy-start.3) | copy-done | bytes 2097176
  6.6 0.7 %shard_map.76 = (bf16[16,128,256]{2,1,0:T(8,128)(2,1)S(1)}, bf16[16,128,256]{2,1,0:T(8,128)(2,1)S(1)}, f32[128,1]{1,0:T(8,128)S(1)}) custom-call(bf16[128,8192]{1,0:T(8,128)(2,1)S(1)} %copy-done.3), custom_call_target="tpu_custom_call" | custom-call | flops 2097152 | bytes 4194304 | tf_op jit(solution)/shard_map/pallas_call | solution.py:114
  7.3 4.0 %collective-permute-done.second = bf16[256,512]{1,0:T(8,128)(2,1)S(1)} collective-permute-done((bf16[256,512]{1,0:T(8,128)(2,1)S(1)}, bf16[256,512]{1,0:T(8,128)(2,1)S(1)}, u32[]{:S(2)}, u32[]{:S(2)}) %collective-permute-start) | collective-permute-done | bytes 262176 | tf_op jit(solution)/shard_map/ppermute | solution.py:223
  11.3 1.5 %shard_map.79 = (bf16[256,512]{1,0:T(8,128)(2,1)S(1)}, f32[512,512]{1,0:T(8,128)}, f32[512,512]{1,0:T(8,128)}) custom-call(bf16[256,512]{1,0:T(8,128)(2,1)S(1)} %shard_map.77.first, bf16[256,512]{1,0:T(8,128)(2,1)S(1)} %collective-permute-done.second, f32[512,512]{1,0:T(8,128)S(1)} %copy-done.1, f32[512,512]{1,0:T(8,128)S(1)} %copy-done.2, f32[64,128]{1,0:T(8,128)S(1)} %bitcast.4), custom_call_target="tpu_custom_call" | custom-call | flops 3932160 | bytes 2883584 | tf_op jit(solution)/shard_map/pallas_call | solution.py:160
  12.8 1.8 %collective-permute-start.2 = (bf16[256,512]{1,0:T(8,128)(2,1)S(1)}, bf16[256,512]{1,0:T(8,128)(2,1)S(1)}, u32[]{:S(2)}, u32[]{:S(2)}) collective-permute-start(bf16[256,512]{1,0:T(8,128)(2,1)S(1)} %get-tuple-element.22.refs_0_), channel_id=1, source_target_pairs={{0,4},{1,3},{2,0},{3,7},{4,8},{5,1},{6,2},{7,11},{8,12},{9,5},{10,... | collective-permute-start | bytes 786440 | tf_op jit(solution)/shard_map/ppermute | solution.py:234
  14.6 1.5 %collective-permute-start.1 = (bf16[16,128,256]{2,1,0:T(8,128)(2,1)S(1)}, bf16[16,128,256]{2,1,0:T(8,128)(2,1)S(1)}, u32[]{:S(2)}, u32[]{:S(2)}) collective-permute-start(bf16[16,128,256]{2,1,0:T(8,128)(2,1)S(1)} %get-tuple-element.20), channel_id=1, source_target_pairs={{0,16},{16,0},{1,17},{17,1},{2,18},{18,2},{3,19},{19,3},{4,20},{20... | collective-permute-start | bytes 3145736 | tf_op jit(solution)/shard_map/ppermute | solution.py:229
  16.2 3.1 %collective-permute-done.2.refs_2_ = bf16[256,512]{1,0:T(8,128)(2,1)S(1)} collective-permute-done((bf16[256,512]{1,0:T(8,128)(2,1)S(1)}, bf16[256,512]{1,0:T(8,128)(2,1)S(1)}, u32[]{:S(2)}, u32[]{:S(2)}) %collective-permute-start.2) | collective-permute-done | bytes 262176 | tf_op jit(solution)/shard_map/ppermute | solution.py:234
  19.2 1.8 %collective-permute-start.3 = (bf16[256,512]{1,0:T(8,128)(2,1)S(1)}, bf16[256,512]{1,0:T(8,128)(2,1)S(1)}, u32[]{:S(2)}, u32[]{:S(2)}) collective-permute-start(bf16[256,512]{1,0:T(8,128)(2,1)S(1)} %collective-permute-done.2.refs_2_), channel_id=1, source_target_pairs={{0,4},{1,3},{2,0},{3,7},{4,8},{5,1},{6,2},{7,11},{8,12},{9,5},{10,... | collective-permute-start | bytes 786440 | tf_op jit(solution)/shard_map/ppermute | solution.py:234
  21.0 1.6 %collective-permute-start.6 = (bf16[256,512]{1,0:T(8,128)(2,1)S(1)}, bf16[256,512]{1,0:T(8,128)(2,1)S(1)}, u32[]{:S(2)}, u32[]{:S(2)}) collective-permute-start(bf16[256,512]{1,0:T(8,128)(2,1)S(1)} %collective-permute-done.5.refs_1_), channel_id=1, source_target_pairs={{0,4},{1,3},{2,0},{3,7},{4,8},{5,1},{6,2},{7,11},{8,12},{9,5},{10,... | collective-permute-start | bytes 786440 | tf_op jit(solution)/shard_map/ppermute | solution.py:234
  22.6 3.0 %collective-permute-done.3.refs_6_ = bf16[256,512]{1,0:T(8,128)(2,1)S(1)} collective-permute-done((bf16[256,512]{1,0:T(8,128)(2,1)S(1)}, bf16[256,512]{1,0:T(8,128)(2,1)S(1)}, u32[]{:S(2)}, u32[]{:S(2)}) %collective-permute-start.3) | collective-permute-done | bytes 262176 | tf_op jit(solution)/shard_map/ppermute | solution.py:234
  25.6 1.8 %collective-permute-start.4 = (bf16[256,512]{1,0:T(8,128)(2,1)S(1)}, bf16[256,512]{1,0:T(8,128)(2,1)S(1)}, u32[]{:S(2)}, u32[]{:S(2)}) collective-permute-start(bf16[256,512]{1,0:T(8,128)(2,1)S(1)} %collective-permute-done.3.refs_6_), channel_id=1, source_target_pairs={{0,4},{1,3},{2,0},{3,7},{4,8},{5,1},{6,2},{7,11},{8,12},{9,5},{10,... | collective-permute-start | bytes 786440 | tf_op jit(solution)/shard_map/ppermute | solution.py:234
  27.4 1.0 %collective-permute-done.6.refs_3_ = bf16[256,512]{1,0:T(8,128)(2,1)S(1)} collective-permute-done((bf16[256,512]{1,0:T(8,128)(2,1)S(1)}, bf16[256,512]{1,0:T(8,128)(2,1)S(1)}, u32[]{:S(2)}, u32[]{:S(2)}) %collective-permute-start.6) | collective-permute-done | bytes 262176 | tf_op jit(solution)/shard_map/ppermute | solution.py:234
  28.4 1.8 %collective-permute-start.7 = (bf16[256,512]{1,0:T(8,128)(2,1)S(1)}, bf16[256,512]{1,0:T(8,128)(2,1)S(1)}, u32[]{:S(2)}, u32[]{:S(2)}) collective-permute-start(bf16[256,512]{1,0:T(8,128)(2,1)S(1)} %collective-permute-done.6.refs_3_), channel_id=1, source_target_pairs={{0,4},{1,3},{2,0},{3,7},{4,8},{5,1},{6,2},{7,11},{8,12},{9,5},{10,... | collective-permute-start | bytes 786440 | tf_op jit(solution)/shard_map/ppermute | solution.py:234
  30.2 0.5 collective-permute-start.15
  30.7 1.3 %collective-permute-done.4.refs_0_ = bf16[256,512]{1,0:T(8,128)(2,1)S(1)} collective-permute-done((bf16[256,512]{1,0:T(8,128)(2,1)S(1)}, bf16[256,512]{1,0:T(8,128)(2,1)S(1)}, u32[]{:S(2)}, u32[]{:S(2)}) %collective-permute-start.4) | collective-permute-done | bytes 262176 | tf_op jit(solution)/shard_map/ppermute | solution.py:234
  31.9 1.8 %collective-permute-start.11 = (bf16[256,512]{1,0:T(8,128)(2,1)S(1)}, bf16[256,512]{1,0:T(8,128)(2,1)S(1)}, u32[]{:S(2)}, u32[]{:S(2)}) collective-permute-start(bf16[256,512]{1,0:T(8,128)(2,1)S(1)} %collective-permute-done.4.refs_0_), channel_id=1, source_target_pairs={{0,4},{1,3},{2,0},{3,7},{4,8},{5,1},{6,2},{7,11},{8,12},{9,5},{10,... | collective-permute-start | bytes 786440 | tf_op jit(solution)/shard_map/ppermute | solution.py:236
  33.7 1.0 %collective-permute-done.7.refs_7_ = bf16[256,512]{1,0:T(8,128)(2,1)S(1)} collective-permute-done((bf16[256,512]{1,0:T(8,128)(2,1)S(1)}, bf16[256,512]{1,0:T(8,128)(2,1)S(1)}, u32[]{:S(2)}, u32[]{:S(2)}) %collective-permute-start.7) | collective-permute-done | bytes 262176 | tf_op jit(solution)/shard_map/ppermute | solution.py:234
  34.8 1.8 %collective-permute-start.8 = (bf16[256,512]{1,0:T(8,128)(2,1)S(1)}, bf16[256,512]{1,0:T(8,128)(2,1)S(1)}, u32[]{:S(2)}, u32[]{:S(2)}) collective-permute-start(bf16[256,512]{1,0:T(8,128)(2,1)S(1)} %collective-permute-done.7.refs_7_), channel_id=1, source_target_pairs={{0,4},{1,3},{2,0},{3,7},{4,8},{5,1},{6,2},{7,11},{8,12},{9,5},{10,... | collective-permute-start | bytes 786440 | tf_op jit(solution)/shard_map/ppermute | solution.py:234
  36.6 0.5 collective-permute-start.16
  37.1 1.2 %collective-permute-done.1.other = bf16[16,128,256]{2,1,0:T(8,128)(2,1)S(1)} collective-permute-done((bf16[16,128,256]{2,1,0:T(8,128)(2,1)S(1)}, bf16[16,128,256]{2,1,0:T(8,128)(2,1)S(1)}, u32[]{:S(2)}, u32[]{:S(2)}) %collective-permute-start.1) | collective-permute-done | bytes 1048608 | tf_op jit(solution)/shard_map/ppermute | solution.py:229
  38.3 0.5 collective-permute-start.12
  38.8 2.3 %collective-permute-done.8.refs_1_ = bf16[256,512]{1,0:T(8,128)(2,1)S(1)} collective-permute-done((bf16[256,512]{1,0:T(8,128)(2,1)S(1)}, bf16[256,512]{1,0:T(8,128)(2,1)S(1)}, u32[]{:S(2)}, u32[]{:S(2)}) %collective-permute-start.8) | collective-permute-done | bytes 262176 | tf_op jit(solution)/shard_map/ppermute | solution.py:234
  41.1 1.7 %collective-permute-start.18 = (bf16[256,512]{1,0:T(8,128)(2,1)S(1)}, bf16[256,512]{1,0:T(8,128)(2,1)S(1)}, u32[]{:S(2)}, u32[]{:S(2)}) collective-permute-start(bf16[256,512]{1,0:T(8,128)(2,1)S(1)} %shard_map.77.first), channel_id=1, source_target_pairs={{0,16},{16,0},{1,17},{17,1},{2,18},{18,2},{3,19},{19,3},{4,20},{20... | collective-permute-start | bytes 786440 | tf_op jit(solution)/shard_map/ppermute | solution.py:240
  42.9 0.8 %shard_map.80.refs_6_ = f32[256,512]{1,0:T(8,128)S(1)} custom-call(bf16[16,128,256]{2,1,0:T(8,128)(2,1)S(1)} %get-tuple-element.17.own, bf16[16,128,256]{2,1,0:T(8,128)(2,1)S(1)} %collective-permute-done.1.other, bf16[256,512]{1,0:T(8,128)(2,1)S(1)} %get-tuple-element.22.refs_0_, bf16[256,512]{1,0:T(8,128)(2,1)S(1)} %collective-permute-done.5.refs_1_, ...), custom_call_target="tpu_custom_call" | custom-call | flops 671088640 | bytes 3932160 | tf_op jit(solution)/shard_map/pallas_call | solution.py:199
  43.8 0.6 %shard_map.81 = (f32[128,512]{1,0:T(8,128)S(1)}, bf16[128,512]{1,0:T(8,128)(2,1)S(1)}) custom-call(bf16[16,128,256]{2,1,0:T(8,128)(2,1)S(1)} %get-tuple-element.17.own, bf16[16,128,256]{2,1,0:T(8,128)(2,1)S(1)} %collective-permute-done.1.other, bf16[256,512]{1,0:T(8,128)(2,1)S(1)} %collective-permute-done.4.refs_0_, ...), custom_call_target="tpu_custom_call" | custom-call | flops 402653184 | bytes 2359296 | tf_op jit(solution)/shard_map/pallas_call | solution.py:199
  44.3 0.7 %collective-permute-start.17 = (bf16[128,512]{1,0:T(8,128)(2,1)S(1)}, bf16[128,512]{1,0:T(8,128)(2,1)S(1)}, u32[]{:S(2)}, u32[]{:S(2)}) collective-permute-start(bf16[128,512]{1,0:T(8,128)(2,1)S(1)} %get-tuple-element.24), channel_id=1, source_target_pairs={{0,16},{16,0},{1,17},{17,1},{2,18},{18,2},{3,19},{19,3},{4,20},{20... | collective-permute-start | bytes 393224 | tf_op jit(solution)/shard_map/ppermute | solution.py:247
  45.0 5.2 %collective-permute-done.18.second = bf16[256,512]{1,0:T(8,128)(2,1)S(1)} collective-permute-done((bf16[256,512]{1,0:T(8,128)(2,1)S(1)}, bf16[256,512]{1,0:T(8,128)(2,1)S(1)}, u32[]{:S(2)}, u32[]{:S(2)}) %collective-permute-start.18) | collective-permute-done | bytes 262176 | tf_op jit(solution)/shard_map/ppermute | solution.py:240
  50.2 1.5 %shard_map.83 = (bf16[256,512]{1,0:T(8,128)(2,1)}, f32[512,512]{1,0:T(8,128)}, f32[512,512]{1,0:T(8,128)}) custom-call(bf16[256,512]{1,0:T(8,128)(2,1)S(1)} %shard_map.78.first, bf16[256,512]{1,0:T(8,128)(2,1)S(1)} %collective-permute-done.18.second, f32[512,512]{1,0:T(8,128)S(1)} %copy-done.1, ...), custom_call_target="tpu_custom_call", output_to_operand_aliasing={{1}: (5, {}), {2}: (6, {})} | custom-call | flops 3932160 | bytes 2883584 | tf_op jit(solution)/shard_map/pallas_call | solution.py:160
  51.8 0.9 %collective-permute-done.17.other_part = bf16[128,512]{1,0:T(8,128)(2,1)S(1)} collective-permute-done((bf16[128,512]{1,0:T(8,128)(2,1)S(1)}, bf16[128,512]{1,0:T(8,128)(2,1)S(1)}, u32[]{:S(2)}, u32[]{:S(2)}) %collective-permute-start.17) | collective-permute-done | bytes 131104 | tf_op jit(solution)/shard_map/ppermute | solution.py:247
  52.7 0.7 %shard_map.82 = bf16[128,512]{1,0:T(8,128)(2,1)} custom-call(f32[128,512]{1,0:T(8,128)S(1)} %get-tuple-element.23.mine_part, bf16[128,512]{1,0:T(8,128)(2,1)S(1)} %collective-permute-done.17.other_part, f32[128,1]{1,0:T(8,128)S(1)} %get-tuple-element.25.inverse), custom_call_target="tpu_custom_call" | custom-call | tf_op jit(solution)/shard_map/pallas_call | solution.py:248
  (24 shorter events, 0.2 us)
Async XLA Ops:
  0.6 1.2 %copy-start = (f32[1,512,512]{2,1,0:T(8,128)S(1)}, f32[1,512,512]{2,1,0:T(8,128)}, u32[]{:S(2)}) copy-start(f32[1,512,512]{2,1,0:T(8,128)} %param.9) | copy-start | bytes 3145732
  1.9 9.4 %copy-start.1 = (f32[512,512]{1,0:T(8,128)S(1)}, f32[512,512]{1,0:T(8,128)}, u32[]{:S(2)}) copy-start(f32[512,512]{1,0:T(8,128)} %master.3) | copy-start | bytes 3145732
  1.9 9.4 %copy-start.2 = (f32[512,512]{1,0:T(8,128)S(1)}, f32[512,512]{1,0:T(8,128)}, u32[]{:S(2)}) copy-start(f32[512,512]{1,0:T(8,128)} %momentum.3) | copy-start | bytes 3145732
  1.9 9.4 %copy-start.4 = (f32[8192]{0:T(1024)S(1)}, f32[8192]{0:T(1024)}, u32[]{:S(2)}) copy-start(f32[8192]{0:T(1024)} %param.6) | copy-start | bytes 98308
  1.9 9.3 %collective-permute-start = (bf16[256,512]{1,0:T(8,128)(2,1)S(1)}, bf16[256,512]{1,0:T(8,128)(2,1)S(1)}, u32[]{:S(2)}, u32[]{:S(2)}) collective-permute-start(bf16[256,512]{1,0:T(8,128)(2,1)S(1)} %shard_map.78.first), channel_id=1, source_target_pairs={{0,16},{16,0},{1,17},{17,1},{2,18},{18,2},{3,19},{19,3},{4,20},{20... | collective-permute-start | bytes 786440 | tf_op jit(solution)/shard_map/ppermute | solution.py:223
  5.0 1.6 %copy-start.3 = (bf16[128,8192]{1,0:T(8,128)(2,1)S(1)}, bf16[128,8192]{1,0:T(8,128)(2,1)}, u32[]{:S(2)}) copy-start(bf16[128,8192]{1,0:T(8,128)(2,1)} %tokens.1) | copy-start | bytes 6291460
  12.8 6.4 %collective-permute-start.2 = (bf16[256,512]{1,0:T(8,128)(2,1)S(1)}, bf16[256,512]{1,0:T(8,128)(2,1)S(1)}, u32[]{:S(2)}, u32[]{:S(2)}) collective-permute-start(bf16[256,512]{1,0:T(8,128)(2,1)S(1)} %get-tuple-element.22.refs_0_), channel_id=1, source_target_pairs={{0,4},{1,3},{2,0},{3,7},{4,8},{5,1},{6,2},{7,11},{8,12},{9,5},{10,... | collective-permute-start | bytes 786440 | tf_op jit(solution)/shard_map/ppermute | solution.py:234
  14.6 23.7 %collective-permute-start.1 = (bf16[16,128,256]{2,1,0:T(8,128)(2,1)S(1)}, bf16[16,128,256]{2,1,0:T(8,128)(2,1)S(1)}, u32[]{:S(2)}, u32[]{:S(2)}) collective-permute-start(bf16[16,128,256]{2,1,0:T(8,128)(2,1)S(1)} %get-tuple-element.20), channel_id=1, source_target_pairs={{0,16},{16,0},{1,17},{17,1},{2,18},{18,2},{3,19},{19,3},{4,20},{20... | collective-permute-start | bytes 3145736 | tf_op jit(solution)/shard_map/ppermute | solution.py:229
  16.1 4.9 %collective-permute-start.5 = (bf16[256,512]{1,0:T(8,128)(2,1)S(1)}, bf16[256,512]{1,0:T(8,128)(2,1)S(1)}, u32[]{:S(2)}, u32[]{:S(2)}) collective-permute-start(bf16[256,512]{1,0:T(8,128)(2,1)S(1)} %get-tuple-element.22.refs_0_), channel_id=1, source_target_pairs={{0,1},{1,0},{2,3},{3,2},{4,5},{5,4},{6,7},{7,6},{8,9},{9,8},{10,11... | collective-permute-start | bytes 786440 | tf_op jit(solution)/shard_map/ppermute | solution.py:231
  19.2 6.4 %collective-permute-start.3 = (bf16[256,512]{1,0:T(8,128)(2,1)S(1)}, bf16[256,512]{1,0:T(8,128)(2,1)S(1)}, u32[]{:S(2)}, u32[]{:S(2)}) collective-permute-start(bf16[256,512]{1,0:T(8,128)(2,1)S(1)} %collective-permute-done.2.refs_2_), channel_id=1, source_target_pairs={{0,4},{1,3},{2,0},{3,7},{4,8},{5,1},{6,2},{7,11},{8,12},{9,5},{10,... | collective-permute-start | bytes 786440 | tf_op jit(solution)/shard_map/ppermute | solution.py:234
  21.0 7.4 %collective-permute-start.6 = (bf16[256,512]{1,0:T(8,128)(2,1)S(1)}, bf16[256,512]{1,0:T(8,128)(2,1)S(1)}, u32[]{:S(2)}, u32[]{:S(2)}) collective-permute-start(bf16[256,512]{1,0:T(8,128)(2,1)S(1)} %collective-permute-done.5.refs_1_), channel_id=1, source_target_pairs={{0,4},{1,3},{2,0},{3,7},{4,8},{5,1},{6,2},{7,11},{8,12},{9,5},{10,... | collective-permute-start | bytes 786440 | tf_op jit(solution)/shard_map/ppermute | solution.py:234
  25.6 6.4 %collective-permute-start.4 = (bf16[256,512]{1,0:T(8,128)(2,1)S(1)}, bf16[256,512]{1,0:T(8,128)(2,1)S(1)}, u32[]{:S(2)}, u32[]{:S(2)}) collective-permute-start(bf16[256,512]{1,0:T(8,128)(2,1)S(1)} %collective-permute-done.3.refs_6_), channel_id=1, source_target_pairs={{0,4},{1,3},{2,0},{3,7},{4,8},{5,1},{6,2},{7,11},{8,12},{9,5},{10,... | collective-permute-start | bytes 786440 | tf_op jit(solution)/shard_map/ppermute | solution.py:234
  28.4 6.4 %collective-permute-start.7 = (bf16[256,512]{1,0:T(8,128)(2,1)S(1)}, bf16[256,512]{1,0:T(8,128)(2,1)S(1)}, u32[]{:S(2)}, u32[]{:S(2)}) collective-permute-start(bf16[256,512]{1,0:T(8,128)(2,1)S(1)} %collective-permute-done.6.refs_3_), channel_id=1, source_target_pairs={{0,4},{1,3},{2,0},{3,7},{4,8},{5,1},{6,2},{7,11},{8,12},{9,5},{10,... | collective-permute-start | bytes 786440 | tf_op jit(solution)/shard_map/ppermute | solution.py:234
  30.2 6.4 %collective-permute-start.13 = (bf16[256,512]{1,0:T(8,128)(2,1)S(1)}, bf16[256,512]{1,0:T(8,128)(2,1)S(1)}, u32[]{:S(2)}, u32[]{:S(2)}) collective-permute-start(bf16[256,512]{1,0:T(8,128)(2,1)S(1)} %collective-permute-done.2.refs_2_), channel_id=1, source_target_pairs={{0,1},{1,0},{2,3},{3,2},{4,5},{5,4},{6,7},{7,6},{8,9},{9,8},{10,11... | collective-permute-start | bytes 786440 | tf_op jit(solution)/shard_map/ppermute | solution.py:235
  30.2 6.4 %collective-permute-start.15 = (bf16[256,512]{1,0:T(8,128)(2,1)S(1)}, bf16[256,512]{1,0:T(8,128)(2,1)S(1)}, u32[]{:S(2)}, u32[]{:S(2)}) collective-permute-start(bf16[256,512]{1,0:T(8,128)(2,1)S(1)} %collective-permute-done.3.refs_6_), channel_id=1, source_target_pairs={{0,1},{1,0},{2,3},{3,2},{4,5},{5,4},{6,7},{7,6},{8,9},{9,8},{10,11... | collective-permute-start | bytes 786440 | tf_op jit(solution)/shard_map/ppermute | solution.py:235
  31.9 6.4 %collective-permute-start.11 = (bf16[256,512]{1,0:T(8,128)(2,1)S(1)}, bf16[256,512]{1,0:T(8,128)(2,1)S(1)}, u32[]{:S(2)}, u32[]{:S(2)}) collective-permute-start(bf16[256,512]{1,0:T(8,128)(2,1)S(1)} %collective-permute-done.4.refs_0_), channel_id=1, source_target_pairs={{0,4},{1,3},{2,0},{3,7},{4,8},{5,1},{6,2},{7,11},{8,12},{9,5},{10,... | collective-permute-start | bytes 786440 | tf_op jit(solution)/shard_map/ppermute | solution.py:236
  34.8 6.4 %collective-permute-start.8 = (bf16[256,512]{1,0:T(8,128)(2,1)S(1)}, bf16[256,512]{1,0:T(8,128)(2,1)S(1)}, u32[]{:S(2)}, u32[]{:S(2)}) collective-permute-start(bf16[256,512]{1,0:T(8,128)(2,1)S(1)} %collective-permute-done.7.refs_7_), channel_id=1, source_target_pairs={{0,4},{1,3},{2,0},{3,7},{4,8},{5,1},{6,2},{7,11},{8,12},{9,5},{10,... | collective-permute-start | bytes 786440 | tf_op jit(solution)/shard_map/ppermute | solution.py:234
  36.6 4.6 %collective-permute-start.14 = (bf16[256,512]{1,0:T(8,128)(2,1)S(1)}, bf16[256,512]{1,0:T(8,128)(2,1)S(1)}, u32[]{:S(2)}, u32[]{:S(2)}) collective-permute-start(bf16[256,512]{1,0:T(8,128)(2,1)S(1)} %collective-permute-done.6.refs_3_), channel_id=1, source_target_pairs={{0,1},{1,0},{2,3},{3,2},{4,5},{5,4},{6,7},{7,6},{8,9},{9,8},{10,11... | collective-permute-start | bytes 786440 | tf_op jit(solution)/shard_map/ppermute | solution.py:235
  36.6 6.3 %collective-permute-start.16 = (bf16[256,512]{1,0:T(8,128)(2,1)S(1)}, bf16[256,512]{1,0:T(8,128)(2,1)S(1)}, u32[]{:S(2)}, u32[]{:S(2)}) collective-permute-start(bf16[256,512]{1,0:T(8,128)(2,1)S(1)} %collective-permute-done.7.refs_7_), channel_id=1, source_target_pairs={{0,1},{1,0},{2,3},{3,2},{4,5},{5,4},{6,7},{7,6},{8,9},{9,8},{10,11... | collective-permute-start | bytes 786440 | tf_op jit(solution)/shard_map/ppermute | solution.py:235
  38.3 5.4 %collective-permute-start.9 = (bf16[256,512]{1,0:T(8,128)(2,1)S(1)}, bf16[256,512]{1,0:T(8,128)(2,1)S(1)}, u32[]{:S(2)}, u32[]{:S(2)}) collective-permute-start(bf16[256,512]{1,0:T(8,128)(2,1)S(1)} %collective-permute-done.4.refs_0_), channel_id=1, source_target_pairs={{0,1},{1,0},{2,3},{3,2},{4,5},{5,4},{6,7},{7,6},{8,9},{9,8},{10,11... | collective-permute-start | bytes 786440 | tf_op jit(solution)/shard_map/ppermute | solution.py:235
  38.3 5.4 %collective-permute-start.12 = (bf16[256,512]{1,0:T(8,128)(2,1)S(1)}, bf16[256,512]{1,0:T(8,128)(2,1)S(1)}, u32[]{:S(2)}, u32[]{:S(2)}) collective-permute-start(bf16[256,512]{1,0:T(8,128)(2,1)S(1)} %collective-permute-done.11.refs_4_), channel_id=1, source_target_pairs={{0,1},{1,0},{2,3},{3,2},{4,5},{5,4},{6,7},{7,6},{8,9},{9,8},{10,11... | collective-permute-start | bytes 786440 | tf_op jit(solution)/shard_map/ppermute | solution.py:237
  41.1 2.6 %collective-permute-start.10 = (bf16[256,512]{1,0:T(8,128)(2,1)S(1)}, bf16[256,512]{1,0:T(8,128)(2,1)S(1)}, u32[]{:S(2)}, u32[]{:S(2)}) collective-permute-start(bf16[256,512]{1,0:T(8,128)(2,1)S(1)} %collective-permute-done.8.refs_1_), channel_id=1, source_target_pairs={{0,1},{1,0},{2,3},{3,2},{4,5},{5,4},{6,7},{7,6},{8,9},{9,8},{10,11... | collective-permute-start | bytes 786440 | tf_op jit(solution)/shard_map/ppermute | solution.py:235
  41.1 9.1 %collective-permute-start.18 = (bf16[256,512]{1,0:T(8,128)(2,1)S(1)}, bf16[256,512]{1,0:T(8,128)(2,1)S(1)}, u32[]{:S(2)}, u32[]{:S(2)}) collective-permute-start(bf16[256,512]{1,0:T(8,128)(2,1)S(1)} %shard_map.77.first), channel_id=1, source_target_pairs={{0,16},{16,0},{1,17},{17,1},{2,18},{18,2},{3,19},{19,3},{4,20},{20... | collective-permute-start | bytes 786440 | tf_op jit(solution)/shard_map/ppermute | solution.py:240
  44.3 8.3 %collective-permute-start.17 = (bf16[128,512]{1,0:T(8,128)(2,1)S(1)}, bf16[128,512]{1,0:T(8,128)(2,1)S(1)}, u32[]{:S(2)}, u32[]{:S(2)}) collective-permute-start(bf16[128,512]{1,0:T(8,128)(2,1)S(1)} %get-tuple-element.24), channel_id=1, source_target_pairs={{0,16},{16,0},{1,17},{17,1},{2,18},{18,2},{3,19},{19,3},{4,20},{20... | collective-permute-start | bytes 393224 | tf_op jit(solution)/shard_map/ppermute | solution.py:247

commit v2 on v0

--- a/solution.py
+++ b/solution.py
@@ -1,16 +1,332 @@
+import functools
+
 import jax
 import jax.numpy as jnp
 from jax import lax
+from jax.experimental import pallas as pl
+from jax.experimental.pallas import tpu as pltpu
 from jax.sharding import PartitionSpec as P
 
 BLOCK = 128
-
+CORES = 2
+RING_LIMIT = 16
 
 outer_rate = 0.7
 outer_mu = 0.9
-
-
-def on_device(tokens, norm_gain, master, momentum, pseudo_grad):
+VMEM = pl.BlockSpec(memory_space=pltpu.VMEM)
+VMEM_LIMIT = 40 * 1024 * 1024
+
+
+def params():
+    return pltpu.CompilerParams(vmem_limit_bytes=VMEM_LIMIT)
+
+
+def chip_at(place, chips):
+    up = 2 * place
+    down = 2 * (chips - 1 - place) + 1
+    if isinstance(place, int):
+        return up if place < chips // 2 else down
+    return jnp.where(place < chips // 2, up, down)
+
+
+def place_of(chip, chips):
+    if isinstance(chip, int):
+        return chip // 2 if chip % 2 == 0 else chips - 1 - chip // 2
+    return jnp.where(chip % 2 == 0, chip // 2, chips - 1 - chip // 2)
+
+
+def ring_pairs(chips):
+    pairs = []
+    for chip in range(chips):
+        for core in range(CORES):
+            step = 1 if core == 0 else -1
+            target = chip_at((place_of(chip, chips) + step) % chips, chips)
+            pairs.append((chip * CORES + core, target * CORES + core))
+    return pairs
+
+
+def swap_pairs(chips):
+    return [(f, f ^ 1) for f in range(CORES * chips)]
+
+
+def slots(chips):
+    shared = []
+    for step in range(1, chips // 2):
+        shared += [(step, 0), (step, 1), (-step, 1), (-step, 0)]
+    return shared + [(chips // 2, 0), (chips // 2, 1)], [(0, 0), (0, 1)]
+
+
+def shard_of(slot, chips):
+    back, other = slot
+    me = lax.axis_index("fsdp")
+    core = me % CORES
+    direction = jnp.where(core == 0, -1, 1)
+    place = (place_of(me // CORES, chips) + direction * back + chips) % chips
+    return chip_at(place, chips) * CORES + (1 - core if other else core)
+
+
+def cast_kernel(grad, out):
+    out[...] = grad[...].astype(out.dtype)
+
+
+def cast_half(grad, which):
+    rows, cols = grad.shape
+    half = rows // 2
+    steps = 2
+    tall = half // steps
+    return pl.pallas_call(
+        cast_kernel,
+        grid=(steps,),
+        in_specs=[pl.BlockSpec((tall, cols), lambda g: (which() * steps + g, 0))],
+        out_specs=pl.BlockSpec((tall, cols), lambda g: (g, 0)),
+        out_shape=jax.ShapeDtypeStruct((half, cols), jnp.bfloat16),
+        compiler_params=params(),
+        cost_estimate=pl.CostEstimate(flops=half * cols, bytes_accessed=6 * half * cols, transcendentals=0),
+    )(grad)
+
+
+def mine():
+    return lax.axis_index("island")
+
+
+def others():
+    return 1 - lax.axis_index("island")
+
+
+def token_kernel(chips, half, tokens, own, sent, whole, inverse):
+    rows, width = tokens.shape
+    shared, kept = slots(chips)
+
+    def columns(slot, which):
+        start = shard_of(slot, chips) * 2 * half + which * half
+        return tokens[:, pl.ds(pl.multiple_of(start, half), half)]
+
+    for k, slot in enumerate(shared):
+        own[k] = columns(slot, mine())
+        sent[k] = columns(slot, others())
+    for k, slot in enumerate(kept):
+        whole[2 * k] = columns(slot, mine())
+        whole[2 * k + 1] = columns(slot, others())
+    total = jnp.zeros((rows, BLOCK), jnp.float32)
+    for k in range(width // BLOCK):
+        part = tokens[:, k * BLOCK : (k + 1) * BLOCK].astype(jnp.float32)
+        total += part * part
+    mean = jnp.sum(total, axis=1, keepdims=True) / width
+    inverse[...] = lax.rsqrt(mean + 1e-05) / jnp.sqrt(jnp.float32(width))
+
+
+def split_tokens(tokens, chips):
+    rows, width = tokens.shape
+    half = width // (chips * CORES * 2)
+    shared, kept = slots(chips)
+    split = jax.ShapeDtypeStruct((len(shared), rows, half), tokens.dtype)
+    whole = jax.ShapeDtypeStruct((2 * len(kept), rows, half), tokens.dtype)
+    return pl.pallas_call(
+        functools.partial(token_kernel, chips, half),
+        in_specs=[VMEM],
+        out_specs=[VMEM] * 4,
+        out_shape=[split, split, whole, jax.ShapeDtypeStruct((rows, 1), jnp.float32)],
+        compiler_params=params(),
+        cost_estimate=pl.CostEstimate(flops=2 * rows * width, bytes_accessed=4 * rows * width, transcendentals=0),
+    )(tokens)
+
+
+def synced(a, b):
+    a, b = a.astype(jnp.float32), b.astype(jnp.float32)
+    peak_a = jnp.max(jnp.abs(a), axis=1, keepdims=True)
+    peak_b = jnp.max(jnp.abs(b), axis=1, keepdims=True)
+    shared = (peak_a + peak_b) / 2 + 1e-06
+    over = 1.0 / shared
+    low_a = jnp.clip(a * over, -1.0, 1.0).astype(jnp.bfloat16).astype(jnp.float32)
+    low_b = jnp.clip(b * over, -1.0, 1.0).astype(jnp.bfloat16).astype(jnp.float32)
+    return shared * (low_a + low_b) / 2
+
+
+def gains_of(gain, row):
+    return jnp.transpose(jnp.broadcast_to(gain[pl.ds(row // BLOCK, 1), :], (BLOCK, BLOCK)))
+
+
+def weight_kernel(which, first, second, master, momentum, gain, weight):
+    half, cols = first.shape
+    base = lax.axis_index("fsdp") * (2 * half)
+    for start in range(0, half, BLOCK):
+        rows = slice(start, start + BLOCK)
+        there = which() * half + start
+        held = pl.ds(pl.multiple_of(there, BLOCK), BLOCK)
+        gains = gains_of(gain, base + there)
+        for col in range(0, cols, BLOCK):
+            at = slice(col, col + BLOCK)
+            outer_grad = synced(first[rows, at], second[rows, at])
+            moved = outer_mu * momentum[held, at] + outer_grad
+            fresh = master[held, at] - outer_rate * (outer_grad + outer_mu * moved)
+            weight[rows, at] = (gains * fresh).astype(weight.dtype)
+
+
+def sync_weight(which, first, second, master, momentum, gain):
+    half, cols = first.shape
+    return pl.pallas_call(
+        functools.partial(weight_kernel, which),
+        in_specs=[VMEM] * 5,
+        out_specs=VMEM,
+        out_shape=jax.ShapeDtypeStruct((half, cols), jnp.bfloat16),
+        compiler_params=params(),
+        cost_estimate=pl.CostEstimate(
+            flops=30 * half * cols, bytes_accessed=14 * half * cols, transcendentals=0
+        ),
+    )(first, second, master, momentum, gain)
+
+
+def outer_kernel(here_a, here_b, there_a, there_b, master, momentum, master_new, momentum_new):
+    half, cols = here_a.shape
+    for which, a, b in ((mine(), here_a, here_b), (others(), there_a, there_b)):
+        for start in range(0, half, BLOCK):
+            rows = slice(start, start + BLOCK)
+            held = pl.ds(pl.multiple_of(which * half + start, BLOCK), BLOCK)
+            for col in range(0, cols, BLOCK):
+                at = slice(col, col + BLOCK)
+                outer_grad = synced(a[rows, at], b[rows, at])
+                moved = outer_mu * momentum[held, at] + outer_grad
+                momentum_new[held, at] = moved
+                master_new[held, at] = master[held, at] - outer_rate * (outer_grad + outer_mu * moved)
+
+
+def sync_outer(here_a, here_b, there_a, there_b, master, momentum):
+    rows, cols = master.shape
+    full = jax.ShapeDtypeStruct(master.shape, jnp.float32)
+    return pl.pallas_call(
+        outer_kernel,
+        in_specs=[VMEM] * 6,
+        out_specs=[VMEM] * 2,
+        out_shape=[full, full],
+        compiler_params=params(),
+        cost_estimate=pl.CostEstimate(flops=30 * rows * cols, bytes_accessed=20 * rows * cols, transcendentals=0),
+    )(here_a, here_b, there_a, there_b, master, momentum)
+
+
+def cost_of(blocks, rows):
+    depth, cols = blocks[0].shape
+    count = len(blocks)
+    return pl.CostEstimate(
+        flops=2 * rows * cols * depth * count, bytes_accessed=2 * count * depth * (cols + rows), transcendentals=0
+    )
+
+
+def own_kernel(first, count, whole, *refs):
+    blocks, out = refs[:count], refs[-1]
+    total = refs[count][...] if len(refs) > count + 1 else jnp.zeros(out.shape, jnp.float32)
+    for k, block in enumerate(blocks):
+        total += jnp.dot(whole[first + k], block[...], preferred_element_type=jnp.float32)
+    out[...] = total
+
+
+def dot_own(first, whole, blocks, *total):
+    return pl.pallas_call(
+        functools.partial(own_kernel, first, len(blocks)),
+        in_specs=[VMEM] * (1 + len(blocks) + len(total)),
+        out_specs=VMEM,
+        out_shape=jax.ShapeDtypeStruct((whole.shape[1], blocks[0].shape[1]), jnp.float32),
+        compiler_params=params(),
+        cost_estimate=cost_of(blocks, whole.shape[1]),
+    )(whole, *blocks, *total)
+
+
+def early_kernel(own, other, *refs):
+    *blocks, total = refs
+    total[...] = jnp.zeros(total.shape, jnp.float32)
+    for k, block in enumerate(blocks):
+        left = jnp.concatenate([own[k], other[k]], axis=0)
+        total[...] += jnp.dot(left, block[...], preferred_element_type=jnp.float32)
+
+
+def dot_early(own, other, blocks):
+    shape = (2 * own.shape[1], blocks[0].shape[1])
+    return pl.pallas_call(
+        early_kernel,
+        in_specs=[VMEM] * (2 + len(blocks)),
+        out_specs=VMEM,
+        out_shape=jax.ShapeDtypeStruct(shape, jnp.float32),
+        compiler_params=params(),
+        cost_estimate=cost_of(blocks, shape[0]),
+    )(own, other, *blocks)
+
+
+def late_kernel(first, own, other, early, *refs):
+    *blocks, mine_part, sent_part = refs
+    rows = own.shape[1]
+    total = early[...]
+    for k, block in enumerate(blocks):
+        left = jnp.concatenate([own[first + k], other[first + k]], axis=0)
+        total += jnp.dot(left, block[...], preferred_element_type=jnp.float32)
+    mine_part[...] = total[:rows]
+    sent_part[...] = total[rows:].astype(sent_part.dtype)
+
+
+def dot_late(first, own, other, early, blocks):
+    shape = (own.shape[1], blocks[0].shape[1])
+    return pl.pallas_call(
+        functools.partial(late_kernel, first),
+        in_specs=[VMEM] * (3 + len(blocks)),
+        out_specs=[VMEM] * 2,
+        out_shape=[jax.ShapeDtypeStruct(shape, jnp.float32), jax.ShapeDtypeStruct(shape, jnp.bfloat16)],
+        compiler_params=params(),
+        cost_estimate=cost_of(blocks, 2 * shape[0]),
+    )(own, other, early, *blocks)
+
+
+def close_kernel(own_part, mine_part, other_part, inverse, keys):
+    total = own_part[...] + mine_part[...] + other_part[...].astype(jnp.float32)
+    keys[...] = (total * inverse[...]).astype(keys.dtype)
+
+
+def close(own_part, mine_part, other_part, inverse):
+    return pl.pallas_call(
+        close_kernel,
+        in_specs=[VMEM] * 4,
+        out_specs=VMEM,
+        out_shape=jax.ShapeDtypeStruct(mine_part.shape, jnp.bfloat16),
+        compiler_params=params(),
+    )(own_part, mine_part, other_part, inverse)
+
+
+def by_permutes(tokens, norm_gain, master, momentum, pseudo_grad):
+    chips = lax.axis_size("fsdp") // CORES
+    ring = functools.partial(lax.ppermute, axis_name="fsdp", perm=ring_pairs(chips))
+    swap = functools.partial(lax.ppermute, axis_name="fsdp", perm=swap_pairs(chips))
+    cross = functools.partial(lax.ppermute, axis_name="island", perm=[(0, 1), (1, 0)])
+    tie = lax.optimization_barrier
+
+    gain = norm_gain.reshape(-1, BLOCK)
+    grad_sent = cast_half(pseudo_grad[0], others)
+    grad_here = cross(grad_sent)
+    grad_own = cast_half(pseudo_grad[0], mine)
+    grad_there = cross(grad_own)
+    own, sent, whole, inverse = split_tokens(tokens, chips)
+    grad_here, own = tie((grad_here, own))
+
+    a = weight = sync_weight(mine, grad_own, grad_here, master, momentum, gain)
+    weight_over = sync_weight(others, grad_sent, grad_there, master, momentum, gain)
+    near_over = swap(weight_over)
+    b = near = swap(weight)
+    other = cross(sent)
+    blocks = []
+    for step in range(1, chips // 2):
+        a, b = ring(a), ring(b)
+        if step == 1:
+            b, near_over = tie((b, near_over))
+        blocks += [a, b, swap(a), swap(b)]
+    a = ring(a)
+    late = [a, swap(a)]
+
+    master_new, momentum_new = sync_outer(grad_own, grad_here, grad_sent, grad_there, master, momentum)
+    early = dot_early(own, other, blocks)
+    mine_part, sent_part = dot_late(len(blocks), own, other, early, late)
+    other_part = cross(sent_part)
+    own_part = dot_own(0, whole, [weight, weight_over, near, near_over])
+    keys = close(own_part, mine_part, other_part, inverse)
+    return (keys, master_new, momentum_new)
+
+
+def by_gathers(tokens, norm_gain, master, momentum, pseudo_grad):
     islands = lax.axis_size("island")
     island_grad = pseudo_grad[0]
     row_total, col_total = island_grad.shape
@@ -36,6 +352,15 @@
     return (keys, master_new, momentum_new)
 
 
+def on_device(tokens, norm_gain, master, momentum, pseudo_grad):
+    shards = lax.axis_size("fsdp")
+    rows = master.shape[0]
+    ringed = shards % (2 * CORES) == 0 and 4 * CORES <= shards <= RING_LIMIT * CORES
+    if lax.axis_size("island") == 2 and ringed and rows % (2 * BLOCK) == 0:
+        return by_permutes(tokens, norm_gain, master, momentum, pseudo_grad)
+    return by_gathers(tokens, norm_gain, master, momentum, pseudo_grad)
+
+
 def solution(mesh):
     placed = (
         P(("island", "fsdp"), None),

time: 132 us -> 48 us (0.36)
  waiting for transfers between devices: 99.4 us -> 14.3 us
  starting transfers between devices: 0.08 us -> 23.2 us
  between operations: 14.1 us -> 0.76 us
  other arithmetic: 9.2 us -> 0 us
  Pallas kernels: 0 us -> 6.65 us
  matrix products: 5.34 us -> 0 us
    all_gather x2 -> x0, waiting for transfers between devices: 99.3 us -> none  [the longest x1 74.5 us: on_device(): gathered = lax.all_gather(weight, 'fsdp', axis=0, tiled=True)]
    ppermute x0 -> x20, starting transfers between devices: none -> 23.2 us  [the longest x6 13.1 us: by_permutes(): a, b = (ring(a), ring(b))]
    ppermute x0 -> x20, waiting for transfers between devices: none -> 14.3 us  [the longest x1 4.68 us: by_permutes(): grad_here = cross(grad_sent)]
    pallas_call x0 -> x10, Pallas kernels: none -> 6.65 us  [the longest x1 2.28 us: sync_outer(): pl.pallas_call(outer_kernel, in_specs=[VMEM] * 6, out_specs=[VMEM] * 2, o...]
    dot_general x1 -> x0, matrix products: 5.34 us -> none  [on_device(): product = jnp.dot(normed, gathered, preferred_element_type=jnp.float32)]
    convert_element_type x2 -> x0, other arithmetic: 4.19 us -> none  [the longest x1 2.11 us: on_device(): weight = master_new.astype(jnp.bfloat16)]
    abs x1 -> x0, other arithmetic: 2.86 us -> none  [on_device(): peaks_all = jnp.max(jnp.abs(grouped_all), axis=3)]
    abs x1 -> x0, local copies, waits for them, and re-layouts: 1.93 us -> none  [on_device(): peaks_all = jnp.max(jnp.abs(grouped_all), axis=3)]
  transfers between devices with their start and end apart: 2 -> 20, of which waited for: 2 -> 10; matrix products, arithmetic and copies ran while one was open for 0% -> 0% of each run, Pallas kernels for 0% -> 12%
where the time goes in v2:
time: 48 us; the launch traced here: 47.8 us
  starting transfers between devices  23.2 us (48%)
  waiting for transfers between devices  14.3 us (30%)
  Pallas kernels  6.65 us (14%)
  local copies, waits for them, and re-layouts  2.82 us (6%)
  between operations  0.76 us (2%)
    ppermute x6, starting transfers between devices, by_permutes(): a, b = (ring(a), ring(b))  13.1 us
    ppermute x1, waiting for transfers between devices, by_permutes(): grad_here = cross(grad_sent)  4.68 us
    ppermute x6, waiting for transfers between devices, by_permutes(): a, b = (ring(a), ring(b))  4.12 us
    ppermute x1, starting transfers between devices, by_permutes(): grad_here = cross(grad_sent)  3.03 us
    unnamed x10, local copies, waits for them, and re-layouts  2.82 us
    ppermute x1, starting transfers between devices, by_permutes(): a = ring(a)  2.38 us
    pallas_call x1, Pallas kernels, sync_outer(): pl.pallas_call(outer_kernel, in_specs=[VMEM] * 6, out_specs=[VMEM] * 2, o...  2.28 us
    ppermute x1, starting transfers between devices, by_permutes(): other_part = cross(sent_part)  1.81 us
  transfers between devices with their start and end apart: 20, of which 10 were waited for; matrix products, arithmetic and copies ran while one was open for 0% of the time, Pallas kernels for 12%

profile of v2, /device:TPU:0, one launch (start us, length us, event | category | flops | bytes accessed | tf_op | source)
XLA Modules:
  0.0 47.8 jit_solution(10916003632894198569)
XLA Ops:
  0.6 1.2 %copy-done.2 = f32[1,512,512]{2,1,0:T(8,128)S(1)} copy-done((f32[1,512,512]{2,1,0:T(8,128)S(1)}, f32[1,512,512]{2,1,0:T(8,128)}, u32[]{:S(2)}) %copy-start.2) | copy-done | bytes 1048600
  1.9 3.0 %collective-permute-start = (bf16[256,512]{1,0:T(8,128)(2,1)S(1)}, bf16[256,512]{1,0:T(8,128)(2,1)S(1)}, u32[]{:S(2)}, u32[]{:S(2)}) collective-permute-start(bf16[256,512]{1,0:T(8,128)(2,1)S(1)} %shard_map.78.first.there_a), channel_id=1, source_target_pairs={{0,16},{16,0},{1,17},{17,1},{2,18},{18,2},{3,19},{19,3},{4,20},{20... | collective-permute-start | bytes 786440 | tf_op jit(solution)/shard_map/ppermute | solution.py:300
  5.2 1.6 %copy-done.3 = bf16[128,8192]{1,0:T(8,128)(2,1)S(1)} copy-done((bf16[128,8192]{1,0:T(8,128)(2,1)S(1)}, bf16[128,8192]{1,0:T(8,128)(2,1)}, u32[]{:S(2)}) %copy-start.3) | copy-done | bytes 2097176
  6.7 0.7 %shard_map.76 = (bf16[14,128,256]{2,1,0:T(8,128)(2,1)S(1)}, bf16[14,128,256]{2,1,0:T(8,128)(2,1)S(1)}, bf16[4,128,256]{2,1,0:T(8,128)(2,1)S(1)}, f32[128,1]{1,0:T(8,128)S(1)}) custom-call(bf16[128,8192]{1,0:T(8,128)(2,1)S(1)} %copy-done.3), custom_call_target="tpu_custom_call" | custom-call | flops 2097152 | bytes 4194304 | tf_op jit(solution)/shard_map/pallas_call | solution.py:124
  7.4 4.7 %collective-permute-done.second.here_b = bf16[256,512]{1,0:T(8,128)(2,1)S(1)} collective-permute-done((bf16[256,512]{1,0:T(8,128)(2,1)S(1)}, bf16[256,512]{1,0:T(8,128)(2,1)S(1)}, u32[]{:S(2)}, u32[]{:S(2)}) %collective-permute-start) | collective-permute-done | bytes 262176 | tf_op jit(solution)/shard_map/ppermute | solution.py:300
  12.1 0.6 %shard_map.79.refs_0_ = bf16[256,512]{1,0:T(8,128)(2,1)S(1)} custom-call(bf16[256,512]{1,0:T(8,128)(2,1)S(1)} %shard_map.77.first.here_a, bf16[256,512]{1,0:T(8,128)(2,1)S(1)} %collective-permute-done.second.here_b, f32[512,512]{1,0:T(8,128)S(1)} %copy-done, f32[512,512]{1,0:T(8,128)S(1)} %copy-done.1, f32[64,128]{1,0:T(8,128)S(1)} %bitcast.4), custom_call_target="tpu_custom_call" | custom-call | flops 3932160 | bytes 1835008 | tf_op jit(solution)/shard_map/pallas_call | solution.py:167
  12.8 2.2 %collective-permute-start.6 = (bf16[256,512]{1,0:T(8,128)(2,1)S(1)}, bf16[256,512]{1,0:T(8,128)(2,1)S(1)}, u32[]{:S(2)}, u32[]{:S(2)}) collective-permute-start(bf16[256,512]{1,0:T(8,128)(2,1)S(1)} %shard_map.79.refs_0_), channel_id=1, source_target_pairs={{0,4},{1,3},{2,0},{3,7},{4,8},{5,1},{6,2},{7,11},{8,12},{9,5},{10,... | collective-permute-start | bytes 786440 | tf_op jit(solution)/shard_map/ppermute | solution.py:313
  15.0 1.5 %collective-permute-start.5 = (bf16[14,128,256]{2,1,0:T(8,128)(2,1)S(1)}, bf16[14,128,256]{2,1,0:T(8,128)(2,1)S(1)}, u32[]{:S(2)}, u32[]{:S(2)}) collective-permute-start(bf16[14,128,256]{2,1,0:T(8,128)(2,1)S(1)} %get-tuple-element.20), channel_id=1, source_target_pairs={{0,16},{16,0},{1,17},{17,1},{2,18},{18,2},{3,19},{19,3},{4,20},{20... | collective-permute-start | bytes 2752520 | tf_op jit(solution)/shard_map/ppermute | solution.py:310
  16.5 0.4 collective-permute-done.1.second.there_b
  16.9 0.6 %shard_map.80.refs_1_ = bf16[256,512]{1,0:T(8,128)(2,1)S(1)} custom-call(bf16[256,512]{1,0:T(8,128)(2,1)S(1)} %shard_map.78.first.there_a, bf16[256,512]{1,0:T(8,128)(2,1)S(1)} %collective-permute-done.1.second.there_b, f32[512,512]{1,0:T(8,128)S(1)} %copy-done, f32[512,512]{1,0:T(8,128)S(1)} %copy-done.1, f32[64,128]{1,0:T(8,128)S(1)} %bitcast.5), custom_call_target="tpu_custom_call" | custom-call | flops 3932160 | bytes 1835008 | tf_op jit(solution)/shard_map/pallas_call | solution.py:167
  17.6 2.4 %collective-permute-start.3 = (bf16[256,512]{1,0:T(8,128)(2,1)S(1)}, bf16[256,512]{1,0:T(8,128)(2,1)S(1)}, u32[]{:S(2)}, u32[]{:S(2)}) collective-permute-start(bf16[256,512]{1,0:T(8,128)(2,1)S(1)} %collective-permute-done.2.refs_2_), channel_id=1, source_target_pairs={{0,4},{1,3},{2,0},{3,7},{4,8},{5,1},{6,2},{7,11},{8,12},{9,5},{10,... | collective-permute-start | bytes 786440 | tf_op jit(solution)/shard_map/ppermute | solution.py:313
  20.0 1.4 %collective-permute-start.9 = (bf16[256,512]{1,0:T(8,128)(2,1)S(1)}, bf16[256,512]{1,0:T(8,128)(2,1)S(1)}, u32[]{:S(2)}, u32[]{:S(2)}) collective-permute-start(bf16[256,512]{1,0:T(8,128)(2,1)S(1)} %collective-permute-done.6.refs_0_), channel_id=1, source_target_pairs={{0,4},{1,3},{2,0},{3,7},{4,8},{5,1},{6,2},{7,11},{8,12},{9,5},{10,... | collective-permute-start | bytes 786440 | tf_op jit(solution)/shard_map/ppermute | solution.py:313
  21.5 2.6 %collective-permute-done.3.refs_1_ = bf16[256,512]{1,0:T(8,128)(2,1)S(1)} collective-permute-done((bf16[256,512]{1,0:T(8,128)(2,1)S(1)}, bf16[256,512]{1,0:T(8,128)(2,1)S(1)}, u32[]{:S(2)}, u32[]{:S(2)}) %collective-permute-start.3) | collective-permute-done | bytes 262176 | tf_op jit(solution)/shard_map/ppermute | solution.py:313
  24.0 2.4 %collective-permute-start.10 = (bf16[256,512]{1,0:T(8,128)(2,1)S(1)}, bf16[256,512]{1,0:T(8,128)(2,1)S(1)}, u32[]{:S(2)}, u32[]{:S(2)}) collective-permute-start(bf16[256,512]{1,0:T(8,128)(2,1)S(1)} %collective-permute-done.3.refs_1_), channel_id=1, source_target_pairs={{0,4},{1,3},{2,0},{3,7},{4,8},{5,1},{6,2},{7,11},{8,12},{9,5},{10,... | collective-permute-start | bytes 786440 | tf_op jit(solution)/shard_map/ppermute | solution.py:313
  26.4 0.4 collective-permute-done.9.refs_4_
  26.8 2.4 %collective-permute-start.13 = (bf16[256,512]{1,0:T(8,128)(2,1)S(1)}, bf16[256,512]{1,0:T(8,128)(2,1)S(1)}, u32[]{:S(2)}, u32[]{:S(2)}) collective-permute-start(bf16[256,512]{1,0:T(8,128)(2,1)S(1)} %collective-permute-done.9.refs_4_), channel_id=1, source_target_pairs={{0,4},{1,3},{2,0},{3,7},{4,8},{5,1},{6,2},{7,11},{8,12},{9,5},{10,... | collective-permute-start | bytes 786440 | tf_op jit(solution)/shard_map/ppermute | solution.py:313
  29.2 0.5 %collective-permute-start.8 = (bf16[256,512]{1,0:T(8,128)(2,1)S(1)}, bf16[256,512]{1,0:T(8,128)(2,1)S(1)}, u32[]{:S(2)}, u32[]{:S(2)}) collective-permute-start(bf16[256,512]{1,0:T(8,128)(2,1)S(1)} %collective-permute-done.3.refs_1_), channel_id=1, source_target_pairs={{0,1},{1,0},{2,3},{3,2},{4,5},{5,4},{6,7},{7,6},{8,9},{9,8},{10,11... | collective-permute-start | bytes 786440 | tf_op jit(solution)/shard_map/ppermute | solution.py:316
  29.7 0.7 %collective-permute-done.10.refs_5_ = bf16[256,512]{1,0:T(8,128)(2,1)S(1)} collective-permute-done((bf16[256,512]{1,0:T(8,128)(2,1)S(1)}, bf16[256,512]{1,0:T(8,128)(2,1)S(1)}, u32[]{:S(2)}, u32[]{:S(2)}) %collective-permute-start.10) | collective-permute-done | bytes 262176 | tf_op jit(solution)/shard_map/ppermute | solution.py:313
  30.4 2.4 %collective-permute-start.14 = (bf16[256,512]{1,0:T(8,128)(2,1)S(1)}, bf16[256,512]{1,0:T(8,128)(2,1)S(1)}, u32[]{:S(2)}, u32[]{:S(2)}) collective-permute-start(bf16[256,512]{1,0:T(8,128)(2,1)S(1)} %collective-permute-done.10.refs_5_), channel_id=1, source_target_pairs={{0,4},{1,3},{2,0},{3,7},{4,8},{5,1},{6,2},{7,11},{8,12},{9,5},{10,... | collective-permute-start | bytes 786440 | tf_op jit(solution)/shard_map/ppermute | solution.py:313
  32.8 0.4 collective-permute-done.13.refs_8_
  33.2 2.4 %collective-permute-start.17 = (bf16[256,512]{1,0:T(8,128)(2,1)S(1)}, bf16[256,512]{1,0:T(8,128)(2,1)S(1)}, u32[]{:S(2)}, u32[]{:S(2)}) collective-permute-start(bf16[256,512]{1,0:T(8,128)(2,1)S(1)} %collective-permute-done.13.refs_8_), channel_id=1, source_target_pairs={{0,4},{1,3},{2,0},{3,7},{4,8},{5,1},{6,2},{7,11},{8,12},{9,5},{10,... | collective-permute-start | bytes 786440 | tf_op jit(solution)/shard_map/ppermute | solution.py:317
  35.6 1.7 %collective-permute-done.5.other = bf16[14,128,256]{2,1,0:T(8,128)(2,1)S(1)} collective-permute-done((bf16[14,128,256]{2,1,0:T(8,128)(2,1)S(1)}, bf16[14,128,256]{2,1,0:T(8,128)(2,1)S(1)}, u32[]{:S(2)}, u32[]{:S(2)}) %collective-permute-start.5) | collective-permute-done | bytes 917536 | tf_op jit(solution)/shard_map/ppermute | solution.py:310
  37.3 0.5 %collective-permute-start.15 = (bf16[256,512]{1,0:T(8,128)(2,1)S(1)}, bf16[256,512]{1,0:T(8,128)(2,1)S(1)}, u32[]{:S(2)}, u32[]{:S(2)}) collective-permute-start(bf16[256,512]{1,0:T(8,128)(2,1)S(1)} %collective-permute-done.13.refs_8_), channel_id=1, source_target_pairs={{0,1},{1,0},{2,3},{3,2},{4,5},{5,4},{6,7},{7,6},{8,9},{9,8},{10,11... | collective-permute-start | bytes 786440 | tf_op jit(solution)/shard_map/ppermute | solution.py:316
  37.9 1.7 %collective-permute-done.17.refs_0_ = bf16[256,512]{1,0:T(8,128)(2,1)S(1)} collective-permute-done((bf16[256,512]{1,0:T(8,128)(2,1)S(1)}, bf16[256,512]{1,0:T(8,128)(2,1)S(1)}, u32[]{:S(2)}, u32[]{:S(2)}) %collective-permute-start.17) | collective-permute-done | bytes 262176 | tf_op jit(solution)/shard_map/ppermute | solution.py:317
  39.6 1.0 %shard_map.82.early = f32[256,512]{1,0:T(8,128)S(1)} custom-call(bf16[14,128,256]{2,1,0:T(8,128)(2,1)S(1)} %get-tuple-element.19.own, bf16[14,128,256]{2,1,0:T(8,128)(2,1)S(1)} %collective-permute-done.5.other, bf16[256,512]{1,0:T(8,128)(2,1)S(1)} %collective-permute-done.6.refs_0_, bf16[256,512]{1,0:T(8,128)(2,1)S(1)} %collective-permute-done.3.refs_1_, ...), custom_call_target="tpu_custom_call" | custom-call | flops 805306368 | bytes 4718592 | tf_op jit(solution)/shard_map/pallas_call | solution.py:243
  40.6 0.5 %collective-permute-done.18.refs_1_ = bf16[256,512]{1,0:T(8,128)(2,1)S(1)} collective-permute-done((bf16[256,512]{1,0:T(8,128)(2,1)S(1)}, bf16[256,512]{1,0:T(8,128)(2,1)S(1)}, u32[]{:S(2)}, u32[]{:S(2)}) %collective-permute-start.18) | collective-permute-done | bytes 262176 | tf_op jit(solution)/shard_map/ppermute | solution.py:318
  41.1 0.3 shard_map.83
  41.4 1.8 %collective-permute-start.19 = (bf16[128,512]{1,0:T(8,128)(2,1)S(1)}, bf16[128,512]{1,0:T(8,128)(2,1)S(1)}, u32[]{:S(2)}, u32[]{:S(2)}) collective-permute-start(bf16[128,512]{1,0:T(8,128)(2,1)S(1)} %get-tuple-element.23), channel_id=1, source_target_pairs={{0,16},{16,0},{1,17},{17,1},{2,18},{18,2},{3,19},{19,3},{4,20},{20... | collective-permute-start | bytes 393224 | tf_op jit(solution)/shard_map/ppermute | solution.py:323
  43.2 2.3 %shard_map.85 = (f32[512,512]{1,0:T(8,128)}, f32[512,512]{1,0:T(8,128)}) custom-call(bf16[256,512]{1,0:T(8,128)(2,1)S(1)} %shard_map.77.first.here_a, bf16[256,512]{1,0:T(8,128)(2,1)S(1)} %collective-permute-done.second.here_b, bf16[256,512]{1,0:T(8,128)(2,1)S(1)} %shard_map.78.first.there_a, bf16[256,512]{1,0:T(8,128)(2,1)S(1)} %collective-permute-done.1.second.there_b, ...), custom_call_target="tpu_custom_call" | custom-call | flops 7864320 | bytes 5242880 | tf_op jit(solution)/shard_map/pallas_call | solution.py:196
  45.5 0.3 shard_map.81.own_part
  45.8 1.2 %collective-permute-done.19.other_part = bf16[128,512]{1,0:T(8,128)(2,1)S(1)} collective-permute-done((bf16[128,512]{1,0:T(8,128)(2,1)S(1)}, bf16[128,512]{1,0:T(8,128)(2,1)S(1)}, u32[]{:S(2)}, u32[]{:S(2)}) %collective-permute-start.19) | collective-permute-done | bytes 131104 | tf_op jit(solution)/shard_map/ppermute | solution.py:323
  47.0 0.7 %shard_map.84 = bf16[128,512]{1,0:T(8,128)(2,1)} custom-call(f32[128,512]{1,0:T(8,128)S(1)} %shard_map.81.own_part, f32[128,512]{1,0:T(8,128)S(1)} %get-tuple-element.22.mine_part, bf16[128,512]{1,0:T(8,128)(2,1)S(1)} %collective-permute-done.19.other_part, f32[128,1]{1,0:T(8,128)S(1)} %get-tuple-element.24.inverse), custom_call_target="tpu_custom_call" | custom-call | tf_op jit(solution)/shard_map/pallas_call | solution.py:282
  (28 shorter events, 0.5 us)
Async XLA Ops:
  0.6 1.2 %copy-start.2 = (f32[1,512,512]{2,1,0:T(8,128)S(1)}, f32[1,512,512]{2,1,0:T(8,128)}, u32[]{:S(2)}) copy-start(f32[1,512,512]{2,1,0:T(8,128)} %param.9) | copy-start | bytes 3145732
  1.9 10.2 %copy-start = (f32[512,512]{1,0:T(8,128)S(1)}, f32[512,512]{1,0:T(8,128)}, u32[]{:S(2)}) copy-start(f32[512,512]{1,0:T(8,128)} %master.5) | copy-start | bytes 3145732
  1.9 10.2 %copy-start.1 = (f32[512,512]{1,0:T(8,128)S(1)}, f32[512,512]{1,0:T(8,128)}, u32[]{:S(2)}) copy-start(f32[512,512]{1,0:T(8,128)} %momentum.5) | copy-start | bytes 3145732
  1.9 10.2 %copy-start.4 = (f32[8192]{0:T(1024)S(1)}, f32[8192]{0:T(1024)}, u32[]{:S(2)}) copy-start(f32[8192]{0:T(1024)} %param.6) | copy-start | bytes 98308
  1.9 10.2 %collective-permute-start = (bf16[256,512]{1,0:T(8,128)(2,1)S(1)}, bf16[256,512]{1,0:T(8,128)(2,1)S(1)}, u32[]{:S(2)}, u32[]{:S(2)}) collective-permute-start(bf16[256,512]{1,0:T(8,128)(2,1)S(1)} %shard_map.78.first.there_a), channel_id=1, source_target_pairs={{0,16},{16,0},{1,17},{17,1},{2,18},{18,2},{3,19},{19,3},{4,20},{20... | collective-permute-start | bytes 786440 | tf_op jit(solution)/shard_map/ppermute | solution.py:300
  5.0 11.9 %collective-permute-start.1 = (bf16[256,512]{1,0:T(8,128)(2,1)S(1)}, bf16[256,512]{1,0:T(8,128)(2,1)S(1)}, u32[]{:S(2)}, u32[]{:S(2)}) collective-permute-start(bf16[256,512]{1,0:T(8,128)(2,1)S(1)} %shard_map.77.first.here_a), channel_id=1, source_target_pairs={{0,16},{16,0},{1,17},{17,1},{2,18},{18,2},{3,19},{19,3},{4,20},{20... | collective-permute-start | bytes 786440 | tf_op jit(solution)/shard_map/ppermute | solution.py:302
  5.2 1.6 %copy-start.3 = (bf16[128,8192]{1,0:T(8,128)(2,1)S(1)}, bf16[128,8192]{1,0:T(8,128)(2,1)}, u32[]{:S(2)}) copy-start(bf16[128,8192]{1,0:T(8,128)(2,1)} %tokens.1) | copy-start | bytes 6291460
  12.8 4.9 %collective-permute-start.2 = (bf16[256,512]{1,0:T(8,128)(2,1)S(1)}, bf16[256,512]{1,0:T(8,128)(2,1)S(1)}, u32[]{:S(2)}, u32[]{:S(2)}) collective-permute-start(bf16[256,512]{1,0:T(8,128)(2,1)S(1)} %shard_map.79.refs_0_), channel_id=1, source_target_pairs={{0,1},{1,0},{2,3},{3,2},{4,5},{5,4},{6,7},{7,6},{8,9},{9,8},{10,11... | collective-permute-start | bytes 786440 | tf_op jit(solution)/shard_map/ppermute | solution.py:309
  12.8 7.2 %collective-permute-start.6 = (bf16[256,512]{1,0:T(8,128)(2,1)S(1)}, bf16[256,512]{1,0:T(8,128)(2,1)S(1)}, u32[]{:S(2)}, u32[]{:S(2)}) collective-permute-start(bf16[256,512]{1,0:T(8,128)(2,1)S(1)} %shard_map.79.refs_0_), channel_id=1, source_target_pairs={{0,4},{1,3},{2,0},{3,7},{4,8},{5,1},{6,2},{7,11},{8,12},{9,5},{10,... | collective-permute-start | bytes 786440 | tf_op jit(solution)/shard_map/ppermute | solution.py:313
  15.0 22.3 %collective-permute-start.5 = (bf16[14,128,256]{2,1,0:T(8,128)(2,1)S(1)}, bf16[14,128,256]{2,1,0:T(8,128)(2,1)S(1)}, u32[]{:S(2)}, u32[]{:S(2)}) collective-permute-start(bf16[14,128,256]{2,1,0:T(8,128)(2,1)S(1)} %get-tuple-element.20), channel_id=1, source_target_pairs={{0,16},{16,0},{1,17},{17,1},{2,18},{18,2},{3,19},{19,3},{4,20},{20... | collective-permute-start | bytes 2752520 | tf_op jit(solution)/shard_map/ppermute | solution.py:310
  17.5 3.9 %collective-permute-start.4 = (bf16[256,512]{1,0:T(8,128)(2,1)S(1)}, bf16[256,512]{1,0:T(8,128)(2,1)S(1)}, u32[]{:S(2)}, u32[]{:S(2)}) collective-permute-start(bf16[256,512]{1,0:T(8,128)(2,1)S(1)} %shard_map.80.refs_1_), channel_id=1, source_target_pairs={{0,1},{1,0},{2,3},{3,2},{4,5},{5,4},{6,7},{7,6},{8,9},{9,8},{10,11... | collective-permute-start | bytes 786440 | tf_op jit(solution)/shard_map/ppermute | solution.py:308
  17.6 6.4 %collective-permute-start.3 = (bf16[256,512]{1,0:T(8,128)(2,1)S(1)}, bf16[256,512]{1,0:T(8,128)(2,1)S(1)}, u32[]{:S(2)}, u32[]{:S(2)}) collective-permute-start(bf16[256,512]{1,0:T(8,128)(2,1)S(1)} %collective-permute-done.2.refs_2_), channel_id=1, source_target_pairs={{0,4},{1,3},{2,0},{3,7},{4,8},{5,1},{6,2},{7,11},{8,12},{9,5},{10,... | collective-permute-start | bytes 786440 | tf_op jit(solution)/shard_map/ppermute | solution.py:313
  20.0 6.8 %collective-permute-start.9 = (bf16[256,512]{1,0:T(8,128)(2,1)S(1)}, bf16[256,512]{1,0:T(8,128)(2,1)S(1)}, u32[]{:S(2)}, u32[]{:S(2)}) collective-permute-start(bf16[256,512]{1,0:T(8,128)(2,1)S(1)} %collective-permute-done.6.refs_0_), channel_id=1, source_target_pairs={{0,4},{1,3},{2,0},{3,7},{4,8},{5,1},{6,2},{7,11},{8,12},{9,5},{10,... | collective-permute-start | bytes 786440 | tf_op jit(solution)/shard_map/ppermute | solution.py:313
  24.0 6.4 %collective-permute-start.10 = (bf16[256,512]{1,0:T(8,128)(2,1)S(1)}, bf16[256,512]{1,0:T(8,128)(2,1)S(1)}, u32[]{:S(2)}, u32[]{:S(2)}) collective-permute-start(bf16[256,512]{1,0:T(8,128)(2,1)S(1)} %collective-permute-done.3.refs_1_), channel_id=1, source_target_pairs={{0,4},{1,3},{2,0},{3,7},{4,8},{5,1},{6,2},{7,11},{8,12},{9,5},{10,... | collective-permute-start | bytes 786440 | tf_op jit(solution)/shard_map/ppermute | solution.py:313
  26.8 6.4 %collective-permute-start.13 = (bf16[256,512]{1,0:T(8,128)(2,1)S(1)}, bf16[256,512]{1,0:T(8,128)(2,1)S(1)}, u32[]{:S(2)}, u32[]{:S(2)}) collective-permute-start(bf16[256,512]{1,0:T(8,128)(2,1)S(1)} %collective-permute-done.9.refs_4_), channel_id=1, source_target_pairs={{0,4},{1,3},{2,0},{3,7},{4,8},{5,1},{6,2},{7,11},{8,12},{9,5},{10,... | collective-permute-start | bytes 786440 | tf_op jit(solution)/shard_map/ppermute | solution.py:313
  29.2 6.4 %collective-permute-start.7 = (bf16[256,512]{1,0:T(8,128)(2,1)S(1)}, bf16[256,512]{1,0:T(8,128)(2,1)S(1)}, u32[]{:S(2)}, u32[]{:S(2)}) collective-permute-start(bf16[256,512]{1,0:T(8,128)(2,1)S(1)} %collective-permute-done.6.refs_0_), channel_id=1, source_target_pairs={{0,1},{1,0},{2,3},{3,2},{4,5},{5,4},{6,7},{7,6},{8,9},{9,8},{10,11... | collective-permute-start | bytes 786440 | tf_op jit(solution)/shard_map/ppermute | solution.py:316
  29.2 8.1 %collective-permute-start.8 = (bf16[256,512]{1,0:T(8,128)(2,1)S(1)}, bf16[256,512]{1,0:T(8,128)(2,1)S(1)}, u32[]{:S(2)}, u32[]{:S(2)}) collective-permute-start(bf16[256,512]{1,0:T(8,128)(2,1)S(1)} %collective-permute-done.3.refs_1_), channel_id=1, source_target_pairs={{0,1},{1,0},{2,3},{3,2},{4,5},{5,4},{6,7},{7,6},{8,9},{9,8},{10,11... | collective-permute-start | bytes 786440 | tf_op jit(solution)/shard_map/ppermute | solution.py:316
  30.4 7.4 %collective-permute-start.14 = (bf16[256,512]{1,0:T(8,128)(2,1)S(1)}, bf16[256,512]{1,0:T(8,128)(2,1)S(1)}, u32[]{:S(2)}, u32[]{:S(2)}) collective-permute-start(bf16[256,512]{1,0:T(8,128)(2,1)S(1)} %collective-permute-done.10.refs_5_), channel_id=1, source_target_pairs={{0,4},{1,3},{2,0},{3,7},{4,8},{5,1},{6,2},{7,11},{8,12},{9,5},{10,... | collective-permute-start | bytes 786440 | tf_op jit(solution)/shard_map/ppermute | solution.py:313
  33.2 6.4 %collective-permute-start.17 = (bf16[256,512]{1,0:T(8,128)(2,1)S(1)}, bf16[256,512]{1,0:T(8,128)(2,1)S(1)}, u32[]{:S(2)}, u32[]{:S(2)}) collective-permute-start(bf16[256,512]{1,0:T(8,128)(2,1)S(1)} %collective-permute-done.13.refs_8_), channel_id=1, source_target_pairs={{0,4},{1,3},{2,0},{3,7},{4,8},{5,1},{6,2},{7,11},{8,12},{9,5},{10,... | collective-permute-start | bytes 786440 | tf_op jit(solution)/shard_map/ppermute | solution.py:317
  35.6 4.0 %collective-permute-start.11 = (bf16[256,512]{1,0:T(8,128)(2,1)S(1)}, bf16[256,512]{1,0:T(8,128)(2,1)S(1)}, u32[]{:S(2)}, u32[]{:S(2)}) collective-permute-start(bf16[256,512]{1,0:T(8,128)(2,1)S(1)} %collective-permute-done.9.refs_4_), channel_id=1, source_target_pairs={{0,1},{1,0},{2,3},{3,2},{4,5},{5,4},{6,7},{7,6},{8,9},{9,8},{10,11... | collective-permute-start | bytes 786440 | tf_op jit(solution)/shard_map/ppermute | solution.py:316
  37.3 2.3 %collective-permute-start.12 = (bf16[256,512]{1,0:T(8,128)(2,1)S(1)}, bf16[256,512]{1,0:T(8,128)(2,1)S(1)}, u32[]{:S(2)}, u32[]{:S(2)}) collective-permute-start(bf16[256,512]{1,0:T(8,128)(2,1)S(1)} %collective-permute-done.10.refs_5_), channel_id=1, source_target_pairs={{0,1},{1,0},{2,3},{3,2},{4,5},{5,4},{6,7},{7,6},{8,9},{9,8},{10,11... | collective-permute-start | bytes 786440 | tf_op jit(solution)/shard_map/ppermute | solution.py:316
  37.3 2.3 %collective-permute-start.15 = (bf16[256,512]{1,0:T(8,128)(2,1)S(1)}, bf16[256,512]{1,0:T(8,128)(2,1)S(1)}, u32[]{:S(2)}, u32[]{:S(2)}) collective-permute-start(bf16[256,512]{1,0:T(8,128)(2,1)S(1)} %collective-permute-done.13.refs_8_), channel_id=1, source_target_pairs={{0,1},{1,0},{2,3},{3,2},{4,5},{5,4},{6,7},{7,6},{8,9},{9,8},{10,11... | collective-permute-start | bytes 786440 | tf_op jit(solution)/shard_map/ppermute | solution.py:316
  37.9 1.8 %collective-permute-start.16 = (bf16[256,512]{1,0:T(8,128)(2,1)S(1)}, bf16[256,512]{1,0:T(8,128)(2,1)S(1)}, u32[]{:S(2)}, u32[]{:S(2)}) collective-permute-start(bf16[256,512]{1,0:T(8,128)(2,1)S(1)} %collective-permute-done.14.refs_9_), channel_id=1, source_target_pairs={{0,1},{1,0},{2,3},{3,2},{4,5},{5,4},{6,7},{7,6},{8,9},{9,8},{10,11... | collective-permute-start | bytes 786440 | tf_op jit(solution)/shard_map/ppermute | solution.py:316
  39.6 1.5 %collective-permute-start.18 = (bf16[256,512]{1,0:T(8,128)(2,1)S(1)}, bf16[256,512]{1,0:T(8,128)(2,1)S(1)}, u32[]{:S(2)}, u32[]{:S(2)}) collective-permute-start(bf16[256,512]{1,0:T(8,128)(2,1)S(1)} %collective-permute-done.17.refs_0_), channel_id=1, source_target_pairs={{0,1},{1,0},{2,3},{3,2},{4,5},{5,4},{6,7},{7,6},{8,9},{9,8},{10,11... | collective-permute-start | bytes 786440 | tf_op jit(solution)/shard_map/ppermute | solution.py:318
  41.4 5.6 %collective-permute-start.19 = (bf16[128,512]{1,0:T(8,128)(2,1)S(1)}, bf16[128,512]{1,0:T(8,128)(2,1)S(1)}, u32[]{:S(2)}, u32[]{:S(2)}) collective-permute-start(bf16[128,512]{1,0:T(8,128)(2,1)S(1)} %get-tuple-element.23), channel_id=1, source_target_pairs={{0,16},{16,0},{1,17},{17,1},{2,18},{18,2},{3,19},{19,3},{4,20},{20... | collective-permute-start | bytes 393224 | tf_op jit(solution)/shard_map/ppermute | solution.py:323

commit v3 on v2

--- a/solution.py
+++ b/solution.py
@@ -10,6 +10,7 @@
 BLOCK = 128
 CORES = 2
 RING_LIMIT = 16
+EARLY = 10
 
 outer_rate = 0.7
 outer_mu = 0.9
@@ -93,7 +94,12 @@
     return 1 - lax.axis_index("island")
 
 
-def token_kernel(chips, half, tokens, own, sent, whole, inverse):
+def tiles(shape, tall, wide):
+    rows, cols = shape
+    return [(slice(r, r + tall), slice(c, c + wide)) for r in range(0, rows, tall) for c in range(0, cols, wide)]
+
+
+def token_kernel(chips, half, early, tokens, grad, own, sent_early, sent_late, whole, inverse):
     rows, width = tokens.shape
     shared, kept = slots(chips)
 
@@ -103,7 +109,12 @@
 
     for k, slot in enumerate(shared):
         own[k] = columns(slot, mine())
-        sent[k] = columns(slot, others())
+        if k < early:
+            sent_early[k] = columns(slot, others())
+        else:
+            sent_late[k - early] = columns(slot, others())
+    for k, at in enumerate(tiles(grad.shape, rows, half)):
+        sent_early[early + k] = grad[at]
     for k, slot in enumerate(kept):
         whole[2 * k] = columns(slot, mine())
         whole[2 * k + 1] = columns(slot, others())
@@ -115,20 +126,36 @@
     inverse[...] = lax.rsqrt(mean + 1e-05) / jnp.sqrt(jnp.float32(width))
 
 
-def split_tokens(tokens, chips):
+def split_tokens(tokens, grad, chips, early):
     rows, width = tokens.shape
     half = width // (chips * CORES * 2)
     shared, kept = slots(chips)
-    split = jax.ShapeDtypeStruct((len(shared), rows, half), tokens.dtype)
-    whole = jax.ShapeDtypeStruct((2 * len(kept), rows, half), tokens.dtype)
-    return pl.pallas_call(
-        functools.partial(token_kernel, chips, half),
+    counts = len(shared), early + len(tiles(grad.shape, rows, half)), len(shared) - early, 2 * len(kept)
+    return pl.pallas_call(
+        functools.partial(token_kernel, chips, half, early),
+        in_specs=[VMEM] * 2,
+        out_specs=[VMEM] * 5,
+        out_shape=[jax.ShapeDtypeStruct((count, rows, half), tokens.dtype) for count in counts]
+        + [jax.ShapeDtypeStruct((rows, 1), jnp.float32)],
+        compiler_params=params(),
+        cost_estimate=pl.CostEstimate(flops=2 * rows * width, bytes_accessed=4 * rows * width, transcendentals=0),
+    )(tokens, grad)
+
+
+def unpack_kernel(first, packed, grad):
+    for k, at in enumerate(tiles(grad.shape, *packed.shape[1:])):
+        grad[at] = packed[first + k]
+
+
+def unpack(first, packed, shape):
+    return pl.pallas_call(
+        functools.partial(unpack_kernel, first),
         in_specs=[VMEM],
-        out_specs=[VMEM] * 4,
-        out_shape=[split, split, whole, jax.ShapeDtypeStruct((rows, 1), jnp.float32)],
-        compiler_params=params(),
-        cost_estimate=pl.CostEstimate(flops=2 * rows * width, bytes_accessed=4 * rows * width, transcendentals=0),
-    )(tokens)
+        out_specs=VMEM,
+        out_shape=jax.ShapeDtypeStruct(shape, packed.dtype),
+        compiler_params=params(),
+        cost_estimate=pl.CostEstimate(flops=0, bytes_accessed=4 * shape[0] * shape[1], transcendentals=0),
+    )(packed)
 
 
 def synced(a, b):
@@ -230,47 +257,51 @@
     )(whole, *blocks, *total)
 
 
-def early_kernel(own, other, *refs):
-    *blocks, total = refs
-    total[...] = jnp.zeros(total.shape, jnp.float32)
+def pair_of(own, others, k):
+    first, second = others
+    count = own.shape[0] - second.shape[0]
+    return jnp.concatenate([own[k], first[k] if k < count else second[k - count]], axis=0)
+
+
+def early_kernel(start, count, own, first, second, *refs):
+    blocks, total = refs[:count], refs[-1]
+    total[...] = refs[count][...] if len(refs) > count + 1 else jnp.zeros(total.shape, jnp.float32)
     for k, block in enumerate(blocks):
-        left = jnp.concatenate([own[k], other[k]], axis=0)
-        total[...] += jnp.dot(left, block[...], preferred_element_type=jnp.float32)
-
-
-def dot_early(own, other, blocks):
+        total[...] += jnp.dot(pair_of(own, (first, second), start + k), block[...], preferred_element_type=jnp.float32)
+
+
+def dot_early(start, own, others, blocks, *total):
     shape = (2 * own.shape[1], blocks[0].shape[1])
     return pl.pallas_call(
-        early_kernel,
-        in_specs=[VMEM] * (2 + len(blocks)),
+        functools.partial(early_kernel, start, len(blocks)),
+        in_specs=[VMEM] * (3 + len(blocks) + len(total)),
         out_specs=VMEM,
         out_shape=jax.ShapeDtypeStruct(shape, jnp.float32),
         compiler_params=params(),
         cost_estimate=cost_of(blocks, shape[0]),
-    )(own, other, *blocks)
-
-
-def late_kernel(first, own, other, early, *refs):
+    )(own, *others, *blocks, *total)
+
+
+def late_kernel(start, own, first, second, early, *refs):
     *blocks, mine_part, sent_part = refs
     rows = own.shape[1]
     total = early[...]
     for k, block in enumerate(blocks):
-        left = jnp.concatenate([own[first + k], other[first + k]], axis=0)
-        total += jnp.dot(left, block[...], preferred_element_type=jnp.float32)
+        total += jnp.dot(pair_of(own, (first, second), start + k), block[...], preferred_element_type=jnp.float32)
     mine_part[...] = total[:rows]
     sent_part[...] = total[rows:].astype(sent_part.dtype)
 
 
-def dot_late(first, own, other, early, blocks):
+def dot_late(start, own, others, early, blocks):
     shape = (own.shape[1], blocks[0].shape[1])
     return pl.pallas_call(
-        functools.partial(late_kernel, first),
-        in_specs=[VMEM] * (3 + len(blocks)),
+        functools.partial(late_kernel, start),
+        in_specs=[VMEM] * (4 + len(blocks)),
         out_specs=[VMEM] * 2,
         out_shape=[jax.ShapeDtypeStruct(shape, jnp.float32), jax.ShapeDtypeStruct(shape, jnp.bfloat16)],
         compiler_params=params(),
         cost_estimate=cost_of(blocks, 2 * shape[0]),
-    )(own, other, early, *blocks)
+    )(own, *others, early, *blocks)
 
 
 def close_kernel(own_part, mine_part, other_part, inverse, keys):
@@ -299,30 +330,34 @@
     grad_sent = cast_half(pseudo_grad[0], others)
     grad_here = cross(grad_sent)
     grad_own = cast_half(pseudo_grad[0], mine)
-    grad_there = cross(grad_own)
-    own, sent, whole, inverse = split_tokens(tokens, chips)
+    early = EARLY
+    own, sent_early, sent_late, whole, inverse = split_tokens(tokens, grad_own, chips, early)
     grad_here, own = tie((grad_here, own))
+    other_early, other_late = cross(sent_early), cross(sent_late)
 
     a = weight = sync_weight(mine, grad_own, grad_here, master, momentum, gain)
-    weight_over = sync_weight(others, grad_sent, grad_there, master, momentum, gain)
-    near_over = swap(weight_over)
     b = near = swap(weight)
-    other = cross(sent)
-    blocks = []
+    chains = []
     for step in range(1, chips // 2):
         a, b = ring(a), ring(b)
-        if step == 1:
-            b, near_over = tie((b, near_over))
-        blocks += [a, b, swap(a), swap(b)]
+        chains.append((a, b))
+    a, other_early = tie((a, other_early))
+    chains[-1] = (a, b)
+    grad_there = unpack(early, other_early, grad_own.shape)
+    weight_over = sync_weight(others, grad_sent, grad_there, master, momentum, gain)
+    last, weight_over = tie((b, weight_over))
+    blocks = []
+    for k, (a, b) in enumerate(chains):
+        blocks += [a, b, swap(a), swap(last if k == len(chains) - 1 else b)]
     a = ring(a)
     late = [a, swap(a)]
 
+    own_part = dot_own(0, whole, [weight, weight_over, near, swap(weight_over)])
     master_new, momentum_new = sync_outer(grad_own, grad_here, grad_sent, grad_there, master, momentum)
-    early = dot_early(own, other, blocks)
-    mine_part, sent_part = dot_late(len(blocks), own, other, early, late)
-    other_part = cross(sent_part)
-    own_part = dot_own(0, whole, [weight, weight_over, near, near_over])
-    keys = close(own_part, mine_part, other_part, inverse)
+    crossed = (other_early, other_late)
+    total = dot_early(0, own, crossed, blocks)
+    mine_part, sent_part = dot_late(len(blocks), own, crossed, total, late)
+    keys = close(own_part, mine_part, cross(sent_part), inverse)
     return (keys, master_new, momentum_new)
 
 
@@ -356,7 +391,8 @@
     shards = lax.axis_size("fsdp")
     rows = master.shape[0]
     ringed = shards % (2 * CORES) == 0 and 4 * CORES <= shards <= RING_LIMIT * CORES
-    if lax.axis_size("island") == 2 and ringed and rows % (2 * BLOCK) == 0:
+    tiled = tokens.shape[0] == BLOCK and rows % (2 * BLOCK) == 0 and 2 * master.shape[1] % rows == 0
+    if lax.axis_size("island") == 2 and ringed and tiled:
         return by_permutes(tokens, norm_gain, master, momentum, pseudo_grad)
     return by_gathers(tokens, norm_gain, master, momentum, pseudo_grad)
 

time: 48 us -> 47.3 us (0.985)
  local copies, waits for them, and re-layouts: 2.82 us -> 1.24 us
  waiting for transfers between devices: 14.3 us -> 15.5 us
    ppermute x6, waiting for transfers between devices: 4.12 us -> 6.2 us  [by_permutes(): a, b = (ring(a), ring(b))]
    unnamed x10, local copies, waits for them, and re-layouts: 2.82 us -> 1.24 us
    ppermute x10, starting transfers between devices: 4.6 us -> 6.09 us  [the longest x2 2.91 us: by_permutes(): other_early, other_late = (cross(sent_early), cross(sent_late))]
    ppermute x6, starting transfers between devices: 13.1 us -> 12.2 us  [by_permutes(): a, b = (ring(a), ring(b))]
    ppermute x1, starting transfers between devices: 2.38 us -> 1.58 us  [by_permutes(): a = ring(a)]
    ppermute x1, waiting for transfers between devices: 1.67 us -> 1.14 us  [by_permutes(): a = ring(a)]
    ppermute x1, waiting for transfers between devices: 0.52 us -> 0.01 us  [by_permutes(): late = [a, swap(a)]]
    pallas_call x3 -> x4, Pallas kernels: 1.95 us -> 1.98 us  [the longest x1 0.97 us: dot_early(): pl.pallas_call(functools.partial(early_kernel, start, len(blocks)), in_sp...]
  transfers between devices with their start and end apart: 20 -> 20, of which waited for: 10 -> 9; matrix products, arithmetic and copies ran while one was open for 0% -> 0% of each run, Pallas kernels for 12% -> 12%
where the time goes in v3:
time: 47.3 us; the launch traced here: 47.2 us
  starting transfers between devices  22.9 us (48%)
  waiting for transfers between devices  15.5 us (33%)
  Pallas kernels  6.7 us (14%)
  local copies, waits for them, and re-layouts  1.24 us (3%)
  between operations  0.77 us (2%)
    ppermute x6, starting transfers between devices, by_permutes(): a, b = (ring(a), ring(b))  12.2 us
    ppermute x6, waiting for transfers between devices, by_permutes(): a, b = (ring(a), ring(b))  6.2 us
    ppermute x1, waiting for transfers between devices, by_permutes(): grad_here = cross(grad_sent)  4.96 us
    ppermute x1, starting transfers between devices, by_permutes(): grad_here = cross(grad_sent)  3.03 us
    ppermute x2, starting transfers between devices, by_permutes(): other_early, other_late = (cross(sent_early), cross(sent_late))  2.91 us
    pallas_call x1, Pallas kernels, sync_outer(): pl.pallas_call(outer_kernel, in_specs=[VMEM] * 6, out_specs=[VMEM] * 2, o...  2.28 us
    ppermute x2, waiting for transfers between devices, by_permutes(): other_early, other_late = (cross(sent_early), cross(sent_late))  1.75 us
    ppermute x1, starting transfers between devices, by_permutes(): keys = close(own_part, mine_part, cross(sent_part), inverse)  1.59 us
  transfers between devices with their start and end apart: 20, of which 9 were waited for; matrix products, arithmetic and copies ran while one was open for 0% of the time, Pallas kernels for 12%

profile of v3, /device:TPU:0, one launch (start us, length us, event | category | flops | bytes accessed | tf_op | source)
XLA Modules:
  0.0 47.2 jit_solution(13596864899669377104)
XLA Ops:
  0.6 1.2 %copy-done.2 = f32[1,512,512]{2,1,0:T(8,128)S(1)} copy-done((f32[1,512,512]{2,1,0:T(8,128)S(1)}, f32[1,512,512]{2,1,0:T(8,128)}, u32[]{:S(2)}) %copy-start.2) | copy-done | bytes 1048600
  2.0 3.0 %collective-permute-start = (bf16[256,512]{1,0:T(8,128)(2,1)S(1)}, bf16[256,512]{1,0:T(8,128)(2,1)S(1)}, u32[]{:S(2)}, u32[]{:S(2)}) collective-permute-start(bf16[256,512]{1,0:T(8,128)(2,1)S(1)} %shard_map.78.first.there_a), channel_id=1, source_target_pairs={{0,16},{16,0},{1,17},{17,1},{2,18},{18,2},{3,19},{19,3},{4,20},{20... | collective-permute-start | bytes 786440 | tf_op jit(solution)/shard_map/ppermute | solution.py:331
  5.1 0.7 %shard_map.77 = (bf16[14,128,256]{2,1,0:T(8,128)(2,1)S(1)}, bf16[14,128,256]{2,1,0:T(8,128)(2,1)S(1)}, bf16[4,128,256]{2,1,0:T(8,128)(2,1)S(1)}, bf16[4,128,256]{2,1,0:T(8,128)(2,1)S(1)}, f32[128,1]{1,0:T(8,128)S(1)}) custom-call(bf16[128,8192]{1,0:T(8,128)(2,1)S(1)} %copy-done.3, bf16[256,512]{1,0:T(8,128)(2,1)S(1)} %shard_map.76.grad.first.here_a), custom_call_target="tpu_custom_call" | custom-call | flops 2097152 | bytes 4194304 | tf_op jit(solution)/shard_map/pallas_call | solution.py:134
  5.8 1.4 %collective-permute-start.8 = (bf16[14,128,256]{2,1,0:T(8,128)(2,1)S(1)}, bf16[14,128,256]{2,1,0:T(8,128)(2,1)S(1)}, u32[]{:S(2)}, u32[]{:S(2)}) collective-permute-start(bf16[14,128,256]{2,1,0:T(8,128)(2,1)S(1)} %get-tuple-element.21), channel_id=1, source_target_pairs={{0,16},{16,0},{1,17},{17,1},{2,18},{18,2},{3,19},{19,3},{4,20},{20... | collective-permute-start | bytes 2752520 | tf_op jit(solution)/shard_map/ppermute | solution.py:336
  7.2 5.0 %collective-permute-done.second.here_b = bf16[256,512]{1,0:T(8,128)(2,1)S(1)} collective-permute-done((bf16[256,512]{1,0:T(8,128)(2,1)S(1)}, bf16[256,512]{1,0:T(8,128)(2,1)S(1)}, u32[]{:S(2)}, u32[]{:S(2)}) %collective-permute-start) | collective-permute-done | bytes 262176 | tf_op jit(solution)/shard_map/ppermute | solution.py:331
  12.1 0.6 %shard_map.79.refs_0_ = bf16[256,512]{1,0:T(8,128)(2,1)S(1)} custom-call(bf16[256,512]{1,0:T(8,128)(2,1)S(1)} %shard_map.76.grad.first.here_a, bf16[256,512]{1,0:T(8,128)(2,1)S(1)} %collective-permute-done.second.here_b, f32[512,512]{1,0:T(8,128)S(1)} %copy-done, f32[512,512]{1,0:T(8,128)S(1)} %copy-done.1, f32[64,128]{1,0:T(8,128)S(1)} %bitcast.4), custom_call_target="tpu_custom_call" | custom-call | flops 3932160 | bytes 1835008 | tf_op jit(solution)/shard_map/pallas_call | solution.py:194
  12.9 2.2 %collective-permute-start.5 = (bf16[256,512]{1,0:T(8,128)(2,1)S(1)}, bf16[256,512]{1,0:T(8,128)(2,1)S(1)}, u32[]{:S(2)}, u32[]{:S(2)}) collective-permute-start(bf16[256,512]{1,0:T(8,128)(2,1)S(1)} %shard_map.79.refs_0_), channel_id=1, source_target_pairs={{0,4},{1,3},{2,0},{3,7},{4,8},{5,1},{6,2},{7,11},{8,12},{9,5},{10,... | collective-permute-start | bytes 786440 | tf_op jit(solution)/shard_map/ppermute | solution.py:342
  15.0 1.6 %collective-permute-start.2 = (bf16[256,512]{1,0:T(8,128)(2,1)S(1)}, bf16[256,512]{1,0:T(8,128)(2,1)S(1)}, u32[]{:S(2)}, u32[]{:S(2)}) collective-permute-start(bf16[256,512]{1,0:T(8,128)(2,1)S(1)} %collective-permute-done.1.refs_2_), channel_id=1, source_target_pairs={{0,4},{1,3},{2,0},{3,7},{4,8},{5,1},{6,2},{7,11},{8,12},{9,5},{10,... | collective-permute-start | bytes 786440 | tf_op jit(solution)/shard_map/ppermute | solution.py:342
  16.6 2.7 %collective-permute-done.5.refs_0_ = bf16[256,512]{1,0:T(8,128)(2,1)S(1)} collective-permute-done((bf16[256,512]{1,0:T(8,128)(2,1)S(1)}, bf16[256,512]{1,0:T(8,128)(2,1)S(1)}, u32[]{:S(2)}, u32[]{:S(2)}) %collective-permute-start.5) | collective-permute-done | bytes 262176 | tf_op jit(solution)/shard_map/ppermute | solution.py:342
  19.3 2.1 %collective-permute-start.6 = (bf16[256,512]{1,0:T(8,128)(2,1)S(1)}, bf16[256,512]{1,0:T(8,128)(2,1)S(1)}, u32[]{:S(2)}, u32[]{:S(2)}) collective-permute-start(bf16[256,512]{1,0:T(8,128)(2,1)S(1)} %collective-permute-done.5.refs_0_), channel_id=1, source_target_pairs={{0,4},{1,3},{2,0},{3,7},{4,8},{5,1},{6,2},{7,11},{8,12},{9,5},{10,... | collective-permute-start | bytes 786440 | tf_op jit(solution)/shard_map/ppermute | solution.py:342
  21.4 0.7 %collective-permute-done.2.refs_1_ = bf16[256,512]{1,0:T(8,128)(2,1)S(1)} collective-permute-done((bf16[256,512]{1,0:T(8,128)(2,1)S(1)}, bf16[256,512]{1,0:T(8,128)(2,1)S(1)}, u32[]{:S(2)}, u32[]{:S(2)}) %collective-permute-start.2) | collective-permute-done | bytes 262176 | tf_op jit(solution)/shard_map/ppermute | solution.py:342
  22.1 2.1 %collective-permute-start.3 = (bf16[256,512]{1,0:T(8,128)(2,1)S(1)}, bf16[256,512]{1,0:T(8,128)(2,1)S(1)}, u32[]{:S(2)}, u32[]{:S(2)}) collective-permute-start(bf16[256,512]{1,0:T(8,128)(2,1)S(1)} %collective-permute-done.2.refs_1_), channel_id=1, source_target_pairs={{0,4},{1,3},{2,0},{3,7},{4,8},{5,1},{6,2},{7,11},{8,12},{9,5},{10,... | collective-permute-start | bytes 786440 | tf_op jit(solution)/shard_map/ppermute | solution.py:342
  24.2 1.5 %collective-permute-done.6.refs_4_ = bf16[256,512]{1,0:T(8,128)(2,1)S(1)} collective-permute-done((bf16[256,512]{1,0:T(8,128)(2,1)S(1)}, bf16[256,512]{1,0:T(8,128)(2,1)S(1)}, u32[]{:S(2)}, u32[]{:S(2)}) %collective-permute-start.6) | collective-permute-done | bytes 262176 | tf_op jit(solution)/shard_map/ppermute | solution.py:342
  25.7 2.1 %collective-permute-start.7 = (bf16[256,512]{1,0:T(8,128)(2,1)S(1)}, bf16[256,512]{1,0:T(8,128)(2,1)S(1)}, u32[]{:S(2)}, u32[]{:S(2)}) collective-permute-start(bf16[256,512]{1,0:T(8,128)(2,1)S(1)} %collective-permute-done.6.refs_4_), channel_id=1, source_target_pairs={{0,4},{1,3},{2,0},{3,7},{4,8},{5,1},{6,2},{7,11},{8,12},{9,5},{10,... | collective-permute-start | bytes 786440 | tf_op jit(solution)/shard_map/ppermute | solution.py:342
  27.8 0.7 %collective-permute-done.3.refs_5_ = bf16[256,512]{1,0:T(8,128)(2,1)S(1)} collective-permute-done((bf16[256,512]{1,0:T(8,128)(2,1)S(1)}, bf16[256,512]{1,0:T(8,128)(2,1)S(1)}, u32[]{:S(2)}, u32[]{:S(2)}) %collective-permute-start.3) | collective-permute-done | bytes 262176 | tf_op jit(solution)/shard_map/ppermute | solution.py:342
  28.5 2.1 %collective-permute-start.4 = (bf16[256,512]{1,0:T(8,128)(2,1)S(1)}, bf16[256,512]{1,0:T(8,128)(2,1)S(1)}, u32[]{:S(2)}, u32[]{:S(2)}) collective-permute-start(bf16[256,512]{1,0:T(8,128)(2,1)S(1)} %collective-permute-done.3.refs_5_), channel_id=1, source_target_pairs={{0,4},{1,3},{2,0},{3,7},{4,8},{5,1},{6,2},{7,11},{8,12},{9,5},{10,... | collective-permute-start | bytes 786440 | tf_op jit(solution)/shard_map/ppermute | solution.py:342
  30.6 1.5 %collective-permute-start.10 = (bf16[4,128,256]{2,1,0:T(8,128)(2,1)S(1)}, bf16[4,128,256]{2,1,0:T(8,128)(2,1)S(1)}, u32[]{:S(2)}, u32[]{:S(2)}) collective-permute-start(bf16[4,128,256]{2,1,0:T(8,128)(2,1)S(1)} %get-tuple-element.25), channel_id=1, source_target_pairs={{0,16},{16,0},{1,17},{17,1},{2,18},{18,2},{3,19},{19,3},{4,20},{20... | collective-permute-start | bytes 786440 | tf_op jit(solution)/shard_map/ppermute | solution.py:336
  32.1 0.5 %collective-permute-start.12 = (bf16[256,512]{1,0:T(8,128)(2,1)S(1)}, bf16[256,512]{1,0:T(8,128)(2,1)S(1)}, u32[]{:S(2)}, u32[]{:S(2)}) collective-permute-start(bf16[256,512]{1,0:T(8,128)(2,1)S(1)} %collective-permute-done.2.refs_1_), channel_id=1, source_target_pairs={{0,1},{1,0},{2,3},{3,2},{4,5},{5,4},{6,7},{7,6},{8,9},{9,8},{10,11... | collective-permute-start | bytes 786440 | tf_op jit(solution)/shard_map/ppermute | solution.py:351
  32.6 1.6 %collective-permute-start.17 = (bf16[256,512]{1,0:T(8,128)(2,1)S(1)}, bf16[256,512]{1,0:T(8,128)(2,1)S(1)}, u32[]{:S(2)}, u32[]{:S(2)}) collective-permute-start(bf16[256,512]{1,0:T(8,128)(2,1)S(1)} %collective-permute-done.7.refs_8_), channel_id=1, source_target_pairs={{0,4},{1,3},{2,0},{3,7},{4,8},{5,1},{6,2},{7,11},{8,12},{9,5},{10,... | collective-permute-start | bytes 786440 | tf_op jit(solution)/shard_map/ppermute | solution.py:352
  34.2 0.7 %collective-permute-done.4.refs_9_ = bf16[256,512]{1,0:T(8,128)(2,1)S(1)} collective-permute-done((bf16[256,512]{1,0:T(8,128)(2,1)S(1)}, bf16[256,512]{1,0:T(8,128)(2,1)S(1)}, u32[]{:S(2)}, u32[]{:S(2)}) %collective-permute-start.4) | collective-permute-done | bytes 262176 | tf_op jit(solution)/shard_map/ppermute | solution.py:342
  34.9 0.6 %shard_map.81.refs_1_ = bf16[256,512]{1,0:T(8,128)(2,1)S(1)} custom-call(bf16[256,512]{1,0:T(8,128)(2,1)S(1)} %shard_map.78.first.there_a, bf16[256,512]{1,0:T(8,128)(2,1)S(1)} %shard_map.80.second.there_b, f32[512,512]{1,0:T(8,128)S(1)} %copy-done, f32[512,512]{1,0:T(8,128)S(1)} %copy-done.1, f32[64,128]{1,0:T(8,128)S(1)} %bitcast.5), custom_call_target="tpu_custom_call" | custom-call | flops 3932160 | bytes 1835008 | tf_op jit(solution)/shard_map/pallas_call | solution.py:194
  35.5 1.8 %collective-permute-done.10.second = bf16[4,128,256]{2,1,0:T(8,128)(2,1)S(1)} collective-permute-done((bf16[4,128,256]{2,1,0:T(8,128)(2,1)S(1)}, bf16[4,128,256]{2,1,0:T(8,128)(2,1)S(1)}, u32[]{:S(2)}, u32[]{:S(2)}) %collective-permute-start.10) | collective-permute-done | bytes 262176 | tf_op jit(solution)/shard_map/ppermute | solution.py:336
  37.3 0.5 %collective-permute-start.14 = (bf16[256,512]{1,0:T(8,128)(2,1)S(1)}, bf16[256,512]{1,0:T(8,128)(2,1)S(1)}, u32[]{:S(2)}, u32[]{:S(2)}) collective-permute-start(bf16[256,512]{1,0:T(8,128)(2,1)S(1)} %collective-permute-done.3.refs_5_), channel_id=1, source_target_pairs={{0,1},{1,0},{2,3},{3,2},{4,5},{5,4},{6,7},{7,6},{8,9},{9,8},{10,11... | collective-permute-start | bytes 786440 | tf_op jit(solution)/shard_map/ppermute | solution.py:351
  37.9 1.1 %collective-permute-done.17.refs_0_ = bf16[256,512]{1,0:T(8,128)(2,1)S(1)} collective-permute-done((bf16[256,512]{1,0:T(8,128)(2,1)S(1)}, bf16[256,512]{1,0:T(8,128)(2,1)S(1)}, u32[]{:S(2)}, u32[]{:S(2)}) %collective-permute-start.17) | collective-permute-done | bytes 262176 | tf_op jit(solution)/shard_map/ppermute | solution.py:352
  39.0 0.5 %collective-permute-start.9 = (bf16[256,512]{1,0:T(8,128)(2,1)S(1)}, bf16[256,512]{1,0:T(8,128)(2,1)S(1)}, u32[]{:S(2)}, u32[]{:S(2)}) collective-permute-start(bf16[256,512]{1,0:T(8,128)(2,1)S(1)} %shard_map.81.refs_1_), channel_id=1, source_target_pairs={{0,1},{1,0},{2,3},{3,2},{4,5},{5,4},{6,7},{7,6},{8,9},{9,8},{10,11... | collective-permute-start | bytes 786440 | tf_op jit(solution)/shard_map/ppermute | solution.py:355
  39.5 1.0 %shard_map.83.early = f32[256,512]{1,0:T(8,128)S(1)} custom-call(bf16[14,128,256]{2,1,0:T(8,128)(2,1)S(1)} %get-tuple-element.24.own, bf16[14,128,256]{2,1,0:T(8,128)(2,1)S(1)} %collective-permute-done.8.packed.first, bf16[4,128,256]{2,1,0:T(8,128)(2,1)S(1)} %collective-permute-done.10.second, bf16[256,512]{1,0:T(8,128)(2,1)S(1)} %collective-permute-done.5.refs_0_, ...), custom_call_target="tpu_custom_call" | custom-call | flops 805306368 | bytes 4718592 | tf_op jit(solution)/shard_map/pallas_call | solution.py:275
  40.5 0.3 shard_map.84
  40.8 1.6 %collective-permute-start.19 = (bf16[128,512]{1,0:T(8,128)(2,1)S(1)}, bf16[128,512]{1,0:T(8,128)(2,1)S(1)}, u32[]{:S(2)}, u32[]{:S(2)}) collective-permute-start(bf16[128,512]{1,0:T(8,128)(2,1)S(1)} %get-tuple-element.29), channel_id=1, source_target_pairs={{0,16},{16,0},{1,17},{17,1},{2,18},{18,2},{3,19},{19,3},{4,20},{20... | collective-permute-start | bytes 393224 | tf_op jit(solution)/shard_map/ppermute | solution.py:360
  42.4 2.3 %shard_map.86 = (f32[512,512]{1,0:T(8,128)}, f32[512,512]{1,0:T(8,128)}) custom-call(bf16[256,512]{1,0:T(8,128)(2,1)S(1)} %shard_map.76.grad.first.here_a, bf16[256,512]{1,0:T(8,128)(2,1)S(1)} %collective-permute-done.second.here_b, bf16[256,512]{1,0:T(8,128)(2,1)S(1)} %shard_map.78.first.there_a, bf16[256,512]{1,0:T(8,128)(2,1)S(1)} %shard_map.80.second.there_b, ...), custom_call_target="tpu_custom_call" | custom-call | flops 7864320 | bytes 5242880 | tf_op jit(solution)/shard_map/pallas_call | solution.py:223
  44.7 0.3 shard_map.82.own_part
  45.0 1.4 %collective-permute-done.19.other_part = bf16[128,512]{1,0:T(8,128)(2,1)S(1)} collective-permute-done((bf16[128,512]{1,0:T(8,128)(2,1)S(1)}, bf16[128,512]{1,0:T(8,128)(2,1)S(1)}, u32[]{:S(2)}, u32[]{:S(2)}) %collective-permute-start.19) | collective-permute-done | bytes 131104 | tf_op jit(solution)/shard_map/ppermute | solution.py:360
  46.4 0.7 %shard_map.85 = bf16[128,512]{1,0:T(8,128)(2,1)} custom-call(f32[128,512]{1,0:T(8,128)S(1)} %shard_map.82.own_part, f32[128,512]{1,0:T(8,128)S(1)} %get-tuple-element.28.mine_part, bf16[128,512]{1,0:T(8,128)(2,1)S(1)} %collective-permute-done.19.other_part, f32[128,1]{1,0:T(8,128)S(1)} %get-tuple-element.30.inverse), custom_call_target="tpu_custom_call" | custom-call | tf_op jit(solution)/shard_map/pallas_call | solution.py:313
  (29 shorter events, 0.4 us)
Async XLA Ops:
  0.6 1.2 %copy-start.2 = (f32[1,512,512]{2,1,0:T(8,128)S(1)}, f32[1,512,512]{2,1,0:T(8,128)}, u32[]{:S(2)}) copy-start(f32[1,512,512]{2,1,0:T(8,128)} %param.9) | copy-start | bytes 3145732
  1.9 3.2 %copy-start.3 = (bf16[128,8192]{1,0:T(8,128)(2,1)S(1)}, bf16[128,8192]{1,0:T(8,128)(2,1)}, u32[]{:S(2)}) copy-start(bf16[128,8192]{1,0:T(8,128)(2,1)} %tokens.1) | copy-start | bytes 6291460
  1.9 10.2 %copy-start = (f32[512,512]{1,0:T(8,128)S(1)}, f32[512,512]{1,0:T(8,128)}, u32[]{:S(2)}) copy-start(f32[512,512]{1,0:T(8,128)} %master.5) | copy-start | bytes 3145732
  1.9 10.2 %copy-start.1 = (f32[512,512]{1,0:T(8,128)S(1)}, f32[512,512]{1,0:T(8,128)}, u32[]{:S(2)}) copy-start(f32[512,512]{1,0:T(8,128)} %momentum.5) | copy-start | bytes 3145732
  2.0 10.2 %copy-start.4 = (f32[8192]{0:T(1024)S(1)}, f32[8192]{0:T(1024)}, u32[]{:S(2)}) copy-start(f32[8192]{0:T(1024)} %param.6) | copy-start | bytes 98308
  2.0 10.2 %collective-permute-start = (bf16[256,512]{1,0:T(8,128)(2,1)S(1)}, bf16[256,512]{1,0:T(8,128)(2,1)S(1)}, u32[]{:S(2)}, u32[]{:S(2)}) collective-permute-start(bf16[256,512]{1,0:T(8,128)(2,1)S(1)} %shard_map.78.first.there_a), channel_id=1, source_target_pairs={{0,16},{16,0},{1,17},{17,1},{2,18},{18,2},{3,19},{19,3},{4,20},{20... | collective-permute-start | bytes 786440 | tf_op jit(solution)/shard_map/ppermute | solution.py:331
  5.8 26.3 %collective-permute-start.8 = (bf16[14,128,256]{2,1,0:T(8,128)(2,1)S(1)}, bf16[14,128,256]{2,1,0:T(8,128)(2,1)S(1)}, u32[]{:S(2)}, u32[]{:S(2)}) collective-permute-start(bf16[14,128,256]{2,1,0:T(8,128)(2,1)S(1)} %get-tuple-element.21), channel_id=1, source_target_pairs={{0,16},{16,0},{1,17},{17,1},{2,18},{18,2},{3,19},{19,3},{4,20},{20... | collective-permute-start | bytes 2752520 | tf_op jit(solution)/shard_map/ppermute | solution.py:336
  12.8 2.2 %collective-permute-start.1 = (bf16[256,512]{1,0:T(8,128)(2,1)S(1)}, bf16[256,512]{1,0:T(8,128)(2,1)S(1)}, u32[]{:S(2)}, u32[]{:S(2)}) collective-permute-start(bf16[256,512]{1,0:T(8,128)(2,1)S(1)} %shard_map.79.refs_0_), channel_id=1, source_target_pairs={{0,1},{1,0},{2,3},{3,2},{4,5},{5,4},{6,7},{7,6},{8,9},{9,8},{10,11... | collective-permute-start | bytes 786440 | tf_op jit(solution)/shard_map/ppermute | solution.py:339
  12.9 6.4 %collective-permute-start.5 = (bf16[256,512]{1,0:T(8,128)(2,1)S(1)}, bf16[256,512]{1,0:T(8,128)(2,1)S(1)}, u32[]{:S(2)}, u32[]{:S(2)}) collective-permute-start(bf16[256,512]{1,0:T(8,128)(2,1)S(1)} %shard_map.79.refs_0_), channel_id=1, source_target_pairs={{0,4},{1,3},{2,0},{3,7},{4,8},{5,1},{6,2},{7,11},{8,12},{9,5},{10,... | collective-permute-start | bytes 786440 | tf_op jit(solution)/shard_map/ppermute | solution.py:342
  15.0 7.1 %collective-permute-start.2 = (bf16[256,512]{1,0:T(8,128)(2,1)S(1)}, bf16[256,512]{1,0:T(8,128)(2,1)S(1)}, u32[]{:S(2)}, u32[]{:S(2)}) collective-permute-start(bf16[256,512]{1,0:T(8,128)(2,1)S(1)} %collective-permute-done.1.refs_2_), channel_id=1, source_target_pairs={{0,4},{1,3},{2,0},{3,7},{4,8},{5,1},{6,2},{7,11},{8,12},{9,5},{10,... | collective-permute-start | bytes 786440 | tf_op jit(solution)/shard_map/ppermute | solution.py:342
  19.3 6.4 %collective-permute-start.6 = (bf16[256,512]{1,0:T(8,128)(2,1)S(1)}, bf16[256,512]{1,0:T(8,128)(2,1)S(1)}, u32[]{:S(2)}, u32[]{:S(2)}) collective-permute-start(bf16[256,512]{1,0:T(8,128)(2,1)S(1)} %collective-permute-done.5.refs_0_), channel_id=1, source_target_pairs={{0,4},{1,3},{2,0},{3,7},{4,8},{5,1},{6,2},{7,11},{8,12},{9,5},{10,... | collective-permute-start | bytes 786440 | tf_op jit(solution)/shard_map/ppermute | solution.py:342
  22.1 6.4 %collective-permute-start.3 = (bf16[256,512]{1,0:T(8,128)(2,1)S(1)}, bf16[256,512]{1,0:T(8,128)(2,1)S(1)}, u32[]{:S(2)}, u32[]{:S(2)}) collective-permute-start(bf16[256,512]{1,0:T(8,128)(2,1)S(1)} %collective-permute-done.2.refs_1_), channel_id=1, source_target_pairs={{0,4},{1,3},{2,0},{3,7},{4,8},{5,1},{6,2},{7,11},{8,12},{9,5},{10,... | collective-permute-start | bytes 786440 | tf_op jit(solution)/shard_map/ppermute | solution.py:342
  25.7 7.0 %collective-permute-start.7 = (bf16[256,512]{1,0:T(8,128)(2,1)S(1)}, bf16[256,512]{1,0:T(8,128)(2,1)S(1)}, u32[]{:S(2)}, u32[]{:S(2)}) collective-permute-start(bf16[256,512]{1,0:T(8,128)(2,1)S(1)} %collective-permute-done.6.refs_4_), channel_id=1, source_target_pairs={{0,4},{1,3},{2,0},{3,7},{4,8},{5,1},{6,2},{7,11},{8,12},{9,5},{10,... | collective-permute-start | bytes 786440 | tf_op jit(solution)/shard_map/ppermute | solution.py:342
  28.5 6.4 %collective-permute-start.4 = (bf16[256,512]{1,0:T(8,128)(2,1)S(1)}, bf16[256,512]{1,0:T(8,128)(2,1)S(1)}, u32[]{:S(2)}, u32[]{:S(2)}) collective-permute-start(bf16[256,512]{1,0:T(8,128)(2,1)S(1)} %collective-permute-done.3.refs_5_), channel_id=1, source_target_pairs={{0,4},{1,3},{2,0},{3,7},{4,8},{5,1},{6,2},{7,11},{8,12},{9,5},{10,... | collective-permute-start | bytes 786440 | tf_op jit(solution)/shard_map/ppermute | solution.py:342
  30.6 6.7 %collective-permute-start.10 = (bf16[4,128,256]{2,1,0:T(8,128)(2,1)S(1)}, bf16[4,128,256]{2,1,0:T(8,128)(2,1)S(1)}, u32[]{:S(2)}, u32[]{:S(2)}) collective-permute-start(bf16[4,128,256]{2,1,0:T(8,128)(2,1)S(1)} %get-tuple-element.25), channel_id=1, source_target_pairs={{0,16},{16,0},{1,17},{17,1},{2,18},{18,2},{3,19},{19,3},{4,20},{20... | collective-permute-start | bytes 786440 | tf_op jit(solution)/shard_map/ppermute | solution.py:336
  32.1 5.2 %collective-permute-start.11 = (bf16[256,512]{1,0:T(8,128)(2,1)S(1)}, bf16[256,512]{1,0:T(8,128)(2,1)S(1)}, u32[]{:S(2)}, u32[]{:S(2)}) collective-permute-start(bf16[256,512]{1,0:T(8,128)(2,1)S(1)} %collective-permute-done.5.refs_0_), channel_id=1, source_target_pairs={{0,1},{1,0},{2,3},{3,2},{4,5},{5,4},{6,7},{7,6},{8,9},{9,8},{10,11... | collective-permute-start | bytes 786440 | tf_op jit(solution)/shard_map/ppermute | solution.py:351
  32.1 5.7 %collective-permute-start.12 = (bf16[256,512]{1,0:T(8,128)(2,1)S(1)}, bf16[256,512]{1,0:T(8,128)(2,1)S(1)}, u32[]{:S(2)}, u32[]{:S(2)}) collective-permute-start(bf16[256,512]{1,0:T(8,128)(2,1)S(1)} %collective-permute-done.2.refs_1_), channel_id=1, source_target_pairs={{0,1},{1,0},{2,3},{3,2},{4,5},{5,4},{6,7},{7,6},{8,9},{9,8},{10,11... | collective-permute-start | bytes 786440 | tf_op jit(solution)/shard_map/ppermute | solution.py:351
  32.6 6.4 %collective-permute-start.17 = (bf16[256,512]{1,0:T(8,128)(2,1)S(1)}, bf16[256,512]{1,0:T(8,128)(2,1)S(1)}, u32[]{:S(2)}, u32[]{:S(2)}) collective-permute-start(bf16[256,512]{1,0:T(8,128)(2,1)S(1)} %collective-permute-done.7.refs_8_), channel_id=1, source_target_pairs={{0,4},{1,3},{2,0},{3,7},{4,8},{5,1},{6,2},{7,11},{8,12},{9,5},{10,... | collective-permute-start | bytes 786440 | tf_op jit(solution)/shard_map/ppermute | solution.py:352
  34.8 4.2 %collective-permute-start.13 = (bf16[256,512]{1,0:T(8,128)(2,1)S(1)}, bf16[256,512]{1,0:T(8,128)(2,1)S(1)}, u32[]{:S(2)}, u32[]{:S(2)}) collective-permute-start(bf16[256,512]{1,0:T(8,128)(2,1)S(1)} %collective-permute-done.6.refs_4_), channel_id=1, source_target_pairs={{0,1},{1,0},{2,3},{3,2},{4,5},{5,4},{6,7},{7,6},{8,9},{9,8},{10,11... | collective-permute-start | bytes 786440 | tf_op jit(solution)/shard_map/ppermute | solution.py:351
  37.3 2.2 %collective-permute-start.15 = (bf16[256,512]{1,0:T(8,128)(2,1)S(1)}, bf16[256,512]{1,0:T(8,128)(2,1)S(1)}, u32[]{:S(2)}, u32[]{:S(2)}) collective-permute-start(bf16[256,512]{1,0:T(8,128)(2,1)S(1)} %collective-permute-done.7.refs_8_), channel_id=1, source_target_pairs={{0,1},{1,0},{2,3},{3,2},{4,5},{5,4},{6,7},{7,6},{8,9},{9,8},{10,11... | collective-permute-start | bytes 786440 | tf_op jit(solution)/shard_map/ppermute | solution.py:351
  37.3 2.2 %collective-permute-start.14 = (bf16[256,512]{1,0:T(8,128)(2,1)S(1)}, bf16[256,512]{1,0:T(8,128)(2,1)S(1)}, u32[]{:S(2)}, u32[]{:S(2)}) collective-permute-start(bf16[256,512]{1,0:T(8,128)(2,1)S(1)} %collective-permute-done.3.refs_5_), channel_id=1, source_target_pairs={{0,1},{1,0},{2,3},{3,2},{4,5},{5,4},{6,7},{7,6},{8,9},{9,8},{10,11... | collective-permute-start | bytes 786440 | tf_op jit(solution)/shard_map/ppermute | solution.py:351
  37.8 1.8 %collective-permute-start.16 = (bf16[256,512]{1,0:T(8,128)(2,1)S(1)}, bf16[256,512]{1,0:T(8,128)(2,1)S(1)}, u32[]{:S(2)}, u32[]{:S(2)}) collective-permute-start(bf16[256,512]{1,0:T(8,128)(2,1)S(1)} %collective-permute-done.4.refs_9_), channel_id=1, source_target_pairs={{0,1},{1,0},{2,3},{3,2},{4,5},{5,4},{6,7},{7,6},{8,9},{9,8},{10,11... | collective-permute-start | bytes 786440 | tf_op jit(solution)/shard_map/ppermute | solution.py:351
  39.0 1.5 %collective-permute-start.18 = (bf16[256,512]{1,0:T(8,128)(2,1)S(1)}, bf16[256,512]{1,0:T(8,128)(2,1)S(1)}, u32[]{:S(2)}, u32[]{:S(2)}) collective-permute-start(bf16[256,512]{1,0:T(8,128)(2,1)S(1)} %collective-permute-done.17.refs_0_), channel_id=1, source_target_pairs={{0,1},{1,0},{2,3},{3,2},{4,5},{5,4},{6,7},{7,6},{8,9},{9,8},{10,11... | collective-permute-start | bytes 786440 | tf_op jit(solution)/shard_map/ppermute | solution.py:353
  39.0 5.7 %collective-permute-start.9 = (bf16[256,512]{1,0:T(8,128)(2,1)S(1)}, bf16[256,512]{1,0:T(8,128)(2,1)S(1)}, u32[]{:S(2)}, u32[]{:S(2)}) collective-permute-start(bf16[256,512]{1,0:T(8,128)(2,1)S(1)} %shard_map.81.refs_1_), channel_id=1, source_target_pairs={{0,1},{1,0},{2,3},{3,2},{4,5},{5,4},{6,7},{7,6},{8,9},{9,8},{10,11... | collective-permute-start | bytes 786440 | tf_op jit(solution)/shard_map/ppermute | solution.py:355
  40.8 5.6 %collective-permute-start.19 = (bf16[128,512]{1,0:T(8,128)(2,1)S(1)}, bf16[128,512]{1,0:T(8,128)(2,1)S(1)}, u32[]{:S(2)}, u32[]{:S(2)}) collective-permute-start(bf16[128,512]{1,0:T(8,128)(2,1)S(1)} %get-tuple-element.29), channel_id=1, source_target_pairs={{0,16},{16,0},{1,17},{17,1},{2,18},{18,2},{3,19},{19,3},{4,20},{20... | collective-permute-start | bytes 393224 | tf_op jit(solution)/shard_map/ppermute | solution.py:360

commit v4 on v3

--- a/solution.py
+++ b/solution.py
@@ -10,7 +10,6 @@
 BLOCK = 128
 CORES = 2
 RING_LIMIT = 16
-EARLY = 10
 
 outer_rate = 0.7
 outer_mu = 0.9
@@ -99,7 +98,7 @@
     return [(slice(r, r + tall), slice(c, c + wide)) for r in range(0, rows, tall) for c in range(0, cols, wide)]
 
 
-def token_kernel(chips, half, early, tokens, grad, own, sent_early, sent_late, whole, inverse):
+def token_kernel(chips, half, tokens, grad, own, sent, whole, inverse):
     rows, width = tokens.shape
     shared, kept = slots(chips)
 
@@ -109,12 +108,9 @@
 
     for k, slot in enumerate(shared):
         own[k] = columns(slot, mine())
-        if k < early:
-            sent_early[k] = columns(slot, others())
-        else:
-            sent_late[k - early] = columns(slot, others())
+        sent[k] = columns(slot, others())
     for k, at in enumerate(tiles(grad.shape, rows, half)):
-        sent_early[early + k] = grad[at]
+        sent[len(shared) + k] = grad[at]
     for k, slot in enumerate(kept):
         whole[2 * k] = columns(slot, mine())
         whole[2 * k + 1] = columns(slot, others())
@@ -126,15 +122,15 @@
     inverse[...] = lax.rsqrt(mean + 1e-05) / jnp.sqrt(jnp.float32(width))
 
 
-def split_tokens(tokens, grad, chips, early):
+def split_tokens(tokens, grad, chips):
     rows, width = tokens.shape
     half = width // (chips * CORES * 2)
     shared, kept = slots(chips)
-    counts = len(shared), early + len(tiles(grad.shape, rows, half)), len(shared) - early, 2 * len(kept)
-    return pl.pallas_call(
-        functools.partial(token_kernel, chips, half, early),
+    counts = len(shared), len(shared) + len(tiles(grad.shape, rows, half)), 2 * len(kept)
+    return pl.pallas_call(
+        functools.partial(token_kernel, chips, half),
         in_specs=[VMEM] * 2,
-        out_specs=[VMEM] * 5,
+        out_specs=[VMEM] * 4,
         out_shape=[jax.ShapeDtypeStruct((count, rows, half), tokens.dtype) for count in counts]
         + [jax.ShapeDtypeStruct((rows, 1), jnp.float32)],
         compiler_params=params(),
@@ -171,6 +167,63 @@
 
 def gains_of(gain, row):
     return jnp.transpose(jnp.broadcast_to(gain[pl.ds(row // BLOCK, 1), :], (BLOCK, BLOCK)))
+
+
+def ready_kernel(own, master, momentum, gain, peaks, base, steep):
+    half, cols = own.shape
+    first = lax.axis_index("fsdp") * (2 * half)
+    slope = -outer_rate * (1 + outer_mu)
+    for start in range(0, half, BLOCK):
+        rows = slice(start, start + BLOCK)
+        there = mine() * half + start
+        held = pl.ds(pl.multiple_of(there, BLOCK), BLOCK)
+        gains = gains_of(gain, first + there)
+        steep[rows, :] = gains * slope / 2
+        for k, col in enumerate(range(0, cols, BLOCK)):
+            at = slice(col, col + BLOCK)
+            a = jnp.abs(own[rows, at].astype(jnp.float32))
+            peaks[k, rows, :] = jnp.broadcast_to(jnp.max(a, axis=1, keepdims=True) / 2 + 1e-06, a.shape)
+            base[rows, at] = gains * (master[held, at] - outer_rate * outer_mu * (outer_mu * momentum[held, at]))
+
+
+def get_ready(own, master, momentum, gain):
+    half, cols = own.shape
+    shapes = (cols // BLOCK, half, BLOCK), (half, cols), (half, BLOCK)
+    return pl.pallas_call(
+        ready_kernel,
+        in_specs=[VMEM] * 4,
+        out_specs=[VMEM] * 3,
+        out_shape=[jax.ShapeDtypeStruct(shape, jnp.float32) for shape in shapes],
+        compiler_params=params(),
+        cost_estimate=pl.CostEstimate(flops=8 * half * cols, bytes_accessed=18 * half * cols, transcendentals=0),
+    )(own, master, momentum, gain)
+
+
+def first_kernel(own, here, peaks, base, steep, weight):
+    half, cols = own.shape
+    for start in range(0, half, BLOCK):
+        rows = slice(start, start + BLOCK)
+        for k, col in enumerate(range(0, cols, BLOCK)):
+            at = slice(col, col + BLOCK)
+            a = own[rows, at].astype(jnp.float32)
+            b = here[rows, at].astype(jnp.float32)
+            shared = peaks[k, rows, :] + jnp.max(jnp.abs(b), axis=1, keepdims=True) / 2
+            over = 1.0 / shared[:, :1]
+            low_a = jnp.clip(a * over, -1.0, 1.0).astype(jnp.bfloat16).astype(jnp.float32)
+            low_b = jnp.clip(b * over, -1.0, 1.0).astype(jnp.bfloat16).astype(jnp.float32)
+            weight[rows, at] = (base[rows, at] + steep[rows, :] * shared * (low_a + low_b)).astype(weight.dtype)
+
+
+def first_weight(own, here, ready):
+    half, cols = own.shape
+    return pl.pallas_call(
+        first_kernel,
+        in_specs=[VMEM] * 5,
+        out_specs=VMEM,
+        out_shape=jax.ShapeDtypeStruct((half, cols), jnp.bfloat16),
+        compiler_params=params(),
+        cost_estimate=pl.CostEstimate(flops=20 * half * cols, bytes_accessed=14 * half * cols, transcendentals=0),
+    )(own, here, *ready)
 
 
 def weight_kernel(which, first, second, master, momentum, gain, weight):
@@ -257,51 +310,47 @@
     )(whole, *blocks, *total)
 
 
-def pair_of(own, others, k):
-    first, second = others
-    count = own.shape[0] - second.shape[0]
-    return jnp.concatenate([own[k], first[k] if k < count else second[k - count]], axis=0)
-
-
-def early_kernel(start, count, own, first, second, *refs):
+def early_kernel(start, count, own, other, *refs):
     blocks, total = refs[:count], refs[-1]
     total[...] = refs[count][...] if len(refs) > count + 1 else jnp.zeros(total.shape, jnp.float32)
     for k, block in enumerate(blocks):
-        total[...] += jnp.dot(pair_of(own, (first, second), start + k), block[...], preferred_element_type=jnp.float32)
-
-
-def dot_early(start, own, others, blocks, *total):
+        left = jnp.concatenate([own[start + k], other[start + k]], axis=0)
+        total[...] += jnp.dot(left, block[...], preferred_element_type=jnp.float32)
+
+
+def dot_early(start, own, other, blocks, *total):
     shape = (2 * own.shape[1], blocks[0].shape[1])
     return pl.pallas_call(
         functools.partial(early_kernel, start, len(blocks)),
-        in_specs=[VMEM] * (3 + len(blocks) + len(total)),
+        in_specs=[VMEM] * (2 + len(blocks) + len(total)),
         out_specs=VMEM,
         out_shape=jax.ShapeDtypeStruct(shape, jnp.float32),
         compiler_params=params(),
         cost_estimate=cost_of(blocks, shape[0]),
-    )(own, *others, *blocks, *total)
-
-
-def late_kernel(start, own, first, second, early, *refs):
+    )(own, other, *blocks, *total)
+
+
+def late_kernel(start, own, other, early, *refs):
     *blocks, mine_part, sent_part = refs
     rows = own.shape[1]
     total = early[...]
     for k, block in enumerate(blocks):
-        total += jnp.dot(pair_of(own, (first, second), start + k), block[...], preferred_element_type=jnp.float32)
+        left = jnp.concatenate([own[start + k], other[start + k]], axis=0)
+        total += jnp.dot(left, block[...], preferred_element_type=jnp.float32)
     mine_part[...] = total[:rows]
     sent_part[...] = total[rows:].astype(sent_part.dtype)
 
 
-def dot_late(start, own, others, early, blocks):
+def dot_late(start, own, other, early, blocks):
     shape = (own.shape[1], blocks[0].shape[1])
     return pl.pallas_call(
         functools.partial(late_kernel, start),
-        in_specs=[VMEM] * (4 + len(blocks)),
+        in_specs=[VMEM] * (3 + len(blocks)),
         out_specs=[VMEM] * 2,
         out_shape=[jax.ShapeDtypeStruct(shape, jnp.float32), jax.ShapeDtypeStruct(shape, jnp.bfloat16)],
         compiler_params=params(),
         cost_estimate=cost_of(blocks, 2 * shape[0]),
-    )(own, *others, early, *blocks)
+    )(own, other, early, *blocks)
 
 
 def close_kernel(own_part, mine_part, other_part, inverse, keys):
@@ -327,36 +376,33 @@
     tie = lax.optimization_barrier
 
     gain = norm_gain.reshape(-1, BLOCK)
-    grad_sent = cast_half(pseudo_grad[0], others)
+    half = master.shape[0] // 2
+    grad_sent = lax.dynamic_slice_in_dim(pseudo_grad[0], others() * half, half).astype(jnp.bfloat16)
     grad_here = cross(grad_sent)
     grad_own = cast_half(pseudo_grad[0], mine)
-    early = EARLY
-    own, sent_early, sent_late, whole, inverse = split_tokens(tokens, grad_own, chips, early)
-    grad_here, own = tie((grad_here, own))
-    other_early, other_late = cross(sent_early), cross(sent_late)
-
-    a = weight = sync_weight(mine, grad_own, grad_here, master, momentum, gain)
+    own, sent, whole, inverse = split_tokens(tokens, grad_own, chips)
+    ready = get_ready(grad_own, master, momentum, gain)
+    grad_here, own, *ready = tie((grad_here, own, *ready))
+    other = cross(sent)
+
+    a = weight = first_weight(grad_own, grad_here, ready)
     b = near = swap(weight)
-    chains = []
+    blocks = []
     for step in range(1, chips // 2):
         a, b = ring(a), ring(b)
-        chains.append((a, b))
-    a, other_early = tie((a, other_early))
-    chains[-1] = (a, b)
-    grad_there = unpack(early, other_early, grad_own.shape)
+        blocks += [a, b, swap(a), swap(b)]
+    a = ring(a)
+    ahead = len(blocks) - 2 * CORES
+    total = dot_early(0, own, other, blocks[:ahead])
+    far, total = tie((a, total))
+    late = [a, swap(far)]
+
+    grad_there = unpack(len(slots(chips)[0]), other, grad_own.shape)
     weight_over = sync_weight(others, grad_sent, grad_there, master, momentum, gain)
-    last, weight_over = tie((b, weight_over))
-    blocks = []
-    for k, (a, b) in enumerate(chains):
-        blocks += [a, b, swap(a), swap(last if k == len(chains) - 1 else b)]
-    a = ring(a)
-    late = [a, swap(a)]
-
     own_part = dot_own(0, whole, [weight, weight_over, near, swap(weight_over)])
     master_new, momentum_new = sync_outer(grad_own, grad_here, grad_sent, grad_there, master, momentum)
-    crossed = (other_early, other_late)
-    total = dot_early(0, own, crossed, blocks)
-    mine_part, sent_part = dot_late(len(blocks), own, crossed, total, late)
+    total = dot_early(ahead, own, other, blocks[ahead:], total)
+    mine_part, sent_part = dot_late(len(blocks), own, other, total, late)
     keys = close(own_part, mine_part, cross(sent_part), inverse)
     return (keys, master_new, momentum_new)
 

time: 47.3 us -> 46.8 us (0.989)
  local copies, waits for them, and re-layouts: 1.24 us -> 4.65 us
  starting transfers between devices: 22.9 us -> 20 us
  waiting for transfers between devices: 15.5 us -> 14.2 us
    ppermute x9 -> x8, starting transfers between devices: 4 us -> 0.09 us  [the longest x1 0.07 us: by_permutes(): other = cross(sent)]
    ppermute x1, waiting for transfers between devices: 4.96 us -> 1.99 us  [by_permutes(): grad_here = cross(grad_sent)]
    unnamed x10, local copies, waits for them, and re-layouts: 1.24 us -> 3.57 us
    ppermute x6, waiting for transfers between devices: 6.2 us -> 8.22 us  [by_permutes(): a, b = (ring(a), ring(b))]
    convert_element_type x0 -> x1, local copies, waits for them, and re-layouts: none -> 1.08 us  [by_permutes(): lax.dynamic_slice_in_dim(pseudo_grad[0], others() * half, half)]
    ppermute x1, starting transfers between devices: 1.59 us -> 2.52 us  [by_permutes(): keys = close(own_part, mine_part, cross(sent_part), inverse)]
    pallas_call x1 -> x3, Pallas kernels: 0.7 us -> 1.47 us  [the longest x1 0.7 us: split_tokens(): pl.pallas_call(functools.partial(token_kernel, chips, half), in_specs=[VM...]
    pallas_call x2 -> x1, Pallas kernels: 1.26 us -> 0.63 us  [sync_weight(): pl.pallas_call(functools.partial(weight_kernel, which), in_specs=[VMEM] *...]
  transfers between devices with their start and end apart: 20 -> 19, of which waited for: 9 -> 10; matrix products, arithmetic and copies ran while one was open for 0% -> 0% of each run, Pallas kernels for 12% -> 13%
where the time goes in v4:
time: 46.8 us; the launch traced here: 46.5 us
  starting transfers between devices  20 us (43%)
  waiting for transfers between devices  14.2 us (30%)
  Pallas kernels  6.94 us (15%)
  local copies, waits for them, and re-layouts  4.65 us (10%)
  between operations  0.75 us (2%)
    ppermute x6, starting transfers between devices, by_permutes(): a, b = (ring(a), ring(b))  11.7 us
    ppermute x6, waiting for transfers between devices, by_permutes(): a, b = (ring(a), ring(b))  8.22 us
    unnamed x10, local copies, waits for them, and re-layouts  3.57 us
    ppermute x1, starting transfers between devices, by_permutes(): grad_here = cross(grad_sent)  3.03 us
    ppermute x1, starting transfers between devices, by_permutes(): keys = close(own_part, mine_part, cross(sent_part), inverse)  2.52 us
    ppermute x1, waiting for transfers between devices, by_permutes(): other = cross(sent)  2.32 us
    pallas_call x1, Pallas kernels, sync_outer(): pl.pallas_call(outer_kernel, in_specs=[VMEM] * 6, out_specs=[VMEM] * 2, o...  2.28 us
    ppermute x1, starting transfers between devices, by_permutes(): a = ring(a)  2.02 us
  transfers between devices with their start and end apart: 19, of which 10 were waited for; matrix products, arithmetic and copies ran while one was open for 0% of the time, Pallas kernels for 13%

profile of v4, /device:TPU:0, one launch (start us, length us, event | category | flops | bytes accessed | tf_op | source)
XLA Modules:
  0.0 46.5 jit_solution(7547964462226866428)
XLA Ops:
  0.6 1.1 %fusion.first.there_a = bf16[256,512]{1,0:T(8,128)(2,1)S(1)} fusion(f32[1,512,512]{2,1,0:T(8,128)} %param.9, s32[]{:T(128)S(6)} %select_n.3), kind=kLoop, calls=%fused_computation.1 | loop fusion | bytes 524292 | tf_op jit(solution)/shard_map/convert_element_type | solution.py:380
  1.7 3.0 %collective-permute-start = (bf16[256,512]{1,0:T(8,128)(2,1)S(1)}, bf16[256,512]{1,0:T(8,128)(2,1)S(1)}, u32[]{:S(2)}, u32[]{:S(2)}) collective-permute-start(bf16[256,512]{1,0:T(8,128)(2,1)S(1)} %fusion.first.there_a), channel_id=1, source_target_pairs={{0,16},{16,0},{1,17},{17,1},{2,18},{18,2},{3,19},{19,3},{4,20},{20... | collective-permute-start | bytes 786440 | tf_op jit(solution)/shard_map/ppermute | solution.py:381
  4.8 1.2 %copy-done.3 = f32[1,512,512]{2,1,0:T(8,128)S(1)} copy-done((f32[1,512,512]{2,1,0:T(8,128)S(1)}, f32[1,512,512]{2,1,0:T(8,128)}, u32[]{:S(2)}) %copy-start.3) | copy-done | bytes 1048600
  6.1 1.6 %copy-done.2 = bf16[128,8192]{1,0:T(8,128)(2,1)S(1)} copy-done((bf16[128,8192]{1,0:T(8,128)(2,1)S(1)}, bf16[128,8192]{1,0:T(8,128)(2,1)}, u32[]{:S(2)}) %copy-start.2) | copy-done | bytes 2097176
  7.6 0.7 %shard_map.77 = (bf16[14,128,256]{2,1,0:T(8,128)(2,1)S(1)}, bf16[18,128,256]{2,1,0:T(8,128)(2,1)S(1)}, bf16[4,128,256]{2,1,0:T(8,128)(2,1)S(1)}, f32[128,1]{1,0:T(8,128)S(1)}) custom-call(bf16[128,8192]{1,0:T(8,128)(2,1)S(1)} %copy-done.2, bf16[256,512]{1,0:T(8,128)(2,1)S(1)} %shard_map.76.grad.own.here_a), custom_call_target="tpu_custom_call" | custom-call | flops 2097152 | bytes 4194304 | tf_op jit(solution)/shard_map/pallas_call | solution.py:130
  8.4 0.4 copy-done
  8.9 0.3 copy-done.1
  9.5 2.0 %collective-permute-done.here.here_b = bf16[256,512]{1,0:T(8,128)(2,1)S(1)} collective-permute-done((bf16[256,512]{1,0:T(8,128)(2,1)S(1)}, bf16[256,512]{1,0:T(8,128)(2,1)S(1)}, u32[]{:S(2)}, u32[]{:S(2)}) %collective-permute-start) | collective-permute-done | bytes 262176 | tf_op jit(solution)/shard_map/ppermute | solution.py:381
  11.5 0.5 %shard_map.79.refs_0_ = bf16[256,512]{1,0:T(8,128)(2,1)S(1)} custom-call(bf16[256,512]{1,0:T(8,128)(2,1)S(1)} %shard_map.76.grad.own.here_a, bf16[256,512]{1,0:T(8,128)(2,1)S(1)} %collective-permute-done.here.here_b, f32[4,256,128]{2,1,0:T(8,128)S(1)} %get-tuple-element.27.peaks, f32[256,512]{1,0:T(8,128)S(1)} %get-tuple-element.28.base, ...), custom_call_target="tpu_custom_call" | custom-call | flops 2621440 | bytes 1835008 | tf_op jit(solution)/shard_map/pallas_call | solution.py:219
  12.0 2.1 %collective-permute-start.4 = (bf16[256,512]{1,0:T(8,128)(2,1)S(1)}, bf16[256,512]{1,0:T(8,128)(2,1)S(1)}, u32[]{:S(2)}, u32[]{:S(2)}) collective-permute-start(bf16[256,512]{1,0:T(8,128)(2,1)S(1)} %shard_map.79.refs_0_), channel_id=1, source_target_pairs={{0,4},{1,3},{2,0},{3,7},{4,8},{5,1},{6,2},{7,11},{8,12},{9,5},{10,... | collective-permute-start | bytes 786440 | tf_op jit(solution)/shard_map/ppermute | solution.py:392
  14.1 1.6 %collective-permute-start.7 = (bf16[256,512]{1,0:T(8,128)(2,1)S(1)}, bf16[256,512]{1,0:T(8,128)(2,1)S(1)}, u32[]{:S(2)}, u32[]{:S(2)}) collective-permute-start(bf16[256,512]{1,0:T(8,128)(2,1)S(1)} %collective-permute-done.2.refs_2_), channel_id=1, source_target_pairs={{0,4},{1,3},{2,0},{3,7},{4,8},{5,1},{6,2},{7,11},{8,12},{9,5},{10,... | collective-permute-start | bytes 786440 | tf_op jit(solution)/shard_map/ppermute | solution.py:392
  15.7 2.8 %collective-permute-done.4.refs_0_ = bf16[256,512]{1,0:T(8,128)(2,1)S(1)} collective-permute-done((bf16[256,512]{1,0:T(8,128)(2,1)S(1)}, bf16[256,512]{1,0:T(8,128)(2,1)S(1)}, u32[]{:S(2)}, u32[]{:S(2)}) %collective-permute-start.4) | collective-permute-done | bytes 262176 | tf_op jit(solution)/shard_map/ppermute | solution.py:392
  18.5 2.0 %collective-permute-start.5 = (bf16[256,512]{1,0:T(8,128)(2,1)S(1)}, bf16[256,512]{1,0:T(8,128)(2,1)S(1)}, u32[]{:S(2)}, u32[]{:S(2)}) collective-permute-start(bf16[256,512]{1,0:T(8,128)(2,1)S(1)} %collective-permute-done.4.refs_0_), channel_id=1, source_target_pairs={{0,4},{1,3},{2,0},{3,7},{4,8},{5,1},{6,2},{7,11},{8,12},{9,5},{10,... | collective-permute-start | bytes 786440 | tf_op jit(solution)/shard_map/ppermute | solution.py:392
  20.5 0.8 %collective-permute-done.7.refs_1_ = bf16[256,512]{1,0:T(8,128)(2,1)S(1)} collective-permute-done((bf16[256,512]{1,0:T(8,128)(2,1)S(1)}, bf16[256,512]{1,0:T(8,128)(2,1)S(1)}, u32[]{:S(2)}, u32[]{:S(2)}) %collective-permute-start.7) | collective-permute-done | bytes 262176 | tf_op jit(solution)/shard_map/ppermute | solution.py:392
  21.3 2.0 %collective-permute-start.8 = (bf16[256,512]{1,0:T(8,128)(2,1)S(1)}, bf16[256,512]{1,0:T(8,128)(2,1)S(1)}, u32[]{:S(2)}, u32[]{:S(2)}) collective-permute-start(bf16[256,512]{1,0:T(8,128)(2,1)S(1)} %collective-permute-done.7.refs_1_), channel_id=1, source_target_pairs={{0,4},{1,3},{2,0},{3,7},{4,8},{5,1},{6,2},{7,11},{8,12},{9,5},{10,... | collective-permute-start | bytes 786440 | tf_op jit(solution)/shard_map/ppermute | solution.py:392
  23.3 1.5 %collective-permute-done.5.refs_4_ = bf16[256,512]{1,0:T(8,128)(2,1)S(1)} collective-permute-done((bf16[256,512]{1,0:T(8,128)(2,1)S(1)}, bf16[256,512]{1,0:T(8,128)(2,1)S(1)}, u32[]{:S(2)}, u32[]{:S(2)}) %collective-permute-start.5) | collective-permute-done | bytes 262176 | tf_op jit(solution)/shard_map/ppermute | solution.py:392
  24.8 2.0 %collective-permute-start.6 = (bf16[256,512]{1,0:T(8,128)(2,1)S(1)}, bf16[256,512]{1,0:T(8,128)(2,1)S(1)}, u32[]{:S(2)}, u32[]{:S(2)}) collective-permute-start(bf16[256,512]{1,0:T(8,128)(2,1)S(1)} %collective-permute-done.5.refs_4_), channel_id=1, source_target_pairs={{0,4},{1,3},{2,0},{3,7},{4,8},{5,1},{6,2},{7,11},{8,12},{9,5},{10,... | collective-permute-start | bytes 786440 | tf_op jit(solution)/shard_map/ppermute | solution.py:392
  26.9 0.8 %collective-permute-done.8.refs_5_ = bf16[256,512]{1,0:T(8,128)(2,1)S(1)} collective-permute-done((bf16[256,512]{1,0:T(8,128)(2,1)S(1)}, bf16[256,512]{1,0:T(8,128)(2,1)S(1)}, u32[]{:S(2)}, u32[]{:S(2)}) %collective-permute-start.8) | collective-permute-done | bytes 262176 | tf_op jit(solution)/shard_map/ppermute | solution.py:392
  27.6 2.0 %collective-permute-start.9 = (bf16[256,512]{1,0:T(8,128)(2,1)S(1)}, bf16[256,512]{1,0:T(8,128)(2,1)S(1)}, u32[]{:S(2)}, u32[]{:S(2)}) collective-permute-start(bf16[256,512]{1,0:T(8,128)(2,1)S(1)} %collective-permute-done.8.refs_5_), channel_id=1, source_target_pairs={{0,4},{1,3},{2,0},{3,7},{4,8},{5,1},{6,2},{7,11},{8,12},{9,5},{10,... | collective-permute-start | bytes 786440 | tf_op jit(solution)/shard_map/ppermute | solution.py:392
  29.7 1.5 %collective-permute-done.6.refs_0_ = bf16[256,512]{1,0:T(8,128)(2,1)S(1)} collective-permute-done((bf16[256,512]{1,0:T(8,128)(2,1)S(1)}, bf16[256,512]{1,0:T(8,128)(2,1)S(1)}, u32[]{:S(2)}, u32[]{:S(2)}) %collective-permute-start.6) | collective-permute-done | bytes 262176 | tf_op jit(solution)/shard_map/ppermute | solution.py:392
  31.2 2.0 %collective-permute-start.12 = (bf16[256,512]{1,0:T(8,128)(2,1)S(1)}, bf16[256,512]{1,0:T(8,128)(2,1)S(1)}, u32[]{:S(2)}, u32[]{:S(2)}) collective-permute-start(bf16[256,512]{1,0:T(8,128)(2,1)S(1)} %collective-permute-done.6.refs_0_), channel_id=1, source_target_pairs={{0,4},{1,3},{2,0},{3,7},{4,8},{5,1},{6,2},{7,11},{8,12},{9,5},{10,... | collective-permute-start | bytes 786440 | tf_op jit(solution)/shard_map/ppermute | solution.py:394
  33.2 0.8 %collective-permute-done.9.refs_1_ = bf16[256,512]{1,0:T(8,128)(2,1)S(1)} collective-permute-done((bf16[256,512]{1,0:T(8,128)(2,1)S(1)}, bf16[256,512]{1,0:T(8,128)(2,1)S(1)}, u32[]{:S(2)}, u32[]{:S(2)}) %collective-permute-start.9) | collective-permute-done | bytes 262176 | tf_op jit(solution)/shard_map/ppermute | solution.py:392
  34.0 2.3 %collective-permute-done.1.packed.other = bf16[18,128,256]{2,1,0:T(8,128)(2,1)S(1)} collective-permute-done((bf16[18,128,256]{2,1,0:T(8,128)(2,1)S(1)}, bf16[18,128,256]{2,1,0:T(8,128)(2,1)S(1)}, u32[]{:S(2)}, u32[]{:S(2)}) %collective-permute-start.1) | collective-permute-done | bytes 1179680 | tf_op jit(solution)/shard_map/ppermute | solution.py:386
  36.3 0.7 %shard_map.83.refs_4_ = f32[256,512]{1,0:T(8,128)S(1)} custom-call(bf16[14,128,256]{2,1,0:T(8,128)(2,1)S(1)} %get-tuple-element.31.own, bf16[18,128,256]{2,1,0:T(8,128)(2,1)S(1)} %collective-permute-done.1.packed.other, bf16[256,512]{1,0:T(8,128)(2,1)S(1)} %collective-permute-done.4.refs_0_, bf16[256,512]{1,0:T(8,128)(2,1)S(1)} %collective-permute-done.7.refs_1_, ...), custom_call_target="tpu_custom_call" | custom-call | flops 536870912 | bytes 3145728 | tf_op jit(solution)/shard_map/pallas_call | solution.py:323
  37.0 0.5 %collective-permute-done.12.refs_0_ = bf16[256,512]{1,0:T(8,128)(2,1)S(1)} collective-permute-done((bf16[256,512]{1,0:T(8,128)(2,1)S(1)}, bf16[256,512]{1,0:T(8,128)(2,1)S(1)}, u32[]{:S(2)}, u32[]{:S(2)}) %collective-permute-start.12) | collective-permute-done | bytes 262176 | tf_op jit(solution)/shard_map/ppermute | solution.py:394
  37.6 0.6 %shard_map.81.refs_1_ = bf16[256,512]{1,0:T(8,128)(2,1)S(1)} custom-call(bf16[256,512]{1,0:T(8,128)(2,1)S(1)} %fusion.first.there_a, bf16[256,512]{1,0:T(8,128)(2,1)S(1)} %shard_map.80.second.there_b, f32[512,512]{1,0:T(8,128)S(1)} %copy-done, f32[512,512]{1,0:T(8,128)S(1)} %copy-done.1, f32[64,128]{1,0:T(8,128)S(1)} %bitcast.6), custom_call_target="tpu_custom_call" | custom-call | flops 3932160 | bytes 1835008 | tf_op jit(solution)/shard_map/pallas_call | solution.py:247
  38.2 0.6 %collective-permute-start.3 = (bf16[256,512]{1,0:T(8,128)(2,1)S(1)}, bf16[256,512]{1,0:T(8,128)(2,1)S(1)}, u32[]{:S(2)}, u32[]{:S(2)}) collective-permute-start(bf16[256,512]{1,0:T(8,128)(2,1)S(1)} %shard_map.81.refs_1_), channel_id=1, source_target_pairs={{0,1},{1,0},{2,3},{3,2},{4,5},{5,4},{6,7},{7,6},{8,9},{9,8},{10,11... | collective-permute-start | bytes 786440 | tf_op jit(solution)/shard_map/ppermute | solution.py:402
  38.8 0.4 shard_map.84.early
  39.6 2.5 %collective-permute-start.18 = (bf16[128,512]{1,0:T(8,128)(2,1)S(1)}, bf16[128,512]{1,0:T(8,128)(2,1)S(1)}, u32[]{:S(2)}, u32[]{:S(2)}) collective-permute-start(bf16[128,512]{1,0:T(8,128)(2,1)S(1)} %get-tuple-element.35), channel_id=1, source_target_pairs={{0,16},{16,0},{1,17},{17,1},{2,18},{18,2},{3,19},{19,3},{4,20},{20... | collective-permute-start | bytes 393224 | tf_op jit(solution)/shard_map/ppermute | solution.py:406
  42.1 2.3 %shard_map.87 = (f32[512,512]{1,0:T(8,128)}, f32[512,512]{1,0:T(8,128)}) custom-call(bf16[256,512]{1,0:T(8,128)(2,1)S(1)} %shard_map.76.grad.own.here_a, bf16[256,512]{1,0:T(8,128)(2,1)S(1)} %collective-permute-done.here.here_b, bf16[256,512]{1,0:T(8,128)(2,1)S(1)} %fusion.first.there_a, bf16[256,512]{1,0:T(8,128)(2,1)S(1)} %shard_map.80.second.there_b, ...), custom_call_target="tpu_custom_call" | custom-call | flops 7864320 | bytes 5242880 | tf_op jit(solution)/shard_map/pallas_call | solution.py:276
  44.7 1.1 %collective-permute-done.18.other_part = bf16[128,512]{1,0:T(8,128)(2,1)S(1)} collective-permute-done((bf16[128,512]{1,0:T(8,128)(2,1)S(1)}, bf16[128,512]{1,0:T(8,128)(2,1)S(1)}, u32[]{:S(2)}, u32[]{:S(2)}) %collective-permute-start.18) | collective-permute-done | bytes 131104 | tf_op jit(solution)/shard_map/ppermute | solution.py:406
  45.8 0.7 %shard_map.86 = bf16[128,512]{1,0:T(8,128)(2,1)} custom-call(f32[128,512]{1,0:T(8,128)S(1)} %shard_map.82.own_part, f32[128,512]{1,0:T(8,128)S(1)} %get-tuple-element.34.mine_part, bf16[128,512]{1,0:T(8,128)(2,1)S(1)} %collective-permute-done.18.other_part, f32[128,1]{1,0:T(8,128)S(1)} %get-tuple-element.36.inverse), custom_call_target="tpu_custom_call" | custom-call | tf_op jit(solution)/shard_map/pallas_call | solution.py:362
  (29 shorter events, 1.2 us)
Async XLA Ops:
  1.7 9.8 %collective-permute-start = (bf16[256,512]{1,0:T(8,128)(2,1)S(1)}, bf16[256,512]{1,0:T(8,128)(2,1)S(1)}, u32[]{:S(2)}, u32[]{:S(2)}) collective-permute-start(bf16[256,512]{1,0:T(8,128)(2,1)S(1)} %fusion.first.there_a), channel_id=1, source_target_pairs={{0,16},{16,0},{1,17},{17,1},{2,18},{18,2},{3,19},{19,3},{4,20},{20... | collective-permute-start | bytes 786440 | tf_op jit(solution)/shard_map/ppermute | solution.py:381
  4.7 1.2 %copy-start.3 = (f32[1,512,512]{2,1,0:T(8,128)S(1)}, f32[1,512,512]{2,1,0:T(8,128)}, u32[]{:S(2)}) copy-start(f32[1,512,512]{2,1,0:T(8,128)} %param.9) | copy-start | bytes 3145732
  6.0 1.6 %copy-start.2 = (bf16[128,8192]{1,0:T(8,128)(2,1)S(1)}, bf16[128,8192]{1,0:T(8,128)(2,1)}, u32[]{:S(2)}) copy-start(bf16[128,8192]{1,0:T(8,128)(2,1)} %tokens.1) | copy-start | bytes 6291460
  7.6 1.2 %copy-start = (f32[512,512]{1,0:T(8,128)S(1)}, f32[512,512]{1,0:T(8,128)}, u32[]{:S(2)}) copy-start(f32[512,512]{1,0:T(8,128)} %master.5) | copy-start | bytes 3145732
  7.6 1.5 %copy-start.1 = (f32[512,512]{1,0:T(8,128)S(1)}, f32[512,512]{1,0:T(8,128)}, u32[]{:S(2)}) copy-start(f32[512,512]{1,0:T(8,128)} %momentum.5) | copy-start | bytes 3145732
  7.6 1.5 %copy-start.4 = (f32[8192]{0:T(1024)S(1)}, f32[8192]{0:T(1024)}, u32[]{:S(2)}) copy-start(f32[8192]{0:T(1024)} %param.6) | copy-start | bytes 98308
  8.3 28.0 %collective-permute-start.1 = (bf16[18,128,256]{2,1,0:T(8,128)(2,1)S(1)}, bf16[18,128,256]{2,1,0:T(8,128)(2,1)S(1)}, u32[]{:S(2)}, u32[]{:S(2)}) collective-permute-start(bf16[18,128,256]{2,1,0:T(8,128)(2,1)S(1)} %get-tuple-element.30), channel_id=1, source_target_pairs={{0,16},{16,0},{1,17},{17,1},{2,18},{18,2},{3,19},{19,3},{4,20},{20... | collective-permute-start | bytes 3538952 | tf_op jit(solution)/shard_map/ppermute | solution.py:386
  12.0 2.2 %collective-permute-start.2 = (bf16[256,512]{1,0:T(8,128)(2,1)S(1)}, bf16[256,512]{1,0:T(8,128)(2,1)S(1)}, u32[]{:S(2)}, u32[]{:S(2)}) collective-permute-start(bf16[256,512]{1,0:T(8,128)(2,1)S(1)} %shard_map.79.refs_0_), channel_id=1, source_target_pairs={{0,1},{1,0},{2,3},{3,2},{4,5},{5,4},{6,7},{7,6},{8,9},{9,8},{10,11... | collective-permute-start | bytes 786440 | tf_op jit(solution)/shard_map/ppermute | solution.py:389
  12.0 6.4 %collective-permute-start.4 = (bf16[256,512]{1,0:T(8,128)(2,1)S(1)}, bf16[256,512]{1,0:T(8,128)(2,1)S(1)}, u32[]{:S(2)}, u32[]{:S(2)}) collective-permute-start(bf16[256,512]{1,0:T(8,128)(2,1)S(1)} %shard_map.79.refs_0_), channel_id=1, source_target_pairs={{0,4},{1,3},{2,0},{3,7},{4,8},{5,1},{6,2},{7,11},{8,12},{9,5},{10,... | collective-permute-start | bytes 786440 | tf_op jit(solution)/shard_map/ppermute | solution.py:392
  14.1 7.2 %collective-permute-start.7 = (bf16[256,512]{1,0:T(8,128)(2,1)S(1)}, bf16[256,512]{1,0:T(8,128)(2,1)S(1)}, u32[]{:S(2)}, u32[]{:S(2)}) collective-permute-start(bf16[256,512]{1,0:T(8,128)(2,1)S(1)} %collective-permute-done.2.refs_2_), channel_id=1, source_target_pairs={{0,4},{1,3},{2,0},{3,7},{4,8},{5,1},{6,2},{7,11},{8,12},{9,5},{10,... | collective-permute-start | bytes 786440 | tf_op jit(solution)/shard_map/ppermute | solution.py:392
  18.5 6.4 %collective-permute-start.5 = (bf16[256,512]{1,0:T(8,128)(2,1)S(1)}, bf16[256,512]{1,0:T(8,128)(2,1)S(1)}, u32[]{:S(2)}, u32[]{:S(2)}) collective-permute-start(bf16[256,512]{1,0:T(8,128)(2,1)S(1)} %collective-permute-done.4.refs_0_), channel_id=1, source_target_pairs={{0,4},{1,3},{2,0},{3,7},{4,8},{5,1},{6,2},{7,11},{8,12},{9,5},{10,... | collective-permute-start | bytes 786440 | tf_op jit(solution)/shard_map/ppermute | solution.py:392
  20.5 6.4 %collective-permute-start.13 = (bf16[256,512]{1,0:T(8,128)(2,1)S(1)}, bf16[256,512]{1,0:T(8,128)(2,1)S(1)}, u32[]{:S(2)}, u32[]{:S(2)}) collective-permute-start(bf16[256,512]{1,0:T(8,128)(2,1)S(1)} %collective-permute-done.4.refs_0_), channel_id=1, source_target_pairs={{0,1},{1,0},{2,3},{3,2},{4,5},{5,4},{6,7},{7,6},{8,9},{9,8},{10,11... | collective-permute-start | bytes 786440 | tf_op jit(solution)/shard_map/ppermute | solution.py:393
  21.3 6.4 %collective-permute-start.8 = (bf16[256,512]{1,0:T(8,128)(2,1)S(1)}, bf16[256,512]{1,0:T(8,128)(2,1)S(1)}, u32[]{:S(2)}, u32[]{:S(2)}) collective-permute-start(bf16[256,512]{1,0:T(8,128)(2,1)S(1)} %collective-permute-done.7.refs_1_), channel_id=1, source_target_pairs={{0,4},{1,3},{2,0},{3,7},{4,8},{5,1},{6,2},{7,11},{8,12},{9,5},{10,... | collective-permute-start | bytes 786440 | tf_op jit(solution)/shard_map/ppermute | solution.py:392
  23.3 6.4 %collective-permute-start.14 = (bf16[256,512]{1,0:T(8,128)(2,1)S(1)}, bf16[256,512]{1,0:T(8,128)(2,1)S(1)}, u32[]{:S(2)}, u32[]{:S(2)}) collective-permute-start(bf16[256,512]{1,0:T(8,128)(2,1)S(1)} %collective-permute-done.7.refs_1_), channel_id=1, source_target_pairs={{0,1},{1,0},{2,3},{3,2},{4,5},{5,4},{6,7},{7,6},{8,9},{9,8},{10,11... | collective-permute-start | bytes 786440 | tf_op jit(solution)/shard_map/ppermute | solution.py:393
  24.8 6.4 %collective-permute-start.6 = (bf16[256,512]{1,0:T(8,128)(2,1)S(1)}, bf16[256,512]{1,0:T(8,128)(2,1)S(1)}, u32[]{:S(2)}, u32[]{:S(2)}) collective-permute-start(bf16[256,512]{1,0:T(8,128)(2,1)S(1)} %collective-permute-done.5.refs_4_), channel_id=1, source_target_pairs={{0,4},{1,3},{2,0},{3,7},{4,8},{5,1},{6,2},{7,11},{8,12},{9,5},{10,... | collective-permute-start | bytes 786440 | tf_op jit(solution)/shard_map/ppermute | solution.py:392
  26.9 6.4 %collective-permute-start.15 = (bf16[256,512]{1,0:T(8,128)(2,1)S(1)}, bf16[256,512]{1,0:T(8,128)(2,1)S(1)}, u32[]{:S(2)}, u32[]{:S(2)}) collective-permute-start(bf16[256,512]{1,0:T(8,128)(2,1)S(1)} %collective-permute-done.5.refs_4_), channel_id=1, source_target_pairs={{0,1},{1,0},{2,3},{3,2},{4,5},{5,4},{6,7},{7,6},{8,9},{9,8},{10,11... | collective-permute-start | bytes 786440 | tf_op jit(solution)/shard_map/ppermute | solution.py:393
  27.6 6.4 %collective-permute-start.9 = (bf16[256,512]{1,0:T(8,128)(2,1)S(1)}, bf16[256,512]{1,0:T(8,128)(2,1)S(1)}, u32[]{:S(2)}, u32[]{:S(2)}) collective-permute-start(bf16[256,512]{1,0:T(8,128)(2,1)S(1)} %collective-permute-done.8.refs_5_), channel_id=1, source_target_pairs={{0,4},{1,3},{2,0},{3,7},{4,8},{5,1},{6,2},{7,11},{8,12},{9,5},{10,... | collective-permute-start | bytes 786440 | tf_op jit(solution)/shard_map/ppermute | solution.py:392
  29.7 6.7 %collective-permute-start.16 = (bf16[256,512]{1,0:T(8,128)(2,1)S(1)}, bf16[256,512]{1,0:T(8,128)(2,1)S(1)}, u32[]{:S(2)}, u32[]{:S(2)}) collective-permute-start(bf16[256,512]{1,0:T(8,128)(2,1)S(1)} %collective-permute-done.8.refs_5_), channel_id=1, source_target_pairs={{0,1},{1,0},{2,3},{3,2},{4,5},{5,4},{6,7},{7,6},{8,9},{9,8},{10,11... | collective-permute-start | bytes 786440 | tf_op jit(solution)/shard_map/ppermute | solution.py:393
  31.2 6.4 %collective-permute-start.12 = (bf16[256,512]{1,0:T(8,128)(2,1)S(1)}, bf16[256,512]{1,0:T(8,128)(2,1)S(1)}, u32[]{:S(2)}, u32[]{:S(2)}) collective-permute-start(bf16[256,512]{1,0:T(8,128)(2,1)S(1)} %collective-permute-done.6.refs_0_), channel_id=1, source_target_pairs={{0,4},{1,3},{2,0},{3,7},{4,8},{5,1},{6,2},{7,11},{8,12},{9,5},{10,... | collective-permute-start | bytes 786440 | tf_op jit(solution)/shard_map/ppermute | solution.py:394
  33.2 5.6 %collective-permute-start.10 = (bf16[256,512]{1,0:T(8,128)(2,1)S(1)}, bf16[256,512]{1,0:T(8,128)(2,1)S(1)}, u32[]{:S(2)}, u32[]{:S(2)}) collective-permute-start(bf16[256,512]{1,0:T(8,128)(2,1)S(1)} %collective-permute-done.6.refs_0_), channel_id=1, source_target_pairs={{0,1},{1,0},{2,3},{3,2},{4,5},{5,4},{6,7},{7,6},{8,9},{9,8},{10,11... | collective-permute-start | bytes 786440 | tf_op jit(solution)/shard_map/ppermute | solution.py:393
  34.0 4.8 %collective-permute-start.11 = (bf16[256,512]{1,0:T(8,128)(2,1)S(1)}, bf16[256,512]{1,0:T(8,128)(2,1)S(1)}, u32[]{:S(2)}, u32[]{:S(2)}) collective-permute-start(bf16[256,512]{1,0:T(8,128)(2,1)S(1)} %collective-permute-done.9.refs_1_), channel_id=1, source_target_pairs={{0,1},{1,0},{2,3},{3,2},{4,5},{5,4},{6,7},{7,6},{8,9},{9,8},{10,11... | collective-permute-start | bytes 786440 | tf_op jit(solution)/shard_map/ppermute | solution.py:393
  37.6 1.7 %collective-permute-start.17 = (bf16[256,512]{1,0:T(8,128)(2,1)S(1)}, bf16[256,512]{1,0:T(8,128)(2,1)S(1)}, u32[]{:S(2)}, u32[]{:S(2)}) collective-permute-start(bf16[256,512]{1,0:T(8,128)(2,1)S(1)} %collective-permute-done.12.refs_0_), channel_id=1, source_target_pairs={{0,1},{1,0},{2,3},{3,2},{4,5},{5,4},{6,7},{7,6},{8,9},{9,8},{10,11... | collective-permute-start | bytes 786440 | tf_op jit(solution)/shard_map/ppermute | solution.py:398
  38.2 6.1 %collective-permute-start.3 = (bf16[256,512]{1,0:T(8,128)(2,1)S(1)}, bf16[256,512]{1,0:T(8,128)(2,1)S(1)}, u32[]{:S(2)}, u32[]{:S(2)}) collective-permute-start(bf16[256,512]{1,0:T(8,128)(2,1)S(1)} %shard_map.81.refs_1_), channel_id=1, source_target_pairs={{0,1},{1,0},{2,3},{3,2},{4,5},{5,4},{6,7},{7,6},{8,9},{9,8},{10,11... | collective-permute-start | bytes 786440 | tf_op jit(solution)/shard_map/ppermute | solution.py:402
  39.6 6.2 %collective-permute-start.18 = (bf16[128,512]{1,0:T(8,128)(2,1)S(1)}, bf16[128,512]{1,0:T(8,128)(2,1)S(1)}, u32[]{:S(2)}, u32[]{:S(2)}) collective-permute-start(bf16[128,512]{1,0:T(8,128)(2,1)S(1)} %get-tuple-element.35), channel_id=1, source_target_pairs={{0,16},{16,0},{1,17},{17,1},{2,18},{18,2},{3,19},{19,3},{4,20},{20... | collective-permute-start | bytes 393224 | tf_op jit(solution)/shard_map/ppermute | solution.py:406

commit v5 on v4

--- a/solution.py
+++ b/solution.py
@@ -10,6 +10,8 @@
 BLOCK = 128
 CORES = 2
 RING_LIMIT = 16
+PACKED = 2
+COPIES = 2
 
 outer_rate = 0.7
 outer_mu = 0.9
@@ -65,24 +67,45 @@
     return chip_at(place, chips) * CORES + (1 - core if other else core)
 
 
-def cast_kernel(grad, out):
-    out[...] = grad[...].astype(out.dtype)
-
-
-def cast_half(grad, which):
+def cast_kernel(grad, *outs):
+    start = 0
+    for out in outs:
+        out[...] = grad[start : start + out.shape[0]].astype(out.dtype)
+        start += out.shape[0]
+
+
+def cast_half(grad, which, *heights):
     rows, cols = grad.shape
     half = rows // 2
-    steps = 2
-    tall = half // steps
     return pl.pallas_call(
         cast_kernel,
-        grid=(steps,),
-        in_specs=[pl.BlockSpec((tall, cols), lambda g: (which() * steps + g, 0))],
-        out_specs=pl.BlockSpec((tall, cols), lambda g: (g, 0)),
-        out_shape=jax.ShapeDtypeStruct((half, cols), jnp.bfloat16),
+        grid=(1,),
+        in_specs=[pl.BlockSpec((half, cols), lambda g: (which(), 0))],
+        out_specs=[pl.BlockSpec((height, cols), lambda g: (0, 0)) for height in heights],
+        out_shape=[jax.ShapeDtypeStruct((height, cols), jnp.bfloat16) for height in heights],
         compiler_params=params(),
         cost_estimate=pl.CostEstimate(flops=half * cols, bytes_accessed=6 * half * cols, transcendentals=0),
     )(grad)
+
+
+def join_kernel(*refs):
+    *parts, out = refs
+    start = 0
+    for part in parts:
+        out[start : start + part.shape[0]] = part[...]
+        start += part.shape[0]
+
+
+def join(*parts):
+    rows, cols = sum(part.shape[0] for part in parts), parts[0].shape[1]
+    return pl.pallas_call(
+        join_kernel,
+        in_specs=[VMEM] * len(parts),
+        out_specs=VMEM,
+        out_shape=jax.ShapeDtypeStruct((rows, cols), parts[0].dtype),
+        compiler_params=params(),
+        cost_estimate=pl.CostEstimate(flops=0, bytes_accessed=4 * rows * cols, transcendentals=0),
+    )(*parts)
 
 
 def mine():
@@ -98,7 +121,7 @@
     return [(slice(r, r + tall), slice(c, c + wide)) for r in range(0, rows, tall) for c in range(0, cols, wide)]
 
 
-def token_kernel(chips, half, tokens, grad, own, sent, whole, inverse):
+def token_kernel(chips, half, tokens, grad, own, sent, more, whole, inverse):
     rows, width = tokens.shape
     shared, kept = slots(chips)
 
@@ -110,7 +133,10 @@
         own[k] = columns(slot, mine())
         sent[k] = columns(slot, others())
     for k, at in enumerate(tiles(grad.shape, rows, half)):
-        sent[len(shared) + k] = grad[at]
+        if k < PACKED:
+            sent[len(shared) + k] = grad[at]
+        else:
+            more[k - PACKED] = grad[at]
     for k, slot in enumerate(kept):
         whole[2 * k] = columns(slot, mine())
         whole[2 * k + 1] = columns(slot, others())
@@ -126,11 +152,12 @@
     rows, width = tokens.shape
     half = width // (chips * CORES * 2)
     shared, kept = slots(chips)
-    counts = len(shared), len(shared) + len(tiles(grad.shape, rows, half)), 2 * len(kept)
+    count = len(tiles(grad.shape, rows, half))
+    counts = len(shared), len(shared) + PACKED, count - PACKED, 2 * len(kept)
     return pl.pallas_call(
         functools.partial(token_kernel, chips, half),
         in_specs=[VMEM] * 2,
-        out_specs=[VMEM] * 4,
+        out_specs=[VMEM] * 5,
         out_shape=[jax.ShapeDtypeStruct((count, rows, half), tokens.dtype) for count in counts]
         + [jax.ShapeDtypeStruct((rows, 1), jnp.float32)],
         compiler_params=params(),
@@ -138,20 +165,21 @@
     )(tokens, grad)
 
 
-def unpack_kernel(first, packed, grad):
+def unpack_kernel(first, packed, more, grad):
+    count = packed.shape[0] - first
     for k, at in enumerate(tiles(grad.shape, *packed.shape[1:])):
-        grad[at] = packed[first + k]
-
-
-def unpack(first, packed, shape):
+        grad[at] = packed[first + k] if k < count else more[k - count]
+
+
+def unpack(first, packed, more, shape):
     return pl.pallas_call(
         functools.partial(unpack_kernel, first),
-        in_specs=[VMEM],
+        in_specs=[VMEM] * 2,
         out_specs=VMEM,
         out_shape=jax.ShapeDtypeStruct(shape, packed.dtype),
         compiler_params=params(),
         cost_estimate=pl.CostEstimate(flops=0, bytes_accessed=4 * shape[0] * shape[1], transcendentals=0),
-    )(packed)
+    )(packed, more)
 
 
 def synced(a, b):
@@ -199,31 +227,41 @@
     )(own, master, momentum, gain)
 
 
+def first_part(offset, own, here, peaks, base, steep, weight):
+    rows = slice(offset, offset + here.shape[0])
+    for k, col in enumerate(range(0, own.shape[1], BLOCK)):
+        at = slice(col, col + BLOCK)
+        a = own[rows, at].astype(jnp.float32)
+        b = here[:, at].astype(jnp.float32)
+        shared = peaks[k, rows, :] + jnp.max(jnp.abs(b), axis=1, keepdims=True) / 2
+        over = 1.0 / shared[:, :1]
+        low_a = jnp.clip(a * over, -1.0, 1.0).astype(jnp.bfloat16).astype(jnp.float32)
+        low_b = jnp.clip(b * over, -1.0, 1.0).astype(jnp.bfloat16).astype(jnp.float32)
+        weight[:, at] = (base[rows, at] + steep[rows, :] * shared * (low_a + low_b)).astype(weight.dtype)
+
+
 def first_kernel(own, here, peaks, base, steep, weight):
-    half, cols = own.shape
-    for start in range(0, half, BLOCK):
-        rows = slice(start, start + BLOCK)
-        for k, col in enumerate(range(0, cols, BLOCK)):
-            at = slice(col, col + BLOCK)
-            a = own[rows, at].astype(jnp.float32)
-            b = here[rows, at].astype(jnp.float32)
-            shared = peaks[k, rows, :] + jnp.max(jnp.abs(b), axis=1, keepdims=True) / 2
-            over = 1.0 / shared[:, :1]
-            low_a = jnp.clip(a * over, -1.0, 1.0).astype(jnp.bfloat16).astype(jnp.float32)
-            low_b = jnp.clip(b * over, -1.0, 1.0).astype(jnp.bfloat16).astype(jnp.float32)
-            weight[rows, at] = (base[rows, at] + steep[rows, :] * shared * (low_a + low_b)).astype(weight.dtype)
-
-
-def first_weight(own, here, ready):
-    half, cols = own.shape
-    return pl.pallas_call(
-        first_kernel,
-        in_specs=[VMEM] * 5,
-        out_specs=VMEM,
-        out_shape=jax.ShapeDtypeStruct((half, cols), jnp.bfloat16),
-        compiler_params=params(),
-        cost_estimate=pl.CostEstimate(flops=20 * half * cols, bytes_accessed=14 * half * cols, transcendentals=0),
-    )(own, here, *ready)
+    first_part(0, own, here, peaks, base, steep, weight)
+
+
+def second_kernel(own, here, peaks, base, steep, done, weight, whole):
+    offset = done.shape[0]
+    first_part(offset, own, here, peaks, base, steep, weight)
+    whole[:offset] = done[...]
+    whole[offset:] = weight[...]
+
+
+def half_weight(own, here, ready, *done):
+    rows, cols = here.shape
+    shapes = [(rows, cols)] + [(part.shape[0] + rows, cols) for part in done]
+    return pl.pallas_call(
+        second_kernel if done else first_kernel,
+        in_specs=[VMEM] * (5 + len(done)),
+        out_specs=[VMEM] * len(shapes),
+        out_shape=[jax.ShapeDtypeStruct(shape, jnp.bfloat16) for shape in shapes],
+        compiler_params=params(),
+        cost_estimate=pl.CostEstimate(flops=20 * rows * cols, bytes_accessed=14 * rows * cols, transcendentals=0),
+    )(own, here, *ready, *done)
 
 
 def weight_kernel(which, first, second, master, momentum, gain, weight):
@@ -377,19 +415,30 @@
 
     gain = norm_gain.reshape(-1, BLOCK)
     half = master.shape[0] // 2
-    grad_sent = lax.dynamic_slice_in_dim(pseudo_grad[0], others() * half, half).astype(jnp.bfloat16)
-    grad_here = cross(grad_sent)
-    grad_own = cast_half(pseudo_grad[0], mine)
-    own, sent, whole, inverse = split_tokens(tokens, grad_own, chips)
+    sent_parts = cast_half(pseudo_grad[0], others, half // 2, half // 2)
+    here_parts = [cross(part) for part in sent_parts]
+    (grad_own,) = cast_half(pseudo_grad[0], mine, half)
+    own, sent, more, whole, inverse = split_tokens(tokens, grad_own, chips)
     ready = get_ready(grad_own, master, momentum, gain)
-    grad_here, own, *ready = tie((grad_here, own, *ready))
-    other = cross(sent)
-
-    a = weight = first_weight(grad_own, grad_here, ready)
-    b = near = swap(weight)
+    here_parts[0], own, *ready = tie((here_parts[0], own, *ready))
+    other, more = cross(sent), cross(more)
+
+    (head,) = half_weight(grad_own, here_parts[0], ready)
+    tail, weight = half_weight(grad_own, here_parts[1], ready, head)
+    swapped = swap(head)
+    for _ in range(COPIES):
+        swapped = join(swapped)
+    b = near = join(swapped, swap(tail))
     blocks = []
     for step in range(1, chips // 2):
-        a, b = ring(a), ring(b)
+        if step == 1:
+            arrived = ring(head)
+            for _ in range(COPIES):
+                arrived = join(arrived)
+            a = join(arrived, ring(tail))
+        else:
+            a = ring(a)
+        b = ring(b)
         blocks += [a, b, swap(a), swap(b)]
     a = ring(a)
     ahead = len(blocks) - 2 * CORES
@@ -397,7 +446,8 @@
     far, total = tie((a, total))
     late = [a, swap(far)]
 
-    grad_there = unpack(len(slots(chips)[0]), other, grad_own.shape)
+    grad_sent, grad_here = join(*sent_parts), join(*here_parts)
+    grad_there = unpack(len(slots(chips)[0]), other, more, grad_own.shape)
     weight_over = sync_weight(others, grad_sent, grad_there, master, momentum, gain)
     own_part = dot_own(0, whole, [weight, weight_over, near, swap(weight_over)])
     master_new, momentum_new = sync_outer(grad_own, grad_here, grad_sent, grad_there, master, momentum)

time: 46.8 us -> 45.8 us (0.979)
  starting transfers between devices: 20 us -> 26 us
  waiting for transfers between devices: 14.2 us -> 10.3 us
  local copies, waits for them, and re-layouts: 4.65 us -> 1.24 us
    ppermute x9 -> x11, waiting for transfers between devices: 12.5 us -> 5.7 us  [the longest x3 2.86 us: by_permutes(): b = ring(b)]
    ppermute x1 -> x3, starting transfers between devices: 2.02 us -> 6.1 us  [by_permutes(): a = ring(a)]
    ppermute x1 -> x3, waiting for transfers between devices: 0.54 us -> 3.19 us  [by_permutes(): a = ring(a)]
    ppermute x9 -> x11, starting transfers between devices: 14.9 us -> 17.3 us  [the longest x3 6.23 us: by_permutes(): b = ring(b)]
    unnamed x10, local copies, waits for them, and re-layouts: 3.57 us -> 1.24 us
    convert_element_type x1 -> x0, local copies, waits for them, and re-layouts: 1.08 us -> none  [by_permutes(): lax.dynamic_slice_in_dim(pseudo_grad[0], others() * half, half)]
    ppermute x6, starting transfers between devices: 0.02 us -> 0.66 us  [by_permutes(): blocks += [a, b, swap(a), swap(b)]]
    ppermute x1, starting transfers between devices: 2.52 us -> 1.93 us  [by_permutes(): keys = close(own_part, mine_part, cross(sent_part), inverse)]
  transfers between devices with their start and end apart: 19 -> 23, of which waited for: 10 -> 10; matrix products, arithmetic and copies ran while one was open for 0% -> 0% of each run, Pallas kernels for 13% -> 14%
where the time goes in v5:
time: 45.8 us; the launch traced here: 45.6 us
  starting transfers between devices  26 us (57%)
  waiting for transfers between devices  10.3 us (22%)
  Pallas kernels  7.17 us (16%)
  local copies, waits for them, and re-layouts  1.24 us (3%)
  between operations  0.85 us (2%)
    ppermute x3, starting transfers between devices, by_permutes(): b = ring(b)  6.23 us
    ppermute x3, starting transfers between devices, by_permutes(): a = ring(a)  6.1 us
    ppermute x2, starting transfers between devices, by_permutes(): other, more = (cross(sent), cross(more))  3.52 us
    ppermute x3, waiting for transfers between devices, by_permutes(): a = ring(a)  3.19 us
    ppermute x2, starting transfers between devices, by_permutes(): here_parts = [cross(part) for part in sent_parts]  3.11 us
    ppermute x3, waiting for transfers between devices, by_permutes(): b = ring(b)  2.86 us
    pallas_call x1, Pallas kernels, sync_outer(): pl.pallas_call(outer_kernel, in_specs=[VMEM] * 6, out_specs=[VMEM] * 2, o...  2.28 us
    ppermute x1, starting transfers between devices, by_permutes(): arrived = ring(head)  2.17 us
  transfers between devices with their start and end apart: 23, of which 10 were waited for; matrix products, arithmetic and copies ran while one was open for 0% of the time, Pallas kernels for 14%

profile of v5, /device:TPU:0, one launch (start us, length us, event | category | flops | bytes accessed | tf_op | source)
XLA Modules:
  0.0 45.6 jit_solution(5295308511389432654)
XLA Ops:
  0.6 1.2 %copy-done.2 = f32[1,512,512]{2,1,0:T(8,128)S(1)} copy-done((f32[1,512,512]{2,1,0:T(8,128)S(1)}, f32[1,512,512]{2,1,0:T(8,128)}, u32[]{:S(2)}) %copy-start.2) | copy-done | bytes 1048600
  1.9 3.0 %collective-permute-start.1 = (bf16[128,512]{1,0:T(8,128)(2,1)S(1)}, bf16[128,512]{1,0:T(8,128)(2,1)S(1)}, u32[]{:S(2)}, u32[]{:S(2)}) collective-permute-start(bf16[128,512]{1,0:T(8,128)(2,1)S(1)} %get-tuple-element.28.refs_0_), channel_id=1, source_target_pairs={{0,16},{16,0},{1,17},{17,1},{2,18},{18,2},{3,19},{19,3},{4,20},{20... | collective-permute-start | bytes 393224 | tf_op jit(solution)/shard_map/ppermute | solution.py:419
  5.1 0.7 %shard_map.77 = (bf16[14,128,256]{2,1,0:T(8,128)(2,1)S(1)}, bf16[16,128,256]{2,1,0:T(8,128)(2,1)S(1)}, bf16[2,128,256]{2,1,0:T(8,128)(2,1)S(1)}, bf16[4,128,256]{2,1,0:T(8,128)(2,1)S(1)}, f32[128,1]{1,0:T(8,128)S(1)}) custom-call(bf16[128,8192]{1,0:T(8,128)(2,1)S(1)} %copy-done.3, bf16[256,512]{1,0:T(8,128)(2,1)S(1)} %shard_map.76.grad.own.here_a), custom_call_target="tpu_custom_call" | custom-call | flops 2097152 | bytes 4194304 | tf_op jit(solution)/shard_map/pallas_call | solution.py:157
  5.8 2.0 %collective-permute-start.2 = (bf16[16,128,256]{2,1,0:T(8,128)(2,1)S(1)}, bf16[16,128,256]{2,1,0:T(8,128)(2,1)S(1)}, u32[]{:S(2)}, u32[]{:S(2)}) collective-permute-start(bf16[16,128,256]{2,1,0:T(8,128)(2,1)S(1)} %get-tuple-element.38), channel_id=1, source_target_pairs={{0,16},{16,0},{1,17},{17,1},{2,18},{18,2},{3,19},{19,3},{4,20},{20... | collective-permute-start | bytes 3145736 | tf_op jit(solution)/shard_map/ppermute | solution.py:424
  7.8 0.3 shard_map.79
  8.1 1.2 %collective-permute-done.1.here.refs_0_ = bf16[128,512]{1,0:T(8,128)(2,1)S(1)} collective-permute-done((bf16[128,512]{1,0:T(8,128)(2,1)S(1)}, bf16[128,512]{1,0:T(8,128)(2,1)S(1)}, u32[]{:S(2)}, u32[]{:S(2)}) %collective-permute-start.1) | collective-permute-done | bytes 131104 | tf_op jit(solution)/shard_map/ppermute | solution.py:419
  9.6 2.2 %collective-permute-start.7 = (bf16[128,512]{1,0:T(8,128)(2,1)S(1)}, bf16[128,512]{1,0:T(8,128)(2,1)S(1)}, u32[]{:S(2)}, u32[]{:S(2)}) collective-permute-start(bf16[128,512]{1,0:T(8,128)(2,1)S(1)} %shard_map.80.done), channel_id=1, source_target_pairs={{0,4},{1,3},{2,0},{3,7},{4,8},{5,1},{6,2},{7,11},{8,12},{9,5},{10,... | collective-permute-start | bytes 393224 | tf_op jit(solution)/shard_map/ppermute | solution.py:435
  11.7 0.3 collective-permute-done.here.refs_1_
  12.1 0.3 shard_map.81
  12.6 2.0 %collective-permute-start.8 = (bf16[128,512]{1,0:T(8,128)(2,1)S(1)}, bf16[128,512]{1,0:T(8,128)(2,1)S(1)}, u32[]{:S(2)}, u32[]{:S(2)}) collective-permute-start(bf16[128,512]{1,0:T(8,128)(2,1)S(1)} %get-tuple-element.40), channel_id=1, source_target_pairs={{0,4},{1,3},{2,0},{3,7},{4,8},{5,1},{6,2},{7,11},{8,12},{9,5},{10,... | collective-permute-start | bytes 393224 | tf_op jit(solution)/shard_map/ppermute | solution.py:438
  14.8 2.1 %collective-permute-start.11 = (bf16[256,512]{1,0:T(8,128)(2,1)S(1)}, bf16[256,512]{1,0:T(8,128)(2,1)S(1)}, u32[]{:S(2)}, u32[]{:S(2)}) collective-permute-start(bf16[256,512]{1,0:T(8,128)(2,1)S(1)} %shard_map.87.refs_2_), channel_id=1, source_target_pairs={{0,4},{1,3},{2,0},{3,7},{4,8},{5,1},{6,2},{7,11},{8,12},{9,5},{10,... | collective-permute-start | bytes 786440 | tf_op jit(solution)/shard_map/ppermute | solution.py:441
  16.9 0.7 %collective-permute-done.8.refs_1_ = bf16[128,512]{1,0:T(8,128)(2,1)S(1)} collective-permute-done((bf16[128,512]{1,0:T(8,128)(2,1)S(1)}, bf16[128,512]{1,0:T(8,128)(2,1)S(1)}, u32[]{:S(2)}, u32[]{:S(2)}) %collective-permute-start.8) | collective-permute-done | bytes 131104 | tf_op jit(solution)/shard_map/ppermute | solution.py:438
  17.6 2.1 %collective-permute-start.9 = (bf16[256,512]{1,0:T(8,128)(2,1)S(1)}, bf16[256,512]{1,0:T(8,128)(2,1)S(1)}, u32[]{:S(2)}, u32[]{:S(2)}) collective-permute-start(bf16[256,512]{1,0:T(8,128)(2,1)S(1)} %shard_map.91.refs_0_), channel_id=1, source_target_pairs={{0,4},{1,3},{2,0},{3,7},{4,8},{5,1},{6,2},{7,11},{8,12},{9,5},{10,... | collective-permute-start | bytes 786440 | tf_op jit(solution)/shard_map/ppermute | solution.py:440
  19.7 1.5 %collective-permute-done.11.refs_1_ = bf16[256,512]{1,0:T(8,128)(2,1)S(1)} collective-permute-done((bf16[256,512]{1,0:T(8,128)(2,1)S(1)}, bf16[256,512]{1,0:T(8,128)(2,1)S(1)}, u32[]{:S(2)}, u32[]{:S(2)}) %collective-permute-start.11) | collective-permute-done | bytes 262176 | tf_op jit(solution)/shard_map/ppermute | solution.py:441
  21.2 2.1 %collective-permute-start.12 = (bf16[256,512]{1,0:T(8,128)(2,1)S(1)}, bf16[256,512]{1,0:T(8,128)(2,1)S(1)}, u32[]{:S(2)}, u32[]{:S(2)}) collective-permute-start(bf16[256,512]{1,0:T(8,128)(2,1)S(1)} %collective-permute-done.11.refs_1_), channel_id=1, source_target_pairs={{0,4},{1,3},{2,0},{3,7},{4,8},{5,1},{6,2},{7,11},{8,12},{9,5},{10,... | collective-permute-start | bytes 786440 | tf_op jit(solution)/shard_map/ppermute | solution.py:441
  23.3 0.8 %collective-permute-done.9.refs_4_ = bf16[256,512]{1,0:T(8,128)(2,1)S(1)} collective-permute-done((bf16[256,512]{1,0:T(8,128)(2,1)S(1)}, bf16[256,512]{1,0:T(8,128)(2,1)S(1)}, u32[]{:S(2)}, u32[]{:S(2)}) %collective-permute-start.9) | collective-permute-done | bytes 262176 | tf_op jit(solution)/shard_map/ppermute | solution.py:440
  24.0 2.0 %collective-permute-start.10 = (bf16[256,512]{1,0:T(8,128)(2,1)S(1)}, bf16[256,512]{1,0:T(8,128)(2,1)S(1)}, u32[]{:S(2)}, u32[]{:S(2)}) collective-permute-start(bf16[256,512]{1,0:T(8,128)(2,1)S(1)} %collective-permute-done.9.refs_4_), channel_id=1, source_target_pairs={{0,4},{1,3},{2,0},{3,7},{4,8},{5,1},{6,2},{7,11},{8,12},{9,5},{10,... | collective-permute-start | bytes 786440 | tf_op jit(solution)/shard_map/ppermute | solution.py:440
  26.2 1.4 %collective-permute-done.12.refs_5_ = bf16[256,512]{1,0:T(8,128)(2,1)S(1)} collective-permute-done((bf16[256,512]{1,0:T(8,128)(2,1)S(1)}, bf16[256,512]{1,0:T(8,128)(2,1)S(1)}, u32[]{:S(2)}, u32[]{:S(2)}) %collective-permute-start.12) | collective-permute-done | bytes 262176 | tf_op jit(solution)/shard_map/ppermute | solution.py:441
  27.6 2.1 %collective-permute-start.13 = (bf16[256,512]{1,0:T(8,128)(2,1)S(1)}, bf16[256,512]{1,0:T(8,128)(2,1)S(1)}, u32[]{:S(2)}, u32[]{:S(2)}) collective-permute-start(bf16[256,512]{1,0:T(8,128)(2,1)S(1)} %collective-permute-done.12.refs_5_), channel_id=1, source_target_pairs={{0,4},{1,3},{2,0},{3,7},{4,8},{5,1},{6,2},{7,11},{8,12},{9,5},{10,... | collective-permute-start | bytes 786440 | tf_op jit(solution)/shard_map/ppermute | solution.py:441
  29.6 0.8 %collective-permute-done.10.refs_0_ = bf16[256,512]{1,0:T(8,128)(2,1)S(1)} collective-permute-done((bf16[256,512]{1,0:T(8,128)(2,1)S(1)}, bf16[256,512]{1,0:T(8,128)(2,1)S(1)}, u32[]{:S(2)}, u32[]{:S(2)}) %collective-permute-start.10) | collective-permute-done | bytes 262176 | tf_op jit(solution)/shard_map/ppermute | solution.py:440
  30.4 2.0 %collective-permute-start.16 = (bf16[256,512]{1,0:T(8,128)(2,1)S(1)}, bf16[256,512]{1,0:T(8,128)(2,1)S(1)}, u32[]{:S(2)}, u32[]{:S(2)}) collective-permute-start(bf16[256,512]{1,0:T(8,128)(2,1)S(1)} %collective-permute-done.10.refs_0_), channel_id=1, source_target_pairs={{0,4},{1,3},{2,0},{3,7},{4,8},{5,1},{6,2},{7,11},{8,12},{9,5},{10,... | collective-permute-start | bytes 786440 | tf_op jit(solution)/shard_map/ppermute | solution.py:443
  32.4 1.5 %collective-permute-start.3 = (bf16[2,128,256]{2,1,0:T(8,128)(2,1)S(1)}, bf16[2,128,256]{2,1,0:T(8,128)(2,1)S(1)}, u32[]{:S(2)}, u32[]{:S(2)}) collective-permute-start(bf16[2,128,256]{2,1,0:T(8,128)(2,1)S(1)} %get-tuple-element.39), channel_id=1, source_target_pairs={{0,16},{16,0},{1,17},{17,1},{2,18},{18,2},{3,19},{19,3},{4,20},{20... | collective-permute-start | bytes 393224 | tf_op jit(solution)/shard_map/ppermute | solution.py:424
  34.0 0.5 %collective-permute-start.15 = (bf16[256,512]{1,0:T(8,128)(2,1)S(1)}, bf16[256,512]{1,0:T(8,128)(2,1)S(1)}, u32[]{:S(2)}, u32[]{:S(2)}) collective-permute-start(bf16[256,512]{1,0:T(8,128)(2,1)S(1)} %collective-permute-done.13.refs_1_), channel_id=1, source_target_pairs={{0,1},{1,0},{2,3},{3,2},{4,5},{5,4},{6,7},{7,6},{8,9},{9,8},{10,11... | collective-permute-start | bytes 786440 | tf_op jit(solution)/shard_map/ppermute | solution.py:442
  34.5 0.7 %shard_map.92.refs_4_ = f32[256,512]{1,0:T(8,128)S(1)} custom-call(bf16[14,128,256]{2,1,0:T(8,128)(2,1)S(1)} %get-tuple-element.41.own, bf16[16,128,256]{2,1,0:T(8,128)(2,1)S(1)} %collective-permute-done.2.packed.other, bf16[256,512]{1,0:T(8,128)(2,1)S(1)} %shard_map.91.refs_0_, bf16[256,512]{1,0:T(8,128)(2,1)S(1)} %collective-permute-done.11.refs_1_, ...), custom_call_target="tpu_custom_call" | custom-call | flops 536870912 | bytes 3145728 | tf_op jit(solution)/shard_map/pallas_call | solution.py:361
  35.2 1.6 %collective-permute-done.16.refs_0_ = bf16[256,512]{1,0:T(8,128)(2,1)S(1)} collective-permute-done((bf16[256,512]{1,0:T(8,128)(2,1)S(1)}, bf16[256,512]{1,0:T(8,128)(2,1)S(1)}, u32[]{:S(2)}, u32[]{:S(2)}) %collective-permute-start.16) | collective-permute-done | bytes 262176 | tf_op jit(solution)/shard_map/ppermute | solution.py:443
  36.8 0.6 %collective-permute-done.3.more = bf16[2,128,256]{2,1,0:T(8,128)(2,1)S(1)} collective-permute-done((bf16[2,128,256]{2,1,0:T(8,128)(2,1)S(1)}, bf16[2,128,256]{2,1,0:T(8,128)(2,1)S(1)}, u32[]{:S(2)}, u32[]{:S(2)}) %collective-permute-start.3) | collective-permute-done | bytes 131104 | tf_op jit(solution)/shard_map/ppermute | solution.py:424
  37.4 0.6 %shard_map.84.refs_1_ = bf16[256,512]{1,0:T(8,128)(2,1)S(1)} custom-call(bf16[256,512]{1,0:T(8,128)(2,1)S(1)} %shard_map.82.first.there_a, bf16[256,512]{1,0:T(8,128)(2,1)S(1)} %shard_map.83.second.there_b, f32[512,512]{1,0:T(8,128)S(1)} %copy-done, f32[512,512]{1,0:T(8,128)S(1)} %copy-done.1, f32[64,128]{1,0:T(8,128)S(1)} %bitcast.5), custom_call_target="tpu_custom_call" | custom-call | flops 3932160 | bytes 1835008 | tf_op jit(solution)/shard_map/pallas_call | solution.py:285
  38.2 0.4 shard_map.93.early
  38.9 1.9 %collective-permute-start.22 = (bf16[128,512]{1,0:T(8,128)(2,1)S(1)}, bf16[128,512]{1,0:T(8,128)(2,1)S(1)}, u32[]{:S(2)}, u32[]{:S(2)}) collective-permute-start(bf16[128,512]{1,0:T(8,128)(2,1)S(1)} %get-tuple-element.45), channel_id=1, source_target_pairs={{0,16},{16,0},{1,17},{17,1},{2,18},{18,2},{3,19},{19,3},{4,20},{20... | collective-permute-start | bytes 393224 | tf_op jit(solution)/shard_map/ppermute | solution.py:456
  40.9 2.3 %shard_map.97 = (f32[512,512]{1,0:T(8,128)}, f32[512,512]{1,0:T(8,128)}) custom-call(bf16[256,512]{1,0:T(8,128)(2,1)S(1)} %shard_map.76.grad.own.here_a, bf16[256,512]{1,0:T(8,128)(2,1)S(1)} %shard_map.96.here_b, bf16[256,512]{1,0:T(8,128)(2,1)S(1)} %shard_map.82.first.there_a, bf16[256,512]{1,0:T(8,128)(2,1)S(1)} %shard_map.83.second.there_b, ...), custom_call_target="tpu_custom_call" | custom-call | flops 7864320 | bytes 5242880 | tf_op jit(solution)/shard_map/pallas_call | solution.py:314
  43.5 1.4 %collective-permute-done.22.other_part = bf16[128,512]{1,0:T(8,128)(2,1)S(1)} collective-permute-done((bf16[128,512]{1,0:T(8,128)(2,1)S(1)}, bf16[128,512]{1,0:T(8,128)(2,1)S(1)}, u32[]{:S(2)}, u32[]{:S(2)}) %collective-permute-start.22) | collective-permute-done | bytes 131104 | tf_op jit(solution)/shard_map/ppermute | solution.py:456
  44.9 0.7 %shard_map.95 = bf16[128,512]{1,0:T(8,128)(2,1)} custom-call(f32[128,512]{1,0:T(8,128)S(1)} %shard_map.88.own_part, f32[128,512]{1,0:T(8,128)S(1)} %get-tuple-element.44.mine_part, bf16[128,512]{1,0:T(8,128)(2,1)S(1)} %collective-permute-done.22.other_part, f32[128,1]{1,0:T(8,128)S(1)} %get-tuple-element.46.inverse), custom_call_target="tpu_custom_call" | custom-call | tf_op jit(solution)/shard_map/pallas_call | solution.py:400
  (46 shorter events, 1.7 us)
Async XLA Ops:
  0.6 1.2 %copy-start.2 = (f32[1,512,512]{2,1,0:T(8,128)S(1)}, f32[1,512,512]{2,1,0:T(8,128)}, u32[]{:S(2)}) copy-start(f32[1,512,512]{2,1,0:T(8,128)} %param.9) | copy-start | bytes 3145732
  1.9 3.2 %copy-start.3 = (bf16[128,8192]{1,0:T(8,128)(2,1)S(1)}, bf16[128,8192]{1,0:T(8,128)(2,1)}, u32[]{:S(2)}) copy-start(bf16[128,8192]{1,0:T(8,128)(2,1)} %tokens.1) | copy-start | bytes 6291460
  1.9 5.9 %copy-start = (f32[512,512]{1,0:T(8,128)S(1)}, f32[512,512]{1,0:T(8,128)}, u32[]{:S(2)}) copy-start(f32[512,512]{1,0:T(8,128)} %master.5) | copy-start | bytes 3145732
  1.9 5.9 %copy-start.1 = (f32[512,512]{1,0:T(8,128)S(1)}, f32[512,512]{1,0:T(8,128)}, u32[]{:S(2)}) copy-start(f32[512,512]{1,0:T(8,128)} %momentum.5) | copy-start | bytes 3145732
  1.9 5.9 %copy-start.4 = (f32[8192]{0:T(1024)S(1)}, f32[8192]{0:T(1024)}, u32[]{:S(2)}) copy-start(f32[8192]{0:T(1024)} %param.6) | copy-start | bytes 98308
  1.9 7.4 %collective-permute-start.1 = (bf16[128,512]{1,0:T(8,128)(2,1)S(1)}, bf16[128,512]{1,0:T(8,128)(2,1)S(1)}, u32[]{:S(2)}, u32[]{:S(2)}) collective-permute-start(bf16[128,512]{1,0:T(8,128)(2,1)S(1)} %get-tuple-element.28.refs_0_), channel_id=1, source_target_pairs={{0,16},{16,0},{1,17},{17,1},{2,18},{18,2},{3,19},{19,3},{4,20},{20... | collective-permute-start | bytes 393224 | tf_op jit(solution)/shard_map/ppermute | solution.py:419
  5.0 7.1 %collective-permute-start = (bf16[128,512]{1,0:T(8,128)(2,1)S(1)}, bf16[128,512]{1,0:T(8,128)(2,1)S(1)}, u32[]{:S(2)}, u32[]{:S(2)}) collective-permute-start(bf16[128,512]{1,0:T(8,128)(2,1)S(1)} %get-tuple-element.27.refs_1_), channel_id=1, source_target_pairs={{0,16},{16,0},{1,17},{17,1},{2,18},{18,2},{3,19},{19,3},{4,20},{20... | collective-permute-start | bytes 393224 | tf_op jit(solution)/shard_map/ppermute | solution.py:419
  5.8 28.7 %collective-permute-start.2 = (bf16[16,128,256]{2,1,0:T(8,128)(2,1)S(1)}, bf16[16,128,256]{2,1,0:T(8,128)(2,1)S(1)}, u32[]{:S(2)}, u32[]{:S(2)}) collective-permute-start(bf16[16,128,256]{2,1,0:T(8,128)(2,1)S(1)} %get-tuple-element.38), channel_id=1, source_target_pairs={{0,16},{16,0},{1,17},{17,1},{2,18},{18,2},{3,19},{19,3},{4,20},{20... | collective-permute-start | bytes 3145736 | tf_op jit(solution)/shard_map/ppermute | solution.py:424
  9.6 5.1 %collective-permute-start.7 = (bf16[128,512]{1,0:T(8,128)(2,1)S(1)}, bf16[128,512]{1,0:T(8,128)(2,1)S(1)}, u32[]{:S(2)}, u32[]{:S(2)}) collective-permute-start(bf16[128,512]{1,0:T(8,128)(2,1)S(1)} %shard_map.80.done), channel_id=1, source_target_pairs={{0,4},{1,3},{2,0},{3,7},{4,8},{5,1},{6,2},{7,11},{8,12},{9,5},{10,... | collective-permute-start | bytes 393224 | tf_op jit(solution)/shard_map/ppermute | solution.py:435
  11.7 2.9 %collective-permute-start.4 = (bf16[128,512]{1,0:T(8,128)(2,1)S(1)}, bf16[128,512]{1,0:T(8,128)(2,1)S(1)}, u32[]{:S(2)}, u32[]{:S(2)}) collective-permute-start(bf16[128,512]{1,0:T(8,128)(2,1)S(1)} %shard_map.80.done), channel_id=1, source_target_pairs={{0,1},{1,0},{2,3},{3,2},{4,5},{5,4},{6,7},{7,6},{8,9},{9,8},{10,11... | collective-permute-start | bytes 393224 | tf_op jit(solution)/shard_map/ppermute | solution.py:428
  12.4 2.3 %collective-permute-start.5 = (bf16[128,512]{1,0:T(8,128)(2,1)S(1)}, bf16[128,512]{1,0:T(8,128)(2,1)S(1)}, u32[]{:S(2)}, u32[]{:S(2)}) collective-permute-start(bf16[128,512]{1,0:T(8,128)(2,1)S(1)} %get-tuple-element.40), channel_id=1, source_target_pairs={{0,1},{1,0},{2,3},{3,2},{4,5},{5,4},{6,7},{7,6},{8,9},{9,8},{10,11... | collective-permute-start | bytes 393224 | tf_op jit(solution)/shard_map/ppermute | solution.py:431
  12.6 5.0 %collective-permute-start.8 = (bf16[128,512]{1,0:T(8,128)(2,1)S(1)}, bf16[128,512]{1,0:T(8,128)(2,1)S(1)}, u32[]{:S(2)}, u32[]{:S(2)}) collective-permute-start(bf16[128,512]{1,0:T(8,128)(2,1)S(1)} %get-tuple-element.40), channel_id=1, source_target_pairs={{0,4},{1,3},{2,0},{3,7},{4,8},{5,1},{6,2},{7,11},{8,12},{9,5},{10,... | collective-permute-start | bytes 393224 | tf_op jit(solution)/shard_map/ppermute | solution.py:438
  14.8 6.4 %collective-permute-start.11 = (bf16[256,512]{1,0:T(8,128)(2,1)S(1)}, bf16[256,512]{1,0:T(8,128)(2,1)S(1)}, u32[]{:S(2)}, u32[]{:S(2)}) collective-permute-start(bf16[256,512]{1,0:T(8,128)(2,1)S(1)} %shard_map.87.refs_2_), channel_id=1, source_target_pairs={{0,4},{1,3},{2,0},{3,7},{4,8},{5,1},{6,2},{7,11},{8,12},{9,5},{10,... | collective-permute-start | bytes 786440 | tf_op jit(solution)/shard_map/ppermute | solution.py:441
  17.6 6.4 %collective-permute-start.9 = (bf16[256,512]{1,0:T(8,128)(2,1)S(1)}, bf16[256,512]{1,0:T(8,128)(2,1)S(1)}, u32[]{:S(2)}, u32[]{:S(2)}) collective-permute-start(bf16[256,512]{1,0:T(8,128)(2,1)S(1)} %shard_map.91.refs_0_), channel_id=1, source_target_pairs={{0,4},{1,3},{2,0},{3,7},{4,8},{5,1},{6,2},{7,11},{8,12},{9,5},{10,... | collective-permute-start | bytes 786440 | tf_op jit(solution)/shard_map/ppermute | solution.py:440
  19.7 6.4 %collective-permute-start.17 = (bf16[256,512]{1,0:T(8,128)(2,1)S(1)}, bf16[256,512]{1,0:T(8,128)(2,1)S(1)}, u32[]{:S(2)}, u32[]{:S(2)}) collective-permute-start(bf16[256,512]{1,0:T(8,128)(2,1)S(1)} %shard_map.91.refs_0_), channel_id=1, source_target_pairs={{0,1},{1,0},{2,3},{3,2},{4,5},{5,4},{6,7},{7,6},{8,9},{9,8},{10,11... | collective-permute-start | bytes 786440 | tf_op jit(solution)/shard_map/ppermute | solution.py:442
  21.2 6.4 %collective-permute-start.12 = (bf16[256,512]{1,0:T(8,128)(2,1)S(1)}, bf16[256,512]{1,0:T(8,128)(2,1)S(1)}, u32[]{:S(2)}, u32[]{:S(2)}) collective-permute-start(bf16[256,512]{1,0:T(8,128)(2,1)S(1)} %collective-permute-done.11.refs_1_), channel_id=1, source_target_pairs={{0,4},{1,3},{2,0},{3,7},{4,8},{5,1},{6,2},{7,11},{8,12},{9,5},{10,... | collective-permute-start | bytes 786440 | tf_op jit(solution)/shard_map/ppermute | solution.py:441
  24.0 3.5 %collective-permute-start.19 = (bf16[256,512]{1,0:T(8,128)(2,1)S(1)}, bf16[256,512]{1,0:T(8,128)(2,1)S(1)}, u32[]{:S(2)}, u32[]{:S(2)}) collective-permute-start(bf16[256,512]{1,0:T(8,128)(2,1)S(1)} %collective-permute-done.9.refs_4_), channel_id=1, source_target_pairs={{0,1},{1,0},{2,3},{3,2},{4,5},{5,4},{6,7},{7,6},{8,9},{9,8},{10,11... | collective-permute-start | bytes 786440 | tf_op jit(solution)/shard_map/ppermute | solution.py:442
  24.0 6.4 %collective-permute-start.10 = (bf16[256,512]{1,0:T(8,128)(2,1)S(1)}, bf16[256,512]{1,0:T(8,128)(2,1)S(1)}, u32[]{:S(2)}, u32[]{:S(2)}) collective-permute-start(bf16[256,512]{1,0:T(8,128)(2,1)S(1)} %collective-permute-done.9.refs_4_), channel_id=1, source_target_pairs={{0,4},{1,3},{2,0},{3,7},{4,8},{5,1},{6,2},{7,11},{8,12},{9,5},{10,... | collective-permute-start | bytes 786440 | tf_op jit(solution)/shard_map/ppermute | solution.py:440
  26.1 6.4 %collective-permute-start.18 = (bf16[256,512]{1,0:T(8,128)(2,1)S(1)}, bf16[256,512]{1,0:T(8,128)(2,1)S(1)}, u32[]{:S(2)}, u32[]{:S(2)}) collective-permute-start(bf16[256,512]{1,0:T(8,128)(2,1)S(1)} %collective-permute-done.11.refs_1_), channel_id=1, source_target_pairs={{0,1},{1,0},{2,3},{3,2},{4,5},{5,4},{6,7},{7,6},{8,9},{9,8},{10,11... | collective-permute-start | bytes 786440 | tf_op jit(solution)/shard_map/ppermute | solution.py:442
  27.6 6.4 %collective-permute-start.20 = (bf16[256,512]{1,0:T(8,128)(2,1)S(1)}, bf16[256,512]{1,0:T(8,128)(2,1)S(1)}, u32[]{:S(2)}, u32[]{:S(2)}) collective-permute-start(bf16[256,512]{1,0:T(8,128)(2,1)S(1)} %collective-permute-done.12.refs_5_), channel_id=1, source_target_pairs={{0,1},{1,0},{2,3},{3,2},{4,5},{5,4},{6,7},{7,6},{8,9},{9,8},{10,11... | collective-permute-start | bytes 786440 | tf_op jit(solution)/shard_map/ppermute | solution.py:442
  27.6 6.4 %collective-permute-start.13 = (bf16[256,512]{1,0:T(8,128)(2,1)S(1)}, bf16[256,512]{1,0:T(8,128)(2,1)S(1)}, u32[]{:S(2)}, u32[]{:S(2)}) collective-permute-start(bf16[256,512]{1,0:T(8,128)(2,1)S(1)} %collective-permute-done.12.refs_5_), channel_id=1, source_target_pairs={{0,4},{1,3},{2,0},{3,7},{4,8},{5,1},{6,2},{7,11},{8,12},{9,5},{10,... | collective-permute-start | bytes 786440 | tf_op jit(solution)/shard_map/ppermute | solution.py:441
  30.4 6.4 %collective-permute-start.16 = (bf16[256,512]{1,0:T(8,128)(2,1)S(1)}, bf16[256,512]{1,0:T(8,128)(2,1)S(1)}, u32[]{:S(2)}, u32[]{:S(2)}) collective-permute-start(bf16[256,512]{1,0:T(8,128)(2,1)S(1)} %collective-permute-done.10.refs_0_), channel_id=1, source_target_pairs={{0,4},{1,3},{2,0},{3,7},{4,8},{5,1},{6,2},{7,11},{8,12},{9,5},{10,... | collective-permute-start | bytes 786440 | tf_op jit(solution)/shard_map/ppermute | solution.py:443
  32.4 5.0 %collective-permute-start.3 = (bf16[2,128,256]{2,1,0:T(8,128)(2,1)S(1)}, bf16[2,128,256]{2,1,0:T(8,128)(2,1)S(1)}, u32[]{:S(2)}, u32[]{:S(2)}) collective-permute-start(bf16[2,128,256]{2,1,0:T(8,128)(2,1)S(1)} %get-tuple-element.39), channel_id=1, source_target_pairs={{0,16},{16,0},{1,17},{17,1},{2,18},{18,2},{3,19},{19,3},{4,20},{20... | collective-permute-start | bytes 393224 | tf_op jit(solution)/shard_map/ppermute | solution.py:424
  34.0 4.2 %collective-permute-start.14 = (bf16[256,512]{1,0:T(8,128)(2,1)S(1)}, bf16[256,512]{1,0:T(8,128)(2,1)S(1)}, u32[]{:S(2)}, u32[]{:S(2)}) collective-permute-start(bf16[256,512]{1,0:T(8,128)(2,1)S(1)} %collective-permute-done.10.refs_0_), channel_id=1, source_target_pairs={{0,1},{1,0},{2,3},{3,2},{4,5},{5,4},{6,7},{7,6},{8,9},{9,8},{10,11... | collective-permute-start | bytes 786440 | tf_op jit(solution)/shard_map/ppermute | solution.py:442
  34.0 4.2 %collective-permute-start.15 = (bf16[256,512]{1,0:T(8,128)(2,1)S(1)}, bf16[256,512]{1,0:T(8,128)(2,1)S(1)}, u32[]{:S(2)}, u32[]{:S(2)}) collective-permute-start(bf16[256,512]{1,0:T(8,128)(2,1)S(1)} %collective-permute-done.13.refs_1_), channel_id=1, source_target_pairs={{0,1},{1,0},{2,3},{3,2},{4,5},{5,4},{6,7},{7,6},{8,9},{9,8},{10,11... | collective-permute-start | bytes 786440 | tf_op jit(solution)/shard_map/ppermute | solution.py:442
  36.8 1.8 %collective-permute-start.21 = (bf16[256,512]{1,0:T(8,128)(2,1)S(1)}, bf16[256,512]{1,0:T(8,128)(2,1)S(1)}, u32[]{:S(2)}, u32[]{:S(2)}) collective-permute-start(bf16[256,512]{1,0:T(8,128)(2,1)S(1)} %collective-permute-done.16.refs_0_), channel_id=1, source_target_pairs={{0,1},{1,0},{2,3},{3,2},{4,5},{5,4},{6,7},{7,6},{8,9},{9,8},{10,11... | collective-permute-start | bytes 786440 | tf_op jit(solution)/shard_map/ppermute | solution.py:447
  38.1 5.1 %collective-permute-start.6 = (bf16[256,512]{1,0:T(8,128)(2,1)S(1)}, bf16[256,512]{1,0:T(8,128)(2,1)S(1)}, u32[]{:S(2)}, u32[]{:S(2)}) collective-permute-start(bf16[256,512]{1,0:T(8,128)(2,1)S(1)} %shard_map.84.refs_1_), channel_id=1, source_target_pairs={{0,1},{1,0},{2,3},{3,2},{4,5},{5,4},{6,7},{7,6},{8,9},{9,8},{10,11... | collective-permute-start | bytes 786440 | tf_op jit(solution)/shard_map/ppermute | solution.py:452
  38.9 5.9 %collective-permute-start.22 = (bf16[128,512]{1,0:T(8,128)(2,1)S(1)}, bf16[128,512]{1,0:T(8,128)(2,1)S(1)}, u32[]{:S(2)}, u32[]{:S(2)}) collective-permute-start(bf16[128,512]{1,0:T(8,128)(2,1)S(1)} %get-tuple-element.45), channel_id=1, source_target_pairs={{0,16},{16,0},{1,17},{17,1},{2,18},{18,2},{3,19},{19,3},{4,20},{20... | collective-permute-start | bytes 393224 | tf_op jit(solution)/shard_map/ppermute | solution.py:456

commit v6 on v5

--- a/solution.py
+++ b/solution.py
@@ -234,7 +234,7 @@
         a = own[rows, at].astype(jnp.float32)
         b = here[:, at].astype(jnp.float32)
         shared = peaks[k, rows, :] + jnp.max(jnp.abs(b), axis=1, keepdims=True) / 2
-        over = 1.0 / shared[:, :1]
+        over = 1.0 / shared
         low_a = jnp.clip(a * over, -1.0, 1.0).astype(jnp.bfloat16).astype(jnp.float32)
         low_b = jnp.clip(b * over, -1.0, 1.0).astype(jnp.bfloat16).astype(jnp.float32)
         weight[:, at] = (base[rows, at] + steep[rows, :] * shared * (low_a + low_b)).astype(weight.dtype)
@@ -392,8 +392,11 @@
 
 
 def close_kernel(own_part, mine_part, other_part, inverse, keys):
-    total = own_part[...] + mine_part[...] + other_part[...].astype(jnp.float32)
-    keys[...] = (total * inverse[...]).astype(keys.dtype)
+    scale = jnp.broadcast_to(inverse[...], (inverse.shape[0], BLOCK))
+    for col in range(0, keys.shape[1], BLOCK):
+        at = slice(col, col + BLOCK)
+        total = own_part[:, at] + mine_part[:, at] + other_part[:, at].astype(jnp.float32)
+        keys[:, at] = (total * scale).astype(keys.dtype)
 
 
 def close(own_part, mine_part, other_part, inverse):

time: 45.8 us -> 45.7 us (level)
  no operation moved by 1% of the time
where the time goes in v6:
time: 45.7 us; the launch traced here: 45.6 us
  starting transfers between devices  26.2 us (57%)
  waiting for transfers between devices  10.2 us (22%)
  Pallas kernels  7.06 us (15%)
  local copies, waits for them, and re-layouts  1.24 us (3%)
  between operations  0.85 us (2%)
    ppermute x3, starting transfers between devices, by_permutes(): a = ring(a)  6.25 us
    ppermute x3, starting transfers between devices, by_permutes(): b = ring(b)  6.22 us
    ppermute x2, starting transfers between devices, by_permutes(): other, more = (cross(sent), cross(more))  3.52 us
    ppermute x2, starting transfers between devices, by_permutes(): here_parts = [cross(part) for part in sent_parts]  3.11 us
    ppermute x3, waiting for transfers between devices, by_permutes(): a = ring(a)  3.07 us
    ppermute x3, waiting for transfers between devices, by_permutes(): b = ring(b)  2.86 us
    pallas_call x1, Pallas kernels, sync_outer(): pl.pallas_call(outer_kernel, in_specs=[VMEM] * 6, out_specs=[VMEM] * 2, o...  2.28 us
    ppermute x1, starting transfers between devices, by_permutes(): arrived = ring(head)  2.17 us
  transfers between devices with their start and end apart: 23, of which 10 were waited for; matrix products, arithmetic and copies ran while one was open for 0% of the time, Pallas kernels for 14%

profile of v6, /device:TPU:0, one launch (start us, length us, event | category | flops | bytes accessed | tf_op | source)
XLA Modules:
  0.0 45.6 jit_solution(13411968526191428351)
XLA Ops:
  0.6 1.2 %copy-done.2 = f32[1,512,512]{2,1,0:T(8,128)S(1)} copy-done((f32[1,512,512]{2,1,0:T(8,128)S(1)}, f32[1,512,512]{2,1,0:T(8,128)}, u32[]{:S(2)}) %copy-start.2) | copy-done | bytes 1048600
  1.9 3.0 %collective-permute-start.1 = (bf16[128,512]{1,0:T(8,128)(2,1)S(1)}, bf16[128,512]{1,0:T(8,128)(2,1)S(1)}, u32[]{:S(2)}, u32[]{:S(2)}) collective-permute-start(bf16[128,512]{1,0:T(8,128)(2,1)S(1)} %get-tuple-element.28.refs_0_), channel_id=1, source_target_pairs={{0,16},{16,0},{1,17},{17,1},{2,18},{18,2},{3,19},{19,3},{4,20},{20... | collective-permute-start | bytes 393224 | tf_op jit(solution)/shard_map/ppermute | solution.py:422
  5.1 0.7 %shard_map.77 = (bf16[14,128,256]{2,1,0:T(8,128)(2,1)S(1)}, bf16[16,128,256]{2,1,0:T(8,128)(2,1)S(1)}, bf16[2,128,256]{2,1,0:T(8,128)(2,1)S(1)}, bf16[4,128,256]{2,1,0:T(8,128)(2,1)S(1)}, f32[128,1]{1,0:T(8,128)S(1)}) custom-call(bf16[128,8192]{1,0:T(8,128)(2,1)S(1)} %copy-done.3, bf16[256,512]{1,0:T(8,128)(2,1)S(1)} %shard_map.76.grad.own.here_a), custom_call_target="tpu_custom_call" | custom-call | flops 2097152 | bytes 4194304 | tf_op jit(solution)/shard_map/pallas_call | solution.py:157
  5.8 2.0 %collective-permute-start.2 = (bf16[16,128,256]{2,1,0:T(8,128)(2,1)S(1)}, bf16[16,128,256]{2,1,0:T(8,128)(2,1)S(1)}, u32[]{:S(2)}, u32[]{:S(2)}) collective-permute-start(bf16[16,128,256]{2,1,0:T(8,128)(2,1)S(1)} %get-tuple-element.38), channel_id=1, source_target_pairs={{0,16},{16,0},{1,17},{17,1},{2,18},{18,2},{3,19},{19,3},{4,20},{20... | collective-permute-start | bytes 3145736 | tf_op jit(solution)/shard_map/ppermute | solution.py:427
  7.8 0.3 shard_map.79
  8.1 1.2 %collective-permute-done.1.here.refs_0_ = bf16[128,512]{1,0:T(8,128)(2,1)S(1)} collective-permute-done((bf16[128,512]{1,0:T(8,128)(2,1)S(1)}, bf16[128,512]{1,0:T(8,128)(2,1)S(1)}, u32[]{:S(2)}, u32[]{:S(2)}) %collective-permute-start.1) | collective-permute-done | bytes 131104 | tf_op jit(solution)/shard_map/ppermute | solution.py:422
  9.5 2.2 %collective-permute-start.7 = (bf16[128,512]{1,0:T(8,128)(2,1)S(1)}, bf16[128,512]{1,0:T(8,128)(2,1)S(1)}, u32[]{:S(2)}, u32[]{:S(2)}) collective-permute-start(bf16[128,512]{1,0:T(8,128)(2,1)S(1)} %shard_map.80.done), channel_id=1, source_target_pairs={{0,4},{1,3},{2,0},{3,7},{4,8},{5,1},{6,2},{7,11},{8,12},{9,5},{10,... | collective-permute-start | bytes 393224 | tf_op jit(solution)/shard_map/ppermute | solution.py:438
  11.7 0.4 collective-permute-done.here.refs_1_
  12.5 2.1 %collective-permute-start.8 = (bf16[128,512]{1,0:T(8,128)(2,1)S(1)}, bf16[128,512]{1,0:T(8,128)(2,1)S(1)}, u32[]{:S(2)}, u32[]{:S(2)}) collective-permute-start(bf16[128,512]{1,0:T(8,128)(2,1)S(1)} %get-tuple-element.40), channel_id=1, source_target_pairs={{0,4},{1,3},{2,0},{3,7},{4,8},{5,1},{6,2},{7,11},{8,12},{9,5},{10,... | collective-permute-start | bytes 393224 | tf_op jit(solution)/shard_map/ppermute | solution.py:441
  14.7 2.1 %collective-permute-start.11 = (bf16[256,512]{1,0:T(8,128)(2,1)S(1)}, bf16[256,512]{1,0:T(8,128)(2,1)S(1)}, u32[]{:S(2)}, u32[]{:S(2)}) collective-permute-start(bf16[256,512]{1,0:T(8,128)(2,1)S(1)} %shard_map.87.refs_2_), channel_id=1, source_target_pairs={{0,4},{1,3},{2,0},{3,7},{4,8},{5,1},{6,2},{7,11},{8,12},{9,5},{10,... | collective-permute-start | bytes 786440 | tf_op jit(solution)/shard_map/ppermute | solution.py:444
  16.8 0.7 %collective-permute-done.8.refs_1_ = bf16[128,512]{1,0:T(8,128)(2,1)S(1)} collective-permute-done((bf16[128,512]{1,0:T(8,128)(2,1)S(1)}, bf16[128,512]{1,0:T(8,128)(2,1)S(1)}, u32[]{:S(2)}, u32[]{:S(2)}) %collective-permute-start.8) | collective-permute-done | bytes 131104 | tf_op jit(solution)/shard_map/ppermute | solution.py:441
  17.5 2.1 %collective-permute-start.9 = (bf16[256,512]{1,0:T(8,128)(2,1)S(1)}, bf16[256,512]{1,0:T(8,128)(2,1)S(1)}, u32[]{:S(2)}, u32[]{:S(2)}) collective-permute-start(bf16[256,512]{1,0:T(8,128)(2,1)S(1)} %shard_map.91.refs_0_), channel_id=1, source_target_pairs={{0,4},{1,3},{2,0},{3,7},{4,8},{5,1},{6,2},{7,11},{8,12},{9,5},{10,... | collective-permute-start | bytes 786440 | tf_op jit(solution)/shard_map/ppermute | solution.py:443
  19.6 1.5 %collective-permute-done.11.refs_1_ = bf16[256,512]{1,0:T(8,128)(2,1)S(1)} collective-permute-done((bf16[256,512]{1,0:T(8,128)(2,1)S(1)}, bf16[256,512]{1,0:T(8,128)(2,1)S(1)}, u32[]{:S(2)}, u32[]{:S(2)}) %collective-permute-start.11) | collective-permute-done | bytes 262176 | tf_op jit(solution)/shard_map/ppermute | solution.py:444
  21.1 2.1 %collective-permute-start.12 = (bf16[256,512]{1,0:T(8,128)(2,1)S(1)}, bf16[256,512]{1,0:T(8,128)(2,1)S(1)}, u32[]{:S(2)}, u32[]{:S(2)}) collective-permute-start(bf16[256,512]{1,0:T(8,128)(2,1)S(1)} %collective-permute-done.11.refs_1_), channel_id=1, source_target_pairs={{0,4},{1,3},{2,0},{3,7},{4,8},{5,1},{6,2},{7,11},{8,12},{9,5},{10,... | collective-permute-start | bytes 786440 | tf_op jit(solution)/shard_map/ppermute | solution.py:444
  23.2 0.8 %collective-permute-done.9.refs_4_ = bf16[256,512]{1,0:T(8,128)(2,1)S(1)} collective-permute-done((bf16[256,512]{1,0:T(8,128)(2,1)S(1)}, bf16[256,512]{1,0:T(8,128)(2,1)S(1)}, u32[]{:S(2)}, u32[]{:S(2)}) %collective-permute-start.9) | collective-permute-done | bytes 262176 | tf_op jit(solution)/shard_map/ppermute | solution.py:443
  24.0 2.1 %collective-permute-start.10 = (bf16[256,512]{1,0:T(8,128)(2,1)S(1)}, bf16[256,512]{1,0:T(8,128)(2,1)S(1)}, u32[]{:S(2)}, u32[]{:S(2)}) collective-permute-start(bf16[256,512]{1,0:T(8,128)(2,1)S(1)} %collective-permute-done.9.refs_4_), channel_id=1, source_target_pairs={{0,4},{1,3},{2,0},{3,7},{4,8},{5,1},{6,2},{7,11},{8,12},{9,5},{10,... | collective-permute-start | bytes 786440 | tf_op jit(solution)/shard_map/ppermute | solution.py:443
  26.2 1.4 %collective-permute-done.12.refs_5_ = bf16[256,512]{1,0:T(8,128)(2,1)S(1)} collective-permute-done((bf16[256,512]{1,0:T(8,128)(2,1)S(1)}, bf16[256,512]{1,0:T(8,128)(2,1)S(1)}, u32[]{:S(2)}, u32[]{:S(2)}) %collective-permute-start.12) | collective-permute-done | bytes 262176 | tf_op jit(solution)/shard_map/ppermute | solution.py:444
  27.5 2.1 %collective-permute-start.13 = (bf16[256,512]{1,0:T(8,128)(2,1)S(1)}, bf16[256,512]{1,0:T(8,128)(2,1)S(1)}, u32[]{:S(2)}, u32[]{:S(2)}) collective-permute-start(bf16[256,512]{1,0:T(8,128)(2,1)S(1)} %collective-permute-done.12.refs_5_), channel_id=1, source_target_pairs={{0,4},{1,3},{2,0},{3,7},{4,8},{5,1},{6,2},{7,11},{8,12},{9,5},{10,... | collective-permute-start | bytes 786440 | tf_op jit(solution)/shard_map/ppermute | solution.py:444
  29.6 0.7 %collective-permute-done.10.refs_0_ = bf16[256,512]{1,0:T(8,128)(2,1)S(1)} collective-permute-done((bf16[256,512]{1,0:T(8,128)(2,1)S(1)}, bf16[256,512]{1,0:T(8,128)(2,1)S(1)}, u32[]{:S(2)}, u32[]{:S(2)}) %collective-permute-start.10) | collective-permute-done | bytes 262176 | tf_op jit(solution)/shard_map/ppermute | solution.py:443
  30.3 2.1 %collective-permute-start.16 = (bf16[256,512]{1,0:T(8,128)(2,1)S(1)}, bf16[256,512]{1,0:T(8,128)(2,1)S(1)}, u32[]{:S(2)}, u32[]{:S(2)}) collective-permute-start(bf16[256,512]{1,0:T(8,128)(2,1)S(1)} %collective-permute-done.10.refs_0_), channel_id=1, source_target_pairs={{0,4},{1,3},{2,0},{3,7},{4,8},{5,1},{6,2},{7,11},{8,12},{9,5},{10,... | collective-permute-start | bytes 786440 | tf_op jit(solution)/shard_map/ppermute | solution.py:446
  32.4 1.5 %collective-permute-start.3 = (bf16[2,128,256]{2,1,0:T(8,128)(2,1)S(1)}, bf16[2,128,256]{2,1,0:T(8,128)(2,1)S(1)}, u32[]{:S(2)}, u32[]{:S(2)}) collective-permute-start(bf16[2,128,256]{2,1,0:T(8,128)(2,1)S(1)} %get-tuple-element.39), channel_id=1, source_target_pairs={{0,16},{16,0},{1,17},{17,1},{2,18},{18,2},{3,19},{19,3},{4,20},{20... | collective-permute-start | bytes 393224 | tf_op jit(solution)/shard_map/ppermute | solution.py:427
  33.9 0.5 %collective-permute-start.15 = (bf16[256,512]{1,0:T(8,128)(2,1)S(1)}, bf16[256,512]{1,0:T(8,128)(2,1)S(1)}, u32[]{:S(2)}, u32[]{:S(2)}) collective-permute-start(bf16[256,512]{1,0:T(8,128)(2,1)S(1)} %collective-permute-done.13.refs_1_), channel_id=1, source_target_pairs={{0,1},{1,0},{2,3},{3,2},{4,5},{5,4},{6,7},{7,6},{8,9},{9,8},{10,11... | collective-permute-start | bytes 786440 | tf_op jit(solution)/shard_map/ppermute | solution.py:445
  34.4 0.7 %shard_map.92.refs_4_ = f32[256,512]{1,0:T(8,128)S(1)} custom-call(bf16[14,128,256]{2,1,0:T(8,128)(2,1)S(1)} %get-tuple-element.41.own, bf16[16,128,256]{2,1,0:T(8,128)(2,1)S(1)} %collective-permute-done.2.packed.other, bf16[256,512]{1,0:T(8,128)(2,1)S(1)} %shard_map.91.refs_0_, bf16[256,512]{1,0:T(8,128)(2,1)S(1)} %collective-permute-done.11.refs_1_, ...), custom_call_target="tpu_custom_call" | custom-call | flops 536870912 | bytes 3145728 | tf_op jit(solution)/shard_map/pallas_call | solution.py:361
  35.1 1.6 %collective-permute-done.16.refs_0_ = bf16[256,512]{1,0:T(8,128)(2,1)S(1)} collective-permute-done((bf16[256,512]{1,0:T(8,128)(2,1)S(1)}, bf16[256,512]{1,0:T(8,128)(2,1)S(1)}, u32[]{:S(2)}, u32[]{:S(2)}) %collective-permute-start.16) | collective-permute-done | bytes 262176 | tf_op jit(solution)/shard_map/ppermute | solution.py:446
  36.7 0.6 %collective-permute-done.3.more = bf16[2,128,256]{2,1,0:T(8,128)(2,1)S(1)} collective-permute-done((bf16[2,128,256]{2,1,0:T(8,128)(2,1)S(1)}, bf16[2,128,256]{2,1,0:T(8,128)(2,1)S(1)}, u32[]{:S(2)}, u32[]{:S(2)}) %collective-permute-start.3) | collective-permute-done | bytes 131104 | tf_op jit(solution)/shard_map/ppermute | solution.py:427
  37.4 0.6 %shard_map.84.refs_1_ = bf16[256,512]{1,0:T(8,128)(2,1)S(1)} custom-call(bf16[256,512]{1,0:T(8,128)(2,1)S(1)} %shard_map.82.first.there_a, bf16[256,512]{1,0:T(8,128)(2,1)S(1)} %shard_map.83.second.there_b, f32[512,512]{1,0:T(8,128)S(1)} %copy-done, f32[512,512]{1,0:T(8,128)S(1)} %copy-done.1, f32[64,128]{1,0:T(8,128)S(1)} %bitcast.5), custom_call_target="tpu_custom_call" | custom-call | flops 3932160 | bytes 1835008 | tf_op jit(solution)/shard_map/pallas_call | solution.py:285
  38.1 0.4 shard_map.93.early
  38.6 0.3 shard_map.94
  38.9 1.9 %collective-permute-start.22 = (bf16[128,512]{1,0:T(8,128)(2,1)S(1)}, bf16[128,512]{1,0:T(8,128)(2,1)S(1)}, u32[]{:S(2)}, u32[]{:S(2)}) collective-permute-start(bf16[128,512]{1,0:T(8,128)(2,1)S(1)} %get-tuple-element.45), channel_id=1, source_target_pairs={{0,16},{16,0},{1,17},{17,1},{2,18},{18,2},{3,19},{19,3},{4,20},{20... | collective-permute-start | bytes 393224 | tf_op jit(solution)/shard_map/ppermute | solution.py:459
  40.8 2.3 %shard_map.97 = (f32[512,512]{1,0:T(8,128)}, f32[512,512]{1,0:T(8,128)}) custom-call(bf16[256,512]{1,0:T(8,128)(2,1)S(1)} %shard_map.76.grad.own.here_a, bf16[256,512]{1,0:T(8,128)(2,1)S(1)} %shard_map.96.here_b, bf16[256,512]{1,0:T(8,128)(2,1)S(1)} %shard_map.82.first.there_a, bf16[256,512]{1,0:T(8,128)(2,1)S(1)} %shard_map.83.second.there_b, ...), custom_call_target="tpu_custom_call" | custom-call | flops 7864320 | bytes 5242880 | tf_op jit(solution)/shard_map/pallas_call | solution.py:314
  43.4 1.4 %collective-permute-done.22.other_part = bf16[128,512]{1,0:T(8,128)(2,1)S(1)} collective-permute-done((bf16[128,512]{1,0:T(8,128)(2,1)S(1)}, bf16[128,512]{1,0:T(8,128)(2,1)S(1)}, u32[]{:S(2)}, u32[]{:S(2)}) %collective-permute-start.22) | collective-permute-done | bytes 131104 | tf_op jit(solution)/shard_map/ppermute | solution.py:459
  44.8 0.7 %shard_map.95 = bf16[128,512]{1,0:T(8,128)(2,1)} custom-call(f32[128,512]{1,0:T(8,128)S(1)} %shard_map.88.own_part, f32[128,512]{1,0:T(8,128)S(1)} %get-tuple-element.44.mine_part, bf16[128,512]{1,0:T(8,128)(2,1)S(1)} %collective-permute-done.22.other_part, f32[128,1]{1,0:T(8,128)S(1)} %get-tuple-element.46.inverse), custom_call_target="tpu_custom_call" | custom-call | tf_op jit(solution)/shard_map/pallas_call | solution.py:403
  (46 shorter events, 1.5 us)
Async XLA Ops:
  0.6 1.2 %copy-start.2 = (f32[1,512,512]{2,1,0:T(8,128)S(1)}, f32[1,512,512]{2,1,0:T(8,128)}, u32[]{:S(2)}) copy-start(f32[1,512,512]{2,1,0:T(8,128)} %param.9) | copy-start | bytes 3145732
  1.9 3.2 %copy-start.3 = (bf16[128,8192]{1,0:T(8,128)(2,1)S(1)}, bf16[128,8192]{1,0:T(8,128)(2,1)}, u32[]{:S(2)}) copy-start(bf16[128,8192]{1,0:T(8,128)(2,1)} %tokens.1) | copy-start | bytes 6291460
  1.9 5.9 %copy-start = (f32[512,512]{1,0:T(8,128)S(1)}, f32[512,512]{1,0:T(8,128)}, u32[]{:S(2)}) copy-start(f32[512,512]{1,0:T(8,128)} %master.5) | copy-start | bytes 3145732
  1.9 5.9 %copy-start.1 = (f32[512,512]{1,0:T(8,128)S(1)}, f32[512,512]{1,0:T(8,128)}, u32[]{:S(2)}) copy-start(f32[512,512]{1,0:T(8,128)} %momentum.5) | copy-start | bytes 3145732
  1.9 5.9 %copy-start.4 = (f32[8192]{0:T(1024)S(1)}, f32[8192]{0:T(1024)}, u32[]{:S(2)}) copy-start(f32[8192]{0:T(1024)} %param.6) | copy-start | bytes 98308
  1.9 7.4 %collective-permute-start.1 = (bf16[128,512]{1,0:T(8,128)(2,1)S(1)}, bf16[128,512]{1,0:T(8,128)(2,1)S(1)}, u32[]{:S(2)}, u32[]{:S(2)}) collective-permute-start(bf16[128,512]{1,0:T(8,128)(2,1)S(1)} %get-tuple-element.28.refs_0_), channel_id=1, source_target_pairs={{0,16},{16,0},{1,17},{17,1},{2,18},{18,2},{3,19},{19,3},{4,20},{20... | collective-permute-start | bytes 393224 | tf_op jit(solution)/shard_map/ppermute | solution.py:422
  5.0 7.1 %collective-permute-start = (bf16[128,512]{1,0:T(8,128)(2,1)S(1)}, bf16[128,512]{1,0:T(8,128)(2,1)S(1)}, u32[]{:S(2)}, u32[]{:S(2)}) collective-permute-start(bf16[128,512]{1,0:T(8,128)(2,1)S(1)} %get-tuple-element.27.refs_1_), channel_id=1, source_target_pairs={{0,16},{16,0},{1,17},{17,1},{2,18},{18,2},{3,19},{19,3},{4,20},{20... | collective-permute-start | bytes 393224 | tf_op jit(solution)/shard_map/ppermute | solution.py:422
  5.8 28.6 %collective-permute-start.2 = (bf16[16,128,256]{2,1,0:T(8,128)(2,1)S(1)}, bf16[16,128,256]{2,1,0:T(8,128)(2,1)S(1)}, u32[]{:S(2)}, u32[]{:S(2)}) collective-permute-start(bf16[16,128,256]{2,1,0:T(8,128)(2,1)S(1)} %get-tuple-element.38), channel_id=1, source_target_pairs={{0,16},{16,0},{1,17},{17,1},{2,18},{18,2},{3,19},{19,3},{4,20},{20... | collective-permute-start | bytes 3145736 | tf_op jit(solution)/shard_map/ppermute | solution.py:427
  9.5 5.1 %collective-permute-start.7 = (bf16[128,512]{1,0:T(8,128)(2,1)S(1)}, bf16[128,512]{1,0:T(8,128)(2,1)S(1)}, u32[]{:S(2)}, u32[]{:S(2)}) collective-permute-start(bf16[128,512]{1,0:T(8,128)(2,1)S(1)} %shard_map.80.done), channel_id=1, source_target_pairs={{0,4},{1,3},{2,0},{3,7},{4,8},{5,1},{6,2},{7,11},{8,12},{9,5},{10,... | collective-permute-start | bytes 393224 | tf_op jit(solution)/shard_map/ppermute | solution.py:438
  11.7 2.9 %collective-permute-start.4 = (bf16[128,512]{1,0:T(8,128)(2,1)S(1)}, bf16[128,512]{1,0:T(8,128)(2,1)S(1)}, u32[]{:S(2)}, u32[]{:S(2)}) collective-permute-start(bf16[128,512]{1,0:T(8,128)(2,1)S(1)} %shard_map.80.done), channel_id=1, source_target_pairs={{0,1},{1,0},{2,3},{3,2},{4,5},{5,4},{6,7},{7,6},{8,9},{9,8},{10,11... | collective-permute-start | bytes 393224 | tf_op jit(solution)/shard_map/ppermute | solution.py:431
  12.3 2.3 %collective-permute-start.5 = (bf16[128,512]{1,0:T(8,128)(2,1)S(1)}, bf16[128,512]{1,0:T(8,128)(2,1)S(1)}, u32[]{:S(2)}, u32[]{:S(2)}) collective-permute-start(bf16[128,512]{1,0:T(8,128)(2,1)S(1)} %get-tuple-element.40), channel_id=1, source_target_pairs={{0,1},{1,0},{2,3},{3,2},{4,5},{5,4},{6,7},{7,6},{8,9},{9,8},{10,11... | collective-permute-start | bytes 393224 | tf_op jit(solution)/shard_map/ppermute | solution.py:434
  12.5 5.0 %collective-permute-start.8 = (bf16[128,512]{1,0:T(8,128)(2,1)S(1)}, bf16[128,512]{1,0:T(8,128)(2,1)S(1)}, u32[]{:S(2)}, u32[]{:S(2)}) collective-permute-start(bf16[128,512]{1,0:T(8,128)(2,1)S(1)} %get-tuple-element.40), channel_id=1, source_target_pairs={{0,4},{1,3},{2,0},{3,7},{4,8},{5,1},{6,2},{7,11},{8,12},{9,5},{10,... | collective-permute-start | bytes 393224 | tf_op jit(solution)/shard_map/ppermute | solution.py:441
  14.7 6.4 %collective-permute-start.11 = (bf16[256,512]{1,0:T(8,128)(2,1)S(1)}, bf16[256,512]{1,0:T(8,128)(2,1)S(1)}, u32[]{:S(2)}, u32[]{:S(2)}) collective-permute-start(bf16[256,512]{1,0:T(8,128)(2,1)S(1)} %shard_map.87.refs_2_), channel_id=1, source_target_pairs={{0,4},{1,3},{2,0},{3,7},{4,8},{5,1},{6,2},{7,11},{8,12},{9,5},{10,... | collective-permute-start | bytes 786440 | tf_op jit(solution)/shard_map/ppermute | solution.py:444
  17.5 6.4 %collective-permute-start.9 = (bf16[256,512]{1,0:T(8,128)(2,1)S(1)}, bf16[256,512]{1,0:T(8,128)(2,1)S(1)}, u32[]{:S(2)}, u32[]{:S(2)}) collective-permute-start(bf16[256,512]{1,0:T(8,128)(2,1)S(1)} %shard_map.91.refs_0_), channel_id=1, source_target_pairs={{0,4},{1,3},{2,0},{3,7},{4,8},{5,1},{6,2},{7,11},{8,12},{9,5},{10,... | collective-permute-start | bytes 786440 | tf_op jit(solution)/shard_map/ppermute | solution.py:443
  19.6 6.4 %collective-permute-start.17 = (bf16[256,512]{1,0:T(8,128)(2,1)S(1)}, bf16[256,512]{1,0:T(8,128)(2,1)S(1)}, u32[]{:S(2)}, u32[]{:S(2)}) collective-permute-start(bf16[256,512]{1,0:T(8,128)(2,1)S(1)} %shard_map.91.refs_0_), channel_id=1, source_target_pairs={{0,1},{1,0},{2,3},{3,2},{4,5},{5,4},{6,7},{7,6},{8,9},{9,8},{10,11... | collective-permute-start | bytes 786440 | tf_op jit(solution)/shard_map/ppermute | solution.py:445
  21.1 6.4 %collective-permute-start.12 = (bf16[256,512]{1,0:T(8,128)(2,1)S(1)}, bf16[256,512]{1,0:T(8,128)(2,1)S(1)}, u32[]{:S(2)}, u32[]{:S(2)}) collective-permute-start(bf16[256,512]{1,0:T(8,128)(2,1)S(1)} %collective-permute-done.11.refs_1_), channel_id=1, source_target_pairs={{0,4},{1,3},{2,0},{3,7},{4,8},{5,1},{6,2},{7,11},{8,12},{9,5},{10,... | collective-permute-start | bytes 786440 | tf_op jit(solution)/shard_map/ppermute | solution.py:444
  23.9 3.6 %collective-permute-start.19 = (bf16[256,512]{1,0:T(8,128)(2,1)S(1)}, bf16[256,512]{1,0:T(8,128)(2,1)S(1)}, u32[]{:S(2)}, u32[]{:S(2)}) collective-permute-start(bf16[256,512]{1,0:T(8,128)(2,1)S(1)} %collective-permute-done.9.refs_4_), channel_id=1, source_target_pairs={{0,1},{1,0},{2,3},{3,2},{4,5},{5,4},{6,7},{7,6},{8,9},{9,8},{10,11... | collective-permute-start | bytes 786440 | tf_op jit(solution)/shard_map/ppermute | solution.py:445
  24.0 6.4 %collective-permute-start.10 = (bf16[256,512]{1,0:T(8,128)(2,1)S(1)}, bf16[256,512]{1,0:T(8,128)(2,1)S(1)}, u32[]{:S(2)}, u32[]{:S(2)}) collective-permute-start(bf16[256,512]{1,0:T(8,128)(2,1)S(1)} %collective-permute-done.9.refs_4_), channel_id=1, source_target_pairs={{0,4},{1,3},{2,0},{3,7},{4,8},{5,1},{6,2},{7,11},{8,12},{9,5},{10,... | collective-permute-start | bytes 786440 | tf_op jit(solution)/shard_map/ppermute | solution.py:443
  26.0 6.4 %collective-permute-start.18 = (bf16[256,512]{1,0:T(8,128)(2,1)S(1)}, bf16[256,512]{1,0:T(8,128)(2,1)S(1)}, u32[]{:S(2)}, u32[]{:S(2)}) collective-permute-start(bf16[256,512]{1,0:T(8,128)(2,1)S(1)} %collective-permute-done.11.refs_1_), channel_id=1, source_target_pairs={{0,1},{1,0},{2,3},{3,2},{4,5},{5,4},{6,7},{7,6},{8,9},{9,8},{10,11... | collective-permute-start | bytes 786440 | tf_op jit(solution)/shard_map/ppermute | solution.py:445
  27.5 6.4 %collective-permute-start.20 = (bf16[256,512]{1,0:T(8,128)(2,1)S(1)}, bf16[256,512]{1,0:T(8,128)(2,1)S(1)}, u32[]{:S(2)}, u32[]{:S(2)}) collective-permute-start(bf16[256,512]{1,0:T(8,128)(2,1)S(1)} %collective-permute-done.12.refs_5_), channel_id=1, source_target_pairs={{0,1},{1,0},{2,3},{3,2},{4,5},{5,4},{6,7},{7,6},{8,9},{9,8},{10,11... | collective-permute-start | bytes 786440 | tf_op jit(solution)/shard_map/ppermute | solution.py:445
  27.5 6.4 %collective-permute-start.13 = (bf16[256,512]{1,0:T(8,128)(2,1)S(1)}, bf16[256,512]{1,0:T(8,128)(2,1)S(1)}, u32[]{:S(2)}, u32[]{:S(2)}) collective-permute-start(bf16[256,512]{1,0:T(8,128)(2,1)S(1)} %collective-permute-done.12.refs_5_), channel_id=1, source_target_pairs={{0,4},{1,3},{2,0},{3,7},{4,8},{5,1},{6,2},{7,11},{8,12},{9,5},{10,... | collective-permute-start | bytes 786440 | tf_op jit(solution)/shard_map/ppermute | solution.py:444
  30.3 6.4 %collective-permute-start.16 = (bf16[256,512]{1,0:T(8,128)(2,1)S(1)}, bf16[256,512]{1,0:T(8,128)(2,1)S(1)}, u32[]{:S(2)}, u32[]{:S(2)}) collective-permute-start(bf16[256,512]{1,0:T(8,128)(2,1)S(1)} %collective-permute-done.10.refs_0_), channel_id=1, source_target_pairs={{0,4},{1,3},{2,0},{3,7},{4,8},{5,1},{6,2},{7,11},{8,12},{9,5},{10,... | collective-permute-start | bytes 786440 | tf_op jit(solution)/shard_map/ppermute | solution.py:446
  32.4 5.0 %collective-permute-start.3 = (bf16[2,128,256]{2,1,0:T(8,128)(2,1)S(1)}, bf16[2,128,256]{2,1,0:T(8,128)(2,1)S(1)}, u32[]{:S(2)}, u32[]{:S(2)}) collective-permute-start(bf16[2,128,256]{2,1,0:T(8,128)(2,1)S(1)} %get-tuple-element.39), channel_id=1, source_target_pairs={{0,16},{16,0},{1,17},{17,1},{2,18},{18,2},{3,19},{19,3},{4,20},{20... | collective-permute-start | bytes 393224 | tf_op jit(solution)/shard_map/ppermute | solution.py:427
  33.9 4.2 %collective-permute-start.14 = (bf16[256,512]{1,0:T(8,128)(2,1)S(1)}, bf16[256,512]{1,0:T(8,128)(2,1)S(1)}, u32[]{:S(2)}, u32[]{:S(2)}) collective-permute-start(bf16[256,512]{1,0:T(8,128)(2,1)S(1)} %collective-permute-done.10.refs_0_), channel_id=1, source_target_pairs={{0,1},{1,0},{2,3},{3,2},{4,5},{5,4},{6,7},{7,6},{8,9},{9,8},{10,11... | collective-permute-start | bytes 786440 | tf_op jit(solution)/shard_map/ppermute | solution.py:445
  33.9 4.2 %collective-permute-start.15 = (bf16[256,512]{1,0:T(8,128)(2,1)S(1)}, bf16[256,512]{1,0:T(8,128)(2,1)S(1)}, u32[]{:S(2)}, u32[]{:S(2)}) collective-permute-start(bf16[256,512]{1,0:T(8,128)(2,1)S(1)} %collective-permute-done.13.refs_1_), channel_id=1, source_target_pairs={{0,1},{1,0},{2,3},{3,2},{4,5},{5,4},{6,7},{7,6},{8,9},{9,8},{10,11... | collective-permute-start | bytes 786440 | tf_op jit(solution)/shard_map/ppermute | solution.py:445
  36.7 1.9 %collective-permute-start.21 = (bf16[256,512]{1,0:T(8,128)(2,1)S(1)}, bf16[256,512]{1,0:T(8,128)(2,1)S(1)}, u32[]{:S(2)}, u32[]{:S(2)}) collective-permute-start(bf16[256,512]{1,0:T(8,128)(2,1)S(1)} %collective-permute-done.16.refs_0_), channel_id=1, source_target_pairs={{0,1},{1,0},{2,3},{3,2},{4,5},{5,4},{6,7},{7,6},{8,9},{9,8},{10,11... | collective-permute-start | bytes 786440 | tf_op jit(solution)/shard_map/ppermute | solution.py:450
  38.0 5.1 %collective-permute-start.6 = (bf16[256,512]{1,0:T(8,128)(2,1)S(1)}, bf16[256,512]{1,0:T(8,128)(2,1)S(1)}, u32[]{:S(2)}, u32[]{:S(2)}) collective-permute-start(bf16[256,512]{1,0:T(8,128)(2,1)S(1)} %shard_map.84.refs_1_), channel_id=1, source_target_pairs={{0,1},{1,0},{2,3},{3,2},{4,5},{5,4},{6,7},{7,6},{8,9},{9,8},{10,11... | collective-permute-start | bytes 786440 | tf_op jit(solution)/shard_map/ppermute | solution.py:455
  38.9 5.9 %collective-permute-start.22 = (bf16[128,512]{1,0:T(8,128)(2,1)S(1)}, bf16[128,512]{1,0:T(8,128)(2,1)S(1)}, u32[]{:S(2)}, u32[]{:S(2)}) collective-permute-start(bf16[128,512]{1,0:T(8,128)(2,1)S(1)} %get-tuple-element.45), channel_id=1, source_target_pairs={{0,16},{16,0},{1,17},{17,1},{2,18},{18,2},{3,19},{19,3},{4,20},{20... | collective-permute-start | bytes 393224 | tf_op jit(solution)/shard_map/ppermute | solution.py:459

commit v7 on v6

--- a/solution.py
+++ b/solution.py
@@ -275,8 +275,8 @@
         for col in range(0, cols, BLOCK):
             at = slice(col, col + BLOCK)
             outer_grad = synced(first[rows, at], second[rows, at])
-            moved = outer_mu * momentum[held, at] + outer_grad
-            fresh = master[held, at] - outer_rate * (outer_grad + outer_mu * moved)
+            still = master[held, at] - (outer_rate * outer_mu * outer_mu) * momentum[held, at]
+            fresh = still - (outer_rate * (1 + outer_mu)) * outer_grad
             weight[rows, at] = (gains * fresh).astype(weight.dtype)
 
 

time: 45.7 us -> 45.7 us (level)
  no operation moved by 1% of the time
where the time goes in v7:
time: 45.7 us; the launch traced here: 45.5 us
  starting transfers between devices  26.2 us (57%)
  waiting for transfers between devices  10.2 us (22%)
  Pallas kernels  7.02 us (15%)
  local copies, waits for them, and re-layouts  1.24 us (3%)
  between operations  0.85 us (2%)
    ppermute x3, starting transfers between devices, by_permutes(): a = ring(a)  6.25 us
    ppermute x3, starting transfers between devices, by_permutes(): b = ring(b)  6.22 us
    ppermute x2, starting transfers between devices, by_permutes(): other, more = (cross(sent), cross(more))  3.52 us
    ppermute x2, starting transfers between devices, by_permutes(): here_parts = [cross(part) for part in sent_parts]  3.11 us
    ppermute x3, waiting for transfers between devices, by_permutes(): a = ring(a)  3.07 us
    ppermute x3, waiting for transfers between devices, by_permutes(): b = ring(b)  2.86 us
    pallas_call x1, Pallas kernels, sync_outer(): pl.pallas_call(outer_kernel, in_specs=[VMEM] * 6, out_specs=[VMEM] * 2, o...  2.28 us
    ppermute x1, starting transfers between devices, by_permutes(): arrived = ring(head)  2.17 us
  transfers between devices with their start and end apart: 23, of which 10 were waited for; matrix products, arithmetic and copies ran while one was open for 0% of the time, Pallas kernels for 14%

profile of v7, /device:TPU:0, one launch (start us, length us, event | category | flops | bytes accessed | tf_op | source)
XLA Modules:
  0.0 45.5 jit_solution(1625361207248017149)
XLA Ops:
  0.6 1.2 %copy-done.2 = f32[1,512,512]{2,1,0:T(8,128)S(1)} copy-done((f32[1,512,512]{2,1,0:T(8,128)S(1)}, f32[1,512,512]{2,1,0:T(8,128)}, u32[]{:S(2)}) %copy-start.2) | copy-done | bytes 1048600
  1.9 3.0 %collective-permute-start.1 = (bf16[128,512]{1,0:T(8,128)(2,1)S(1)}, bf16[128,512]{1,0:T(8,128)(2,1)S(1)}, u32[]{:S(2)}, u32[]{:S(2)}) collective-permute-start(bf16[128,512]{1,0:T(8,128)(2,1)S(1)} %get-tuple-element.28.refs_0_), channel_id=1, source_target_pairs={{0,16},{16,0},{1,17},{17,1},{2,18},{18,2},{3,19},{19,3},{4,20},{20... | collective-permute-start | bytes 393224 | tf_op jit(solution)/shard_map/ppermute | solution.py:422
  5.1 0.7 %shard_map.77 = (bf16[14,128,256]{2,1,0:T(8,128)(2,1)S(1)}, bf16[16,128,256]{2,1,0:T(8,128)(2,1)S(1)}, bf16[2,128,256]{2,1,0:T(8,128)(2,1)S(1)}, bf16[4,128,256]{2,1,0:T(8,128)(2,1)S(1)}, f32[128,1]{1,0:T(8,128)S(1)}) custom-call(bf16[128,8192]{1,0:T(8,128)(2,1)S(1)} %copy-done.3, bf16[256,512]{1,0:T(8,128)(2,1)S(1)} %shard_map.76.grad.own.here_a), custom_call_target="tpu_custom_call" | custom-call | flops 2097152 | bytes 4194304 | tf_op jit(solution)/shard_map/pallas_call | solution.py:157
  5.8 2.0 %collective-permute-start.2 = (bf16[16,128,256]{2,1,0:T(8,128)(2,1)S(1)}, bf16[16,128,256]{2,1,0:T(8,128)(2,1)S(1)}, u32[]{:S(2)}, u32[]{:S(2)}) collective-permute-start(bf16[16,128,256]{2,1,0:T(8,128)(2,1)S(1)} %get-tuple-element.38), channel_id=1, source_target_pairs={{0,16},{16,0},{1,17},{17,1},{2,18},{18,2},{3,19},{19,3},{4,20},{20... | collective-permute-start | bytes 3145736 | tf_op jit(solution)/shard_map/ppermute | solution.py:427
  7.8 0.3 shard_map.79
  8.1 1.2 %collective-permute-done.1.here.refs_0_ = bf16[128,512]{1,0:T(8,128)(2,1)S(1)} collective-permute-done((bf16[128,512]{1,0:T(8,128)(2,1)S(1)}, bf16[128,512]{1,0:T(8,128)(2,1)S(1)}, u32[]{:S(2)}, u32[]{:S(2)}) %collective-permute-start.1) | collective-permute-done | bytes 131104 | tf_op jit(solution)/shard_map/ppermute | solution.py:422
  9.5 2.2 %collective-permute-start.7 = (bf16[128,512]{1,0:T(8,128)(2,1)S(1)}, bf16[128,512]{1,0:T(8,128)(2,1)S(1)}, u32[]{:S(2)}, u32[]{:S(2)}) collective-permute-start(bf16[128,512]{1,0:T(8,128)(2,1)S(1)} %shard_map.80.done), channel_id=1, source_target_pairs={{0,4},{1,3},{2,0},{3,7},{4,8},{5,1},{6,2},{7,11},{8,12},{9,5},{10,... | collective-permute-start | bytes 393224 | tf_op jit(solution)/shard_map/ppermute | solution.py:438
  11.7 0.4 collective-permute-done.here.refs_1_
  12.5 2.1 %collective-permute-start.8 = (bf16[128,512]{1,0:T(8,128)(2,1)S(1)}, bf16[128,512]{1,0:T(8,128)(2,1)S(1)}, u32[]{:S(2)}, u32[]{:S(2)}) collective-permute-start(bf16[128,512]{1,0:T(8,128)(2,1)S(1)} %get-tuple-element.40), channel_id=1, source_target_pairs={{0,4},{1,3},{2,0},{3,7},{4,8},{5,1},{6,2},{7,11},{8,12},{9,5},{10,... | collective-permute-start | bytes 393224 | tf_op jit(solution)/shard_map/ppermute | solution.py:441
  14.7 2.1 %collective-permute-start.11 = (bf16[256,512]{1,0:T(8,128)(2,1)S(1)}, bf16[256,512]{1,0:T(8,128)(2,1)S(1)}, u32[]{:S(2)}, u32[]{:S(2)}) collective-permute-start(bf16[256,512]{1,0:T(8,128)(2,1)S(1)} %shard_map.87.refs_2_), channel_id=1, source_target_pairs={{0,4},{1,3},{2,0},{3,7},{4,8},{5,1},{6,2},{7,11},{8,12},{9,5},{10,... | collective-permute-start | bytes 786440 | tf_op jit(solution)/shard_map/ppermute | solution.py:444
  16.8 0.7 %collective-permute-done.8.refs_1_ = bf16[128,512]{1,0:T(8,128)(2,1)S(1)} collective-permute-done((bf16[128,512]{1,0:T(8,128)(2,1)S(1)}, bf16[128,512]{1,0:T(8,128)(2,1)S(1)}, u32[]{:S(2)}, u32[]{:S(2)}) %collective-permute-start.8) | collective-permute-done | bytes 131104 | tf_op jit(solution)/shard_map/ppermute | solution.py:441
  17.5 2.1 %collective-permute-start.9 = (bf16[256,512]{1,0:T(8,128)(2,1)S(1)}, bf16[256,512]{1,0:T(8,128)(2,1)S(1)}, u32[]{:S(2)}, u32[]{:S(2)}) collective-permute-start(bf16[256,512]{1,0:T(8,128)(2,1)S(1)} %shard_map.91.refs_0_), channel_id=1, source_target_pairs={{0,4},{1,3},{2,0},{3,7},{4,8},{5,1},{6,2},{7,11},{8,12},{9,5},{10,... | collective-permute-start | bytes 786440 | tf_op jit(solution)/shard_map/ppermute | solution.py:443
  19.6 1.5 %collective-permute-done.11.refs_1_ = bf16[256,512]{1,0:T(8,128)(2,1)S(1)} collective-permute-done((bf16[256,512]{1,0:T(8,128)(2,1)S(1)}, bf16[256,512]{1,0:T(8,128)(2,1)S(1)}, u32[]{:S(2)}, u32[]{:S(2)}) %collective-permute-start.11) | collective-permute-done | bytes 262176 | tf_op jit(solution)/shard_map/ppermute | solution.py:444
  21.1 2.1 %collective-permute-start.12 = (bf16[256,512]{1,0:T(8,128)(2,1)S(1)}, bf16[256,512]{1,0:T(8,128)(2,1)S(1)}, u32[]{:S(2)}, u32[]{:S(2)}) collective-permute-start(bf16[256,512]{1,0:T(8,128)(2,1)S(1)} %collective-permute-done.11.refs_1_), channel_id=1, source_target_pairs={{0,4},{1,3},{2,0},{3,7},{4,8},{5,1},{6,2},{7,11},{8,12},{9,5},{10,... | collective-permute-start | bytes 786440 | tf_op jit(solution)/shard_map/ppermute | solution.py:444
  23.2 0.8 %collective-permute-done.9.refs_4_ = bf16[256,512]{1,0:T(8,128)(2,1)S(1)} collective-permute-done((bf16[256,512]{1,0:T(8,128)(2,1)S(1)}, bf16[256,512]{1,0:T(8,128)(2,1)S(1)}, u32[]{:S(2)}, u32[]{:S(2)}) %collective-permute-start.9) | collective-permute-done | bytes 262176 | tf_op jit(solution)/shard_map/ppermute | solution.py:443
  24.0 2.1 %collective-permute-start.10 = (bf16[256,512]{1,0:T(8,128)(2,1)S(1)}, bf16[256,512]{1,0:T(8,128)(2,1)S(1)}, u32[]{:S(2)}, u32[]{:S(2)}) collective-permute-start(bf16[256,512]{1,0:T(8,128)(2,1)S(1)} %collective-permute-done.9.refs_4_), channel_id=1, source_target_pairs={{0,4},{1,3},{2,0},{3,7},{4,8},{5,1},{6,2},{7,11},{8,12},{9,5},{10,... | collective-permute-start | bytes 786440 | tf_op jit(solution)/shard_map/ppermute | solution.py:443
  26.2 1.4 %collective-permute-done.12.refs_5_ = bf16[256,512]{1,0:T(8,128)(2,1)S(1)} collective-permute-done((bf16[256,512]{1,0:T(8,128)(2,1)S(1)}, bf16[256,512]{1,0:T(8,128)(2,1)S(1)}, u32[]{:S(2)}, u32[]{:S(2)}) %collective-permute-start.12) | collective-permute-done | bytes 262176 | tf_op jit(solution)/shard_map/ppermute | solution.py:444
  27.5 2.1 %collective-permute-start.13 = (bf16[256,512]{1,0:T(8,128)(2,1)S(1)}, bf16[256,512]{1,0:T(8,128)(2,1)S(1)}, u32[]{:S(2)}, u32[]{:S(2)}) collective-permute-start(bf16[256,512]{1,0:T(8,128)(2,1)S(1)} %collective-permute-done.12.refs_5_), channel_id=1, source_target_pairs={{0,4},{1,3},{2,0},{3,7},{4,8},{5,1},{6,2},{7,11},{8,12},{9,5},{10,... | collective-permute-start | bytes 786440 | tf_op jit(solution)/shard_map/ppermute | solution.py:444
  29.6 0.7 %collective-permute-done.10.refs_0_ = bf16[256,512]{1,0:T(8,128)(2,1)S(1)} collective-permute-done((bf16[256,512]{1,0:T(8,128)(2,1)S(1)}, bf16[256,512]{1,0:T(8,128)(2,1)S(1)}, u32[]{:S(2)}, u32[]{:S(2)}) %collective-permute-start.10) | collective-permute-done | bytes 262176 | tf_op jit(solution)/shard_map/ppermute | solution.py:443
  30.3 2.1 %collective-permute-start.16 = (bf16[256,512]{1,0:T(8,128)(2,1)S(1)}, bf16[256,512]{1,0:T(8,128)(2,1)S(1)}, u32[]{:S(2)}, u32[]{:S(2)}) collective-permute-start(bf16[256,512]{1,0:T(8,128)(2,1)S(1)} %collective-permute-done.10.refs_0_), channel_id=1, source_target_pairs={{0,4},{1,3},{2,0},{3,7},{4,8},{5,1},{6,2},{7,11},{8,12},{9,5},{10,... | collective-permute-start | bytes 786440 | tf_op jit(solution)/shard_map/ppermute | solution.py:446
  32.4 1.5 %collective-permute-start.3 = (bf16[2,128,256]{2,1,0:T(8,128)(2,1)S(1)}, bf16[2,128,256]{2,1,0:T(8,128)(2,1)S(1)}, u32[]{:S(2)}, u32[]{:S(2)}) collective-permute-start(bf16[2,128,256]{2,1,0:T(8,128)(2,1)S(1)} %get-tuple-element.39), channel_id=1, source_target_pairs={{0,16},{16,0},{1,17},{17,1},{2,18},{18,2},{3,19},{19,3},{4,20},{20... | collective-permute-start | bytes 393224 | tf_op jit(solution)/shard_map/ppermute | solution.py:427
  33.9 0.5 %collective-permute-start.15 = (bf16[256,512]{1,0:T(8,128)(2,1)S(1)}, bf16[256,512]{1,0:T(8,128)(2,1)S(1)}, u32[]{:S(2)}, u32[]{:S(2)}) collective-permute-start(bf16[256,512]{1,0:T(8,128)(2,1)S(1)} %collective-permute-done.13.refs_1_), channel_id=1, source_target_pairs={{0,1},{1,0},{2,3},{3,2},{4,5},{5,4},{6,7},{7,6},{8,9},{9,8},{10,11... | collective-permute-start | bytes 786440 | tf_op jit(solution)/shard_map/ppermute | solution.py:445
  34.4 0.7 %shard_map.92.refs_4_ = f32[256,512]{1,0:T(8,128)S(1)} custom-call(bf16[14,128,256]{2,1,0:T(8,128)(2,1)S(1)} %get-tuple-element.41.own, bf16[16,128,256]{2,1,0:T(8,128)(2,1)S(1)} %collective-permute-done.2.packed.other, bf16[256,512]{1,0:T(8,128)(2,1)S(1)} %shard_map.91.refs_0_, bf16[256,512]{1,0:T(8,128)(2,1)S(1)} %collective-permute-done.11.refs_1_, ...), custom_call_target="tpu_custom_call" | custom-call | flops 536870912 | bytes 3145728 | tf_op jit(solution)/shard_map/pallas_call | solution.py:361
  35.1 1.6 %collective-permute-done.16.refs_0_ = bf16[256,512]{1,0:T(8,128)(2,1)S(1)} collective-permute-done((bf16[256,512]{1,0:T(8,128)(2,1)S(1)}, bf16[256,512]{1,0:T(8,128)(2,1)S(1)}, u32[]{:S(2)}, u32[]{:S(2)}) %collective-permute-start.16) | collective-permute-done | bytes 262176 | tf_op jit(solution)/shard_map/ppermute | solution.py:446
  36.7 0.6 %collective-permute-done.3.more = bf16[2,128,256]{2,1,0:T(8,128)(2,1)S(1)} collective-permute-done((bf16[2,128,256]{2,1,0:T(8,128)(2,1)S(1)}, bf16[2,128,256]{2,1,0:T(8,128)(2,1)S(1)}, u32[]{:S(2)}, u32[]{:S(2)}) %collective-permute-start.3) | collective-permute-done | bytes 131104 | tf_op jit(solution)/shard_map/ppermute | solution.py:427
  37.4 0.6 %shard_map.84.refs_1_ = bf16[256,512]{1,0:T(8,128)(2,1)S(1)} custom-call(bf16[256,512]{1,0:T(8,128)(2,1)S(1)} %shard_map.82.first.there_a, bf16[256,512]{1,0:T(8,128)(2,1)S(1)} %shard_map.83.second.there_b, f32[512,512]{1,0:T(8,128)S(1)} %copy-done, f32[512,512]{1,0:T(8,128)S(1)} %copy-done.1, f32[64,128]{1,0:T(8,128)S(1)} %bitcast.5), custom_call_target="tpu_custom_call" | custom-call | flops 3932160 | bytes 1835008 | tf_op jit(solution)/shard_map/pallas_call | solution.py:285
  38.1 0.4 shard_map.93.early
  38.5 0.3 shard_map.94
  38.8 1.9 %collective-permute-start.22 = (bf16[128,512]{1,0:T(8,128)(2,1)S(1)}, bf16[128,512]{1,0:T(8,128)(2,1)S(1)}, u32[]{:S(2)}, u32[]{:S(2)}) collective-permute-start(bf16[128,512]{1,0:T(8,128)(2,1)S(1)} %get-tuple-element.45), channel_id=1, source_target_pairs={{0,16},{16,0},{1,17},{17,1},{2,18},{18,2},{3,19},{19,3},{4,20},{20... | collective-permute-start | bytes 393224 | tf_op jit(solution)/shard_map/ppermute | solution.py:459
  40.8 2.3 %shard_map.97 = (f32[512,512]{1,0:T(8,128)}, f32[512,512]{1,0:T(8,128)}) custom-call(bf16[256,512]{1,0:T(8,128)(2,1)S(1)} %shard_map.76.grad.own.here_a, bf16[256,512]{1,0:T(8,128)(2,1)S(1)} %shard_map.96.here_b, bf16[256,512]{1,0:T(8,128)(2,1)S(1)} %shard_map.82.first.there_a, bf16[256,512]{1,0:T(8,128)(2,1)S(1)} %shard_map.83.second.there_b, ...), custom_call_target="tpu_custom_call" | custom-call | flops 7864320 | bytes 5242880 | tf_op jit(solution)/shard_map/pallas_call | solution.py:314
  43.4 1.4 %collective-permute-done.22.other_part = bf16[128,512]{1,0:T(8,128)(2,1)S(1)} collective-permute-done((bf16[128,512]{1,0:T(8,128)(2,1)S(1)}, bf16[128,512]{1,0:T(8,128)(2,1)S(1)}, u32[]{:S(2)}, u32[]{:S(2)}) %collective-permute-start.22) | collective-permute-done | bytes 131104 | tf_op jit(solution)/shard_map/ppermute | solution.py:459
  44.8 0.7 %shard_map.95 = bf16[128,512]{1,0:T(8,128)(2,1)} custom-call(f32[128,512]{1,0:T(8,128)S(1)} %shard_map.88.own_part, f32[128,512]{1,0:T(8,128)S(1)} %get-tuple-element.44.mine_part, bf16[128,512]{1,0:T(8,128)(2,1)S(1)} %collective-permute-done.22.other_part, f32[128,1]{1,0:T(8,128)S(1)} %get-tuple-element.46.inverse), custom_call_target="tpu_custom_call" | custom-call | tf_op jit(solution)/shard_map/pallas_call | solution.py:403
  (46 shorter events, 1.5 us)
Async XLA Ops:
  0.6 1.2 %copy-start.2 = (f32[1,512,512]{2,1,0:T(8,128)S(1)}, f32[1,512,512]{2,1,0:T(8,128)}, u32[]{:S(2)}) copy-start(f32[1,512,512]{2,1,0:T(8,128)} %param.9) | copy-start | bytes 3145732
  1.9 3.2 %copy-start.3 = (bf16[128,8192]{1,0:T(8,128)(2,1)S(1)}, bf16[128,8192]{1,0:T(8,128)(2,1)}, u32[]{:S(2)}) copy-start(bf16[128,8192]{1,0:T(8,128)(2,1)} %tokens.1) | copy-start | bytes 6291460
  1.9 5.9 %copy-start = (f32[512,512]{1,0:T(8,128)S(1)}, f32[512,512]{1,0:T(8,128)}, u32[]{:S(2)}) copy-start(f32[512,512]{1,0:T(8,128)} %master.5) | copy-start | bytes 3145732
  1.9 5.9 %copy-start.1 = (f32[512,512]{1,0:T(8,128)S(1)}, f32[512,512]{1,0:T(8,128)}, u32[]{:S(2)}) copy-start(f32[512,512]{1,0:T(8,128)} %momentum.5) | copy-start | bytes 3145732
  1.9 5.9 %copy-start.4 = (f32[8192]{0:T(1024)S(1)}, f32[8192]{0:T(1024)}, u32[]{:S(2)}) copy-start(f32[8192]{0:T(1024)} %param.6) | copy-start | bytes 98308
  1.9 7.4 %collective-permute-start.1 = (bf16[128,512]{1,0:T(8,128)(2,1)S(1)}, bf16[128,512]{1,0:T(8,128)(2,1)S(1)}, u32[]{:S(2)}, u32[]{:S(2)}) collective-permute-start(bf16[128,512]{1,0:T(8,128)(2,1)S(1)} %get-tuple-element.28.refs_0_), channel_id=1, source_target_pairs={{0,16},{16,0},{1,17},{17,1},{2,18},{18,2},{3,19},{19,3},{4,20},{20... | collective-permute-start | bytes 393224 | tf_op jit(solution)/shard_map/ppermute | solution.py:422
  5.0 7.1 %collective-permute-start = (bf16[128,512]{1,0:T(8,128)(2,1)S(1)}, bf16[128,512]{1,0:T(8,128)(2,1)S(1)}, u32[]{:S(2)}, u32[]{:S(2)}) collective-permute-start(bf16[128,512]{1,0:T(8,128)(2,1)S(1)} %get-tuple-element.27.refs_1_), channel_id=1, source_target_pairs={{0,16},{16,0},{1,17},{17,1},{2,18},{18,2},{3,19},{19,3},{4,20},{20... | collective-permute-start | bytes 393224 | tf_op jit(solution)/shard_map/ppermute | solution.py:422
  5.8 28.6 %collective-permute-start.2 = (bf16[16,128,256]{2,1,0:T(8,128)(2,1)S(1)}, bf16[16,128,256]{2,1,0:T(8,128)(2,1)S(1)}, u32[]{:S(2)}, u32[]{:S(2)}) collective-permute-start(bf16[16,128,256]{2,1,0:T(8,128)(2,1)S(1)} %get-tuple-element.38), channel_id=1, source_target_pairs={{0,16},{16,0},{1,17},{17,1},{2,18},{18,2},{3,19},{19,3},{4,20},{20... | collective-permute-start | bytes 3145736 | tf_op jit(solution)/shard_map/ppermute | solution.py:427
  9.5 5.1 %collective-permute-start.7 = (bf16[128,512]{1,0:T(8,128)(2,1)S(1)}, bf16[128,512]{1,0:T(8,128)(2,1)S(1)}, u32[]{:S(2)}, u32[]{:S(2)}) collective-permute-start(bf16[128,512]{1,0:T(8,128)(2,1)S(1)} %shard_map.80.done), channel_id=1, source_target_pairs={{0,4},{1,3},{2,0},{3,7},{4,8},{5,1},{6,2},{7,11},{8,12},{9,5},{10,... | collective-permute-start | bytes 393224 | tf_op jit(solution)/shard_map/ppermute | solution.py:438
  11.7 2.9 %collective-permute-start.4 = (bf16[128,512]{1,0:T(8,128)(2,1)S(1)}, bf16[128,512]{1,0:T(8,128)(2,1)S(1)}, u32[]{:S(2)}, u32[]{:S(2)}) collective-permute-start(bf16[128,512]{1,0:T(8,128)(2,1)S(1)} %shard_map.80.done), channel_id=1, source_target_pairs={{0,1},{1,0},{2,3},{3,2},{4,5},{5,4},{6,7},{7,6},{8,9},{9,8},{10,11... | collective-permute-start | bytes 393224 | tf_op jit(solution)/shard_map/ppermute | solution.py:431
  12.3 2.3 %collective-permute-start.5 = (bf16[128,512]{1,0:T(8,128)(2,1)S(1)}, bf16[128,512]{1,0:T(8,128)(2,1)S(1)}, u32[]{:S(2)}, u32[]{:S(2)}) collective-permute-start(bf16[128,512]{1,0:T(8,128)(2,1)S(1)} %get-tuple-element.40), channel_id=1, source_target_pairs={{0,1},{1,0},{2,3},{3,2},{4,5},{5,4},{6,7},{7,6},{8,9},{9,8},{10,11... | collective-permute-start | bytes 393224 | tf_op jit(solution)/shard_map/ppermute | solution.py:434
  12.5 5.0 %collective-permute-start.8 = (bf16[128,512]{1,0:T(8,128)(2,1)S(1)}, bf16[128,512]{1,0:T(8,128)(2,1)S(1)}, u32[]{:S(2)}, u32[]{:S(2)}) collective-permute-start(bf16[128,512]{1,0:T(8,128)(2,1)S(1)} %get-tuple-element.40), channel_id=1, source_target_pairs={{0,4},{1,3},{2,0},{3,7},{4,8},{5,1},{6,2},{7,11},{8,12},{9,5},{10,... | collective-permute-start | bytes 393224 | tf_op jit(solution)/shard_map/ppermute | solution.py:441
  14.7 6.4 %collective-permute-start.11 = (bf16[256,512]{1,0:T(8,128)(2,1)S(1)}, bf16[256,512]{1,0:T(8,128)(2,1)S(1)}, u32[]{:S(2)}, u32[]{:S(2)}) collective-permute-start(bf16[256,512]{1,0:T(8,128)(2,1)S(1)} %shard_map.87.refs_2_), channel_id=1, source_target_pairs={{0,4},{1,3},{2,0},{3,7},{4,8},{5,1},{6,2},{7,11},{8,12},{9,5},{10,... | collective-permute-start | bytes 786440 | tf_op jit(solution)/shard_map/ppermute | solution.py:444
  17.5 6.4 %collective-permute-start.9 = (bf16[256,512]{1,0:T(8,128)(2,1)S(1)}, bf16[256,512]{1,0:T(8,128)(2,1)S(1)}, u32[]{:S(2)}, u32[]{:S(2)}) collective-permute-start(bf16[256,512]{1,0:T(8,128)(2,1)S(1)} %shard_map.91.refs_0_), channel_id=1, source_target_pairs={{0,4},{1,3},{2,0},{3,7},{4,8},{5,1},{6,2},{7,11},{8,12},{9,5},{10,... | collective-permute-start | bytes 786440 | tf_op jit(solution)/shard_map/ppermute | solution.py:443
  19.6 6.4 %collective-permute-start.17 = (bf16[256,512]{1,0:T(8,128)(2,1)S(1)}, bf16[256,512]{1,0:T(8,128)(2,1)S(1)}, u32[]{:S(2)}, u32[]{:S(2)}) collective-permute-start(bf16[256,512]{1,0:T(8,128)(2,1)S(1)} %shard_map.91.refs_0_), channel_id=1, source_target_pairs={{0,1},{1,0},{2,3},{3,2},{4,5},{5,4},{6,7},{7,6},{8,9},{9,8},{10,11... | collective-permute-start | bytes 786440 | tf_op jit(solution)/shard_map/ppermute | solution.py:445
  21.1 6.4 %collective-permute-start.12 = (bf16[256,512]{1,0:T(8,128)(2,1)S(1)}, bf16[256,512]{1,0:T(8,128)(2,1)S(1)}, u32[]{:S(2)}, u32[]{:S(2)}) collective-permute-start(bf16[256,512]{1,0:T(8,128)(2,1)S(1)} %collective-permute-done.11.refs_1_), channel_id=1, source_target_pairs={{0,4},{1,3},{2,0},{3,7},{4,8},{5,1},{6,2},{7,11},{8,12},{9,5},{10,... | collective-permute-start | bytes 786440 | tf_op jit(solution)/shard_map/ppermute | solution.py:444
  23.9 3.6 %collective-permute-start.19 = (bf16[256,512]{1,0:T(8,128)(2,1)S(1)}, bf16[256,512]{1,0:T(8,128)(2,1)S(1)}, u32[]{:S(2)}, u32[]{:S(2)}) collective-permute-start(bf16[256,512]{1,0:T(8,128)(2,1)S(1)} %collective-permute-done.9.refs_4_), channel_id=1, source_target_pairs={{0,1},{1,0},{2,3},{3,2},{4,5},{5,4},{6,7},{7,6},{8,9},{9,8},{10,11... | collective-permute-start | bytes 786440 | tf_op jit(solution)/shard_map/ppermute | solution.py:445
  24.0 6.4 %collective-permute-start.10 = (bf16[256,512]{1,0:T(8,128)(2,1)S(1)}, bf16[256,512]{1,0:T(8,128)(2,1)S(1)}, u32[]{:S(2)}, u32[]{:S(2)}) collective-permute-start(bf16[256,512]{1,0:T(8,128)(2,1)S(1)} %collective-permute-done.9.refs_4_), channel_id=1, source_target_pairs={{0,4},{1,3},{2,0},{3,7},{4,8},{5,1},{6,2},{7,11},{8,12},{9,5},{10,... | collective-permute-start | bytes 786440 | tf_op jit(solution)/shard_map/ppermute | solution.py:443
  26.0 6.4 %collective-permute-start.18 = (bf16[256,512]{1,0:T(8,128)(2,1)S(1)}, bf16[256,512]{1,0:T(8,128)(2,1)S(1)}, u32[]{:S(2)}, u32[]{:S(2)}) collective-permute-start(bf16[256,512]{1,0:T(8,128)(2,1)S(1)} %collective-permute-done.11.refs_1_), channel_id=1, source_target_pairs={{0,1},{1,0},{2,3},{3,2},{4,5},{5,4},{6,7},{7,6},{8,9},{9,8},{10,11... | collective-permute-start | bytes 786440 | tf_op jit(solution)/shard_map/ppermute | solution.py:445
  27.5 6.4 %collective-permute-start.20 = (bf16[256,512]{1,0:T(8,128)(2,1)S(1)}, bf16[256,512]{1,0:T(8,128)(2,1)S(1)}, u32[]{:S(2)}, u32[]{:S(2)}) collective-permute-start(bf16[256,512]{1,0:T(8,128)(2,1)S(1)} %collective-permute-done.12.refs_5_), channel_id=1, source_target_pairs={{0,1},{1,0},{2,3},{3,2},{4,5},{5,4},{6,7},{7,6},{8,9},{9,8},{10,11... | collective-permute-start | bytes 786440 | tf_op jit(solution)/shard_map/ppermute | solution.py:445
  27.5 6.4 %collective-permute-start.13 = (bf16[256,512]{1,0:T(8,128)(2,1)S(1)}, bf16[256,512]{1,0:T(8,128)(2,1)S(1)}, u32[]{:S(2)}, u32[]{:S(2)}) collective-permute-start(bf16[256,512]{1,0:T(8,128)(2,1)S(1)} %collective-permute-done.12.refs_5_), channel_id=1, source_target_pairs={{0,4},{1,3},{2,0},{3,7},{4,8},{5,1},{6,2},{7,11},{8,12},{9,5},{10,... | collective-permute-start | bytes 786440 | tf_op jit(solution)/shard_map/ppermute | solution.py:444
  30.3 6.4 %collective-permute-start.16 = (bf16[256,512]{1,0:T(8,128)(2,1)S(1)}, bf16[256,512]{1,0:T(8,128)(2,1)S(1)}, u32[]{:S(2)}, u32[]{:S(2)}) collective-permute-start(bf16[256,512]{1,0:T(8,128)(2,1)S(1)} %collective-permute-done.10.refs_0_), channel_id=1, source_target_pairs={{0,4},{1,3},{2,0},{3,7},{4,8},{5,1},{6,2},{7,11},{8,12},{9,5},{10,... | collective-permute-start | bytes 786440 | tf_op jit(solution)/shard_map/ppermute | solution.py:446
  32.4 5.0 %collective-permute-start.3 = (bf16[2,128,256]{2,1,0:T(8,128)(2,1)S(1)}, bf16[2,128,256]{2,1,0:T(8,128)(2,1)S(1)}, u32[]{:S(2)}, u32[]{:S(2)}) collective-permute-start(bf16[2,128,256]{2,1,0:T(8,128)(2,1)S(1)} %get-tuple-element.39), channel_id=1, source_target_pairs={{0,16},{16,0},{1,17},{17,1},{2,18},{18,2},{3,19},{19,3},{4,20},{20... | collective-permute-start | bytes 393224 | tf_op jit(solution)/shard_map/ppermute | solution.py:427
  33.9 4.1 %collective-permute-start.14 = (bf16[256,512]{1,0:T(8,128)(2,1)S(1)}, bf16[256,512]{1,0:T(8,128)(2,1)S(1)}, u32[]{:S(2)}, u32[]{:S(2)}) collective-permute-start(bf16[256,512]{1,0:T(8,128)(2,1)S(1)} %collective-permute-done.10.refs_0_), channel_id=1, source_target_pairs={{0,1},{1,0},{2,3},{3,2},{4,5},{5,4},{6,7},{7,6},{8,9},{9,8},{10,11... | collective-permute-start | bytes 786440 | tf_op jit(solution)/shard_map/ppermute | solution.py:445
  33.9 4.1 %collective-permute-start.15 = (bf16[256,512]{1,0:T(8,128)(2,1)S(1)}, bf16[256,512]{1,0:T(8,128)(2,1)S(1)}, u32[]{:S(2)}, u32[]{:S(2)}) collective-permute-start(bf16[256,512]{1,0:T(8,128)(2,1)S(1)} %collective-permute-done.13.refs_1_), channel_id=1, source_target_pairs={{0,1},{1,0},{2,3},{3,2},{4,5},{5,4},{6,7},{7,6},{8,9},{9,8},{10,11... | collective-permute-start | bytes 786440 | tf_op jit(solution)/shard_map/ppermute | solution.py:445
  36.7 1.8 %collective-permute-start.21 = (bf16[256,512]{1,0:T(8,128)(2,1)S(1)}, bf16[256,512]{1,0:T(8,128)(2,1)S(1)}, u32[]{:S(2)}, u32[]{:S(2)}) collective-permute-start(bf16[256,512]{1,0:T(8,128)(2,1)S(1)} %collective-permute-done.16.refs_0_), channel_id=1, source_target_pairs={{0,1},{1,0},{2,3},{3,2},{4,5},{5,4},{6,7},{7,6},{8,9},{9,8},{10,11... | collective-permute-start | bytes 786440 | tf_op jit(solution)/shard_map/ppermute | solution.py:450
  38.0 5.1 %collective-permute-start.6 = (bf16[256,512]{1,0:T(8,128)(2,1)S(1)}, bf16[256,512]{1,0:T(8,128)(2,1)S(1)}, u32[]{:S(2)}, u32[]{:S(2)}) collective-permute-start(bf16[256,512]{1,0:T(8,128)(2,1)S(1)} %shard_map.84.refs_1_), channel_id=1, source_target_pairs={{0,1},{1,0},{2,3},{3,2},{4,5},{5,4},{6,7},{7,6},{8,9},{9,8},{10,11... | collective-permute-start | bytes 786440 | tf_op jit(solution)/shard_map/ppermute | solution.py:455
  38.8 5.9 %collective-permute-start.22 = (bf16[128,512]{1,0:T(8,128)(2,1)S(1)}, bf16[128,512]{1,0:T(8,128)(2,1)S(1)}, u32[]{:S(2)}, u32[]{:S(2)}) collective-permute-start(bf16[128,512]{1,0:T(8,128)(2,1)S(1)} %get-tuple-element.45), channel_id=1, source_target_pairs={{0,16},{16,0},{1,17},{17,1},{2,18},{18,2},{3,19},{19,3},{4,20},{20... | collective-permute-start | bytes 393224 | tf_op jit(solution)/shard_map/ppermute | solution.py:459

commit v8 on v6

--- a/solution.py
+++ b/solution.py
@@ -349,11 +349,12 @@
 
 
 def early_kernel(start, count, own, other, *refs):
-    blocks, total = refs[:count], refs[-1]
-    total[...] = refs[count][...] if len(refs) > count + 1 else jnp.zeros(total.shape, jnp.float32)
+    blocks, out = refs[:count], refs[-1]
+    total = refs[count][...] if len(refs) > count + 1 else jnp.zeros(out.shape, jnp.float32)
     for k, block in enumerate(blocks):
         left = jnp.concatenate([own[start + k], other[start + k]], axis=0)
-        total[...] += jnp.dot(left, block[...], preferred_element_type=jnp.float32)
+        total += jnp.dot(left, block[...], preferred_element_type=jnp.float32)
+    out[...] = total
 
 
 def dot_early(start, own, other, blocks, *total):

time: 45.7 us -> 45.7 us (level)
  no operation moved by 1% of the time
where the time goes in v8:
time: 45.7 us; the launch traced here: 45.6 us
  starting transfers between devices  26.2 us (57%)
  waiting for transfers between devices  10.2 us (22%)
  Pallas kernels  7.06 us (15%)
  local copies, waits for them, and re-layouts  1.24 us (3%)
  between operations  0.85 us (2%)
    ppermute x3, starting transfers between devices, by_permutes(): a = ring(a)  6.25 us
    ppermute x3, starting transfers between devices, by_permutes(): b = ring(b)  6.22 us
    ppermute x2, starting transfers between devices, by_permutes(): other, more = (cross(sent), cross(more))  3.52 us
    ppermute x2, starting transfers between devices, by_permutes(): here_parts = [cross(part) for part in sent_parts]  3.11 us
    ppermute x3, waiting for transfers between devices, by_permutes(): a = ring(a)  3.07 us
    ppermute x3, waiting for transfers between devices, by_permutes(): b = ring(b)  2.86 us
    pallas_call x1, Pallas kernels, sync_outer(): pl.pallas_call(outer_kernel, in_specs=[VMEM] * 6, out_specs=[VMEM] * 2, o...  2.28 us
    ppermute x1, starting transfers between devices, by_permutes(): arrived = ring(head)  2.17 us
  transfers between devices with their start and end apart: 23, of which 10 were waited for; matrix products, arithmetic and copies ran while one was open for 0% of the time, Pallas kernels for 14%

profile of v8, /device:TPU:0, one launch (start us, length us, event | category | flops | bytes accessed | tf_op | source)
XLA Modules:
  0.0 45.6 jit_solution(12052069072137967182)
XLA Ops:
  0.6 1.2 %copy-done.2 = f32[1,512,512]{2,1,0:T(8,128)S(1)} copy-done((f32[1,512,512]{2,1,0:T(8,128)S(1)}, f32[1,512,512]{2,1,0:T(8,128)}, u32[]{:S(2)}) %copy-start.2) | copy-done | bytes 1048600
  1.9 3.0 %collective-permute-start.1 = (bf16[128,512]{1,0:T(8,128)(2,1)S(1)}, bf16[128,512]{1,0:T(8,128)(2,1)S(1)}, u32[]{:S(2)}, u32[]{:S(2)}) collective-permute-start(bf16[128,512]{1,0:T(8,128)(2,1)S(1)} %get-tuple-element.28.refs_0_), channel_id=1, source_target_pairs={{0,16},{16,0},{1,17},{17,1},{2,18},{18,2},{3,19},{19,3},{4,20},{20... | collective-permute-start | bytes 393224 | tf_op jit(solution)/shard_map/ppermute | solution.py:423
  5.1 0.7 %shard_map.77 = (bf16[14,128,256]{2,1,0:T(8,128)(2,1)S(1)}, bf16[16,128,256]{2,1,0:T(8,128)(2,1)S(1)}, bf16[2,128,256]{2,1,0:T(8,128)(2,1)S(1)}, bf16[4,128,256]{2,1,0:T(8,128)(2,1)S(1)}, f32[128,1]{1,0:T(8,128)S(1)}) custom-call(bf16[128,8192]{1,0:T(8,128)(2,1)S(1)} %copy-done.3, bf16[256,512]{1,0:T(8,128)(2,1)S(1)} %shard_map.76.grad.own.here_a), custom_call_target="tpu_custom_call" | custom-call | flops 2097152 | bytes 4194304 | tf_op jit(solution)/shard_map/pallas_call | solution.py:157
  5.8 2.0 %collective-permute-start.2 = (bf16[16,128,256]{2,1,0:T(8,128)(2,1)S(1)}, bf16[16,128,256]{2,1,0:T(8,128)(2,1)S(1)}, u32[]{:S(2)}, u32[]{:S(2)}) collective-permute-start(bf16[16,128,256]{2,1,0:T(8,128)(2,1)S(1)} %get-tuple-element.38), channel_id=1, source_target_pairs={{0,16},{16,0},{1,17},{17,1},{2,18},{18,2},{3,19},{19,3},{4,20},{20... | collective-permute-start | bytes 3145736 | tf_op jit(solution)/shard_map/ppermute | solution.py:428
  7.8 0.3 shard_map.79
  8.1 1.2 %collective-permute-done.1.here.refs_0_ = bf16[128,512]{1,0:T(8,128)(2,1)S(1)} collective-permute-done((bf16[128,512]{1,0:T(8,128)(2,1)S(1)}, bf16[128,512]{1,0:T(8,128)(2,1)S(1)}, u32[]{:S(2)}, u32[]{:S(2)}) %collective-permute-start.1) | collective-permute-done | bytes 131104 | tf_op jit(solution)/shard_map/ppermute | solution.py:423
  9.5 2.2 %collective-permute-start.7 = (bf16[128,512]{1,0:T(8,128)(2,1)S(1)}, bf16[128,512]{1,0:T(8,128)(2,1)S(1)}, u32[]{:S(2)}, u32[]{:S(2)}) collective-permute-start(bf16[128,512]{1,0:T(8,128)(2,1)S(1)} %shard_map.80.done), channel_id=1, source_target_pairs={{0,4},{1,3},{2,0},{3,7},{4,8},{5,1},{6,2},{7,11},{8,12},{9,5},{10,... | collective-permute-start | bytes 393224 | tf_op jit(solution)/shard_map/ppermute | solution.py:439
  11.7 0.4 collective-permute-done.here.refs_1_
  12.5 2.1 %collective-permute-start.8 = (bf16[128,512]{1,0:T(8,128)(2,1)S(1)}, bf16[128,512]{1,0:T(8,128)(2,1)S(1)}, u32[]{:S(2)}, u32[]{:S(2)}) collective-permute-start(bf16[128,512]{1,0:T(8,128)(2,1)S(1)} %get-tuple-element.40), channel_id=1, source_target_pairs={{0,4},{1,3},{2,0},{3,7},{4,8},{5,1},{6,2},{7,11},{8,12},{9,5},{10,... | collective-permute-start | bytes 393224 | tf_op jit(solution)/shard_map/ppermute | solution.py:442
  14.7 2.1 %collective-permute-start.11 = (bf16[256,512]{1,0:T(8,128)(2,1)S(1)}, bf16[256,512]{1,0:T(8,128)(2,1)S(1)}, u32[]{:S(2)}, u32[]{:S(2)}) collective-permute-start(bf16[256,512]{1,0:T(8,128)(2,1)S(1)} %shard_map.87.refs_2_), channel_id=1, source_target_pairs={{0,4},{1,3},{2,0},{3,7},{4,8},{5,1},{6,2},{7,11},{8,12},{9,5},{10,... | collective-permute-start | bytes 786440 | tf_op jit(solution)/shard_map/ppermute | solution.py:445
  16.8 0.7 %collective-permute-done.8.refs_1_ = bf16[128,512]{1,0:T(8,128)(2,1)S(1)} collective-permute-done((bf16[128,512]{1,0:T(8,128)(2,1)S(1)}, bf16[128,512]{1,0:T(8,128)(2,1)S(1)}, u32[]{:S(2)}, u32[]{:S(2)}) %collective-permute-start.8) | collective-permute-done | bytes 131104 | tf_op jit(solution)/shard_map/ppermute | solution.py:442
  17.5 2.1 %collective-permute-start.9 = (bf16[256,512]{1,0:T(8,128)(2,1)S(1)}, bf16[256,512]{1,0:T(8,128)(2,1)S(1)}, u32[]{:S(2)}, u32[]{:S(2)}) collective-permute-start(bf16[256,512]{1,0:T(8,128)(2,1)S(1)} %shard_map.91.refs_0_), channel_id=1, source_target_pairs={{0,4},{1,3},{2,0},{3,7},{4,8},{5,1},{6,2},{7,11},{8,12},{9,5},{10,... | collective-permute-start | bytes 786440 | tf_op jit(solution)/shard_map/ppermute | solution.py:444
  19.6 1.5 %collective-permute-done.11.refs_1_ = bf16[256,512]{1,0:T(8,128)(2,1)S(1)} collective-permute-done((bf16[256,512]{1,0:T(8,128)(2,1)S(1)}, bf16[256,512]{1,0:T(8,128)(2,1)S(1)}, u32[]{:S(2)}, u32[]{:S(2)}) %collective-permute-start.11) | collective-permute-done | bytes 262176 | tf_op jit(solution)/shard_map/ppermute | solution.py:445
  21.1 2.1 %collective-permute-start.12 = (bf16[256,512]{1,0:T(8,128)(2,1)S(1)}, bf16[256,512]{1,0:T(8,128)(2,1)S(1)}, u32[]{:S(2)}, u32[]{:S(2)}) collective-permute-start(bf16[256,512]{1,0:T(8,128)(2,1)S(1)} %collective-permute-done.11.refs_1_), channel_id=1, source_target_pairs={{0,4},{1,3},{2,0},{3,7},{4,8},{5,1},{6,2},{7,11},{8,12},{9,5},{10,... | collective-permute-start | bytes 786440 | tf_op jit(solution)/shard_map/ppermute | solution.py:445
  23.2 0.8 %collective-permute-done.9.refs_4_ = bf16[256,512]{1,0:T(8,128)(2,1)S(1)} collective-permute-done((bf16[256,512]{1,0:T(8,128)(2,1)S(1)}, bf16[256,512]{1,0:T(8,128)(2,1)S(1)}, u32[]{:S(2)}, u32[]{:S(2)}) %collective-permute-start.9) | collective-permute-done | bytes 262176 | tf_op jit(solution)/shard_map/ppermute | solution.py:444
  24.0 2.1 %collective-permute-start.10 = (bf16[256,512]{1,0:T(8,128)(2,1)S(1)}, bf16[256,512]{1,0:T(8,128)(2,1)S(1)}, u32[]{:S(2)}, u32[]{:S(2)}) collective-permute-start(bf16[256,512]{1,0:T(8,128)(2,1)S(1)} %collective-permute-done.9.refs_4_), channel_id=1, source_target_pairs={{0,4},{1,3},{2,0},{3,7},{4,8},{5,1},{6,2},{7,11},{8,12},{9,5},{10,... | collective-permute-start | bytes 786440 | tf_op jit(solution)/shard_map/ppermute | solution.py:444
  26.2 1.4 %collective-permute-done.12.refs_5_ = bf16[256,512]{1,0:T(8,128)(2,1)S(1)} collective-permute-done((bf16[256,512]{1,0:T(8,128)(2,1)S(1)}, bf16[256,512]{1,0:T(8,128)(2,1)S(1)}, u32[]{:S(2)}, u32[]{:S(2)}) %collective-permute-start.12) | collective-permute-done | bytes 262176 | tf_op jit(solution)/shard_map/ppermute | solution.py:445
  27.5 2.1 %collective-permute-start.13 = (bf16[256,512]{1,0:T(8,128)(2,1)S(1)}, bf16[256,512]{1,0:T(8,128)(2,1)S(1)}, u32[]{:S(2)}, u32[]{:S(2)}) collective-permute-start(bf16[256,512]{1,0:T(8,128)(2,1)S(1)} %collective-permute-done.12.refs_5_), channel_id=1, source_target_pairs={{0,4},{1,3},{2,0},{3,7},{4,8},{5,1},{6,2},{7,11},{8,12},{9,5},{10,... | collective-permute-start | bytes 786440 | tf_op jit(solution)/shard_map/ppermute | solution.py:445
  29.6 0.7 %collective-permute-done.10.refs_0_ = bf16[256,512]{1,0:T(8,128)(2,1)S(1)} collective-permute-done((bf16[256,512]{1,0:T(8,128)(2,1)S(1)}, bf16[256,512]{1,0:T(8,128)(2,1)S(1)}, u32[]{:S(2)}, u32[]{:S(2)}) %collective-permute-start.10) | collective-permute-done | bytes 262176 | tf_op jit(solution)/shard_map/ppermute | solution.py:444
  30.3 2.1 %collective-permute-start.16 = (bf16[256,512]{1,0:T(8,128)(2,1)S(1)}, bf16[256,512]{1,0:T(8,128)(2,1)S(1)}, u32[]{:S(2)}, u32[]{:S(2)}) collective-permute-start(bf16[256,512]{1,0:T(8,128)(2,1)S(1)} %collective-permute-done.10.refs_0_), channel_id=1, source_target_pairs={{0,4},{1,3},{2,0},{3,7},{4,8},{5,1},{6,2},{7,11},{8,12},{9,5},{10,... | collective-permute-start | bytes 786440 | tf_op jit(solution)/shard_map/ppermute | solution.py:447
  32.4 1.5 %collective-permute-start.3 = (bf16[2,128,256]{2,1,0:T(8,128)(2,1)S(1)}, bf16[2,128,256]{2,1,0:T(8,128)(2,1)S(1)}, u32[]{:S(2)}, u32[]{:S(2)}) collective-permute-start(bf16[2,128,256]{2,1,0:T(8,128)(2,1)S(1)} %get-tuple-element.39), channel_id=1, source_target_pairs={{0,16},{16,0},{1,17},{17,1},{2,18},{18,2},{3,19},{19,3},{4,20},{20... | collective-permute-start | bytes 393224 | tf_op jit(solution)/shard_map/ppermute | solution.py:428
  33.9 0.5 %collective-permute-start.15 = (bf16[256,512]{1,0:T(8,128)(2,1)S(1)}, bf16[256,512]{1,0:T(8,128)(2,1)S(1)}, u32[]{:S(2)}, u32[]{:S(2)}) collective-permute-start(bf16[256,512]{1,0:T(8,128)(2,1)S(1)} %collective-permute-done.13.refs_1_), channel_id=1, source_target_pairs={{0,1},{1,0},{2,3},{3,2},{4,5},{5,4},{6,7},{7,6},{8,9},{9,8},{10,11... | collective-permute-start | bytes 786440 | tf_op jit(solution)/shard_map/ppermute | solution.py:446
  34.4 0.7 %shard_map.92.refs_4_ = f32[256,512]{1,0:T(8,128)S(1)} custom-call(bf16[14,128,256]{2,1,0:T(8,128)(2,1)S(1)} %get-tuple-element.41.own, bf16[16,128,256]{2,1,0:T(8,128)(2,1)S(1)} %collective-permute-done.2.packed.other, bf16[256,512]{1,0:T(8,128)(2,1)S(1)} %shard_map.91.refs_0_, bf16[256,512]{1,0:T(8,128)(2,1)S(1)} %collective-permute-done.11.refs_1_, ...), custom_call_target="tpu_custom_call" | custom-call | flops 536870912 | bytes 3145728 | tf_op jit(solution)/shard_map/pallas_call | solution.py:362
  35.1 1.6 %collective-permute-done.16.refs_0_ = bf16[256,512]{1,0:T(8,128)(2,1)S(1)} collective-permute-done((bf16[256,512]{1,0:T(8,128)(2,1)S(1)}, bf16[256,512]{1,0:T(8,128)(2,1)S(1)}, u32[]{:S(2)}, u32[]{:S(2)}) %collective-permute-start.16) | collective-permute-done | bytes 262176 | tf_op jit(solution)/shard_map/ppermute | solution.py:447
  36.7 0.6 %collective-permute-done.3.more = bf16[2,128,256]{2,1,0:T(8,128)(2,1)S(1)} collective-permute-done((bf16[2,128,256]{2,1,0:T(8,128)(2,1)S(1)}, bf16[2,128,256]{2,1,0:T(8,128)(2,1)S(1)}, u32[]{:S(2)}, u32[]{:S(2)}) %collective-permute-start.3) | collective-permute-done | bytes 131104 | tf_op jit(solution)/shard_map/ppermute | solution.py:428
  37.4 0.6 %shard_map.84.refs_1_ = bf16[256,512]{1,0:T(8,128)(2,1)S(1)} custom-call(bf16[256,512]{1,0:T(8,128)(2,1)S(1)} %shard_map.82.first.there_a, bf16[256,512]{1,0:T(8,128)(2,1)S(1)} %shard_map.83.second.there_b, f32[512,512]{1,0:T(8,128)S(1)} %copy-done, f32[512,512]{1,0:T(8,128)S(1)} %copy-done.1, f32[64,128]{1,0:T(8,128)S(1)} %bitcast.5), custom_call_target="tpu_custom_call" | custom-call | flops 3932160 | bytes 1835008 | tf_op jit(solution)/shard_map/pallas_call | solution.py:285
  38.1 0.4 shard_map.93.early
  38.6 0.3 shard_map.94
  38.9 1.9 %collective-permute-start.22 = (bf16[128,512]{1,0:T(8,128)(2,1)S(1)}, bf16[128,512]{1,0:T(8,128)(2,1)S(1)}, u32[]{:S(2)}, u32[]{:S(2)}) collective-permute-start(bf16[128,512]{1,0:T(8,128)(2,1)S(1)} %get-tuple-element.45), channel_id=1, source_target_pairs={{0,16},{16,0},{1,17},{17,1},{2,18},{18,2},{3,19},{19,3},{4,20},{20... | collective-permute-start | bytes 393224 | tf_op jit(solution)/shard_map/ppermute | solution.py:460
  40.8 2.3 %shard_map.97 = (f32[512,512]{1,0:T(8,128)}, f32[512,512]{1,0:T(8,128)}) custom-call(bf16[256,512]{1,0:T(8,128)(2,1)S(1)} %shard_map.76.grad.own.here_a, bf16[256,512]{1,0:T(8,128)(2,1)S(1)} %shard_map.96.here_b, bf16[256,512]{1,0:T(8,128)(2,1)S(1)} %shard_map.82.first.there_a, bf16[256,512]{1,0:T(8,128)(2,1)S(1)} %shard_map.83.second.there_b, ...), custom_call_target="tpu_custom_call" | custom-call | flops 7864320 | bytes 5242880 | tf_op jit(solution)/shard_map/pallas_call | solution.py:314
  43.4 1.4 %collective-permute-done.22.other_part = bf16[128,512]{1,0:T(8,128)(2,1)S(1)} collective-permute-done((bf16[128,512]{1,0:T(8,128)(2,1)S(1)}, bf16[128,512]{1,0:T(8,128)(2,1)S(1)}, u32[]{:S(2)}, u32[]{:S(2)}) %collective-permute-start.22) | collective-permute-done | bytes 131104 | tf_op jit(solution)/shard_map/ppermute | solution.py:460
  44.8 0.7 %shard_map.95 = bf16[128,512]{1,0:T(8,128)(2,1)} custom-call(f32[128,512]{1,0:T(8,128)S(1)} %shard_map.88.own_part, f32[128,512]{1,0:T(8,128)S(1)} %get-tuple-element.44.mine_part, bf16[128,512]{1,0:T(8,128)(2,1)S(1)} %collective-permute-done.22.other_part, f32[128,1]{1,0:T(8,128)S(1)} %get-tuple-element.46.inverse), custom_call_target="tpu_custom_call" | custom-call | tf_op jit(solution)/shard_map/pallas_call | solution.py:404
  (46 shorter events, 1.5 us)
Async XLA Ops:
  0.6 1.2 %copy-start.2 = (f32[1,512,512]{2,1,0:T(8,128)S(1)}, f32[1,512,512]{2,1,0:T(8,128)}, u32[]{:S(2)}) copy-start(f32[1,512,512]{2,1,0:T(8,128)} %param.9) | copy-start | bytes 3145732
  1.9 3.2 %copy-start.3 = (bf16[128,8192]{1,0:T(8,128)(2,1)S(1)}, bf16[128,8192]{1,0:T(8,128)(2,1)}, u32[]{:S(2)}) copy-start(bf16[128,8192]{1,0:T(8,128)(2,1)} %tokens.1) | copy-start | bytes 6291460
  1.9 5.9 %copy-start = (f32[512,512]{1,0:T(8,128)S(1)}, f32[512,512]{1,0:T(8,128)}, u32[]{:S(2)}) copy-start(f32[512,512]{1,0:T(8,128)} %master.5) | copy-start | bytes 3145732
  1.9 5.9 %copy-start.1 = (f32[512,512]{1,0:T(8,128)S(1)}, f32[512,512]{1,0:T(8,128)}, u32[]{:S(2)}) copy-start(f32[512,512]{1,0:T(8,128)} %momentum.5) | copy-start | bytes 3145732
  1.9 5.9 %copy-start.4 = (f32[8192]{0:T(1024)S(1)}, f32[8192]{0:T(1024)}, u32[]{:S(2)}) copy-start(f32[8192]{0:T(1024)} %param.6) | copy-start | bytes 98308
  1.9 7.4 %collective-permute-start.1 = (bf16[128,512]{1,0:T(8,128)(2,1)S(1)}, bf16[128,512]{1,0:T(8,128)(2,1)S(1)}, u32[]{:S(2)}, u32[]{:S(2)}) collective-permute-start(bf16[128,512]{1,0:T(8,128)(2,1)S(1)} %get-tuple-element.28.refs_0_), channel_id=1, source_target_pairs={{0,16},{16,0},{1,17},{17,1},{2,18},{18,2},{3,19},{19,3},{4,20},{20... | collective-permute-start | bytes 393224 | tf_op jit(solution)/shard_map/ppermute | solution.py:423
  5.0 7.1 %collective-permute-start = (bf16[128,512]{1,0:T(8,128)(2,1)S(1)}, bf16[128,512]{1,0:T(8,128)(2,1)S(1)}, u32[]{:S(2)}, u32[]{:S(2)}) collective-permute-start(bf16[128,512]{1,0:T(8,128)(2,1)S(1)} %get-tuple-element.27.refs_1_), channel_id=1, source_target_pairs={{0,16},{16,0},{1,17},{17,1},{2,18},{18,2},{3,19},{19,3},{4,20},{20... | collective-permute-start | bytes 393224 | tf_op jit(solution)/shard_map/ppermute | solution.py:423
  5.8 28.6 %collective-permute-start.2 = (bf16[16,128,256]{2,1,0:T(8,128)(2,1)S(1)}, bf16[16,128,256]{2,1,0:T(8,128)(2,1)S(1)}, u32[]{:S(2)}, u32[]{:S(2)}) collective-permute-start(bf16[16,128,256]{2,1,0:T(8,128)(2,1)S(1)} %get-tuple-element.38), channel_id=1, source_target_pairs={{0,16},{16,0},{1,17},{17,1},{2,18},{18,2},{3,19},{19,3},{4,20},{20... | collective-permute-start | bytes 3145736 | tf_op jit(solution)/shard_map/ppermute | solution.py:428
  9.5 5.1 %collective-permute-start.7 = (bf16[128,512]{1,0:T(8,128)(2,1)S(1)}, bf16[128,512]{1,0:T(8,128)(2,1)S(1)}, u32[]{:S(2)}, u32[]{:S(2)}) collective-permute-start(bf16[128,512]{1,0:T(8,128)(2,1)S(1)} %shard_map.80.done), channel_id=1, source_target_pairs={{0,4},{1,3},{2,0},{3,7},{4,8},{5,1},{6,2},{7,11},{8,12},{9,5},{10,... | collective-permute-start | bytes 393224 | tf_op jit(solution)/shard_map/ppermute | solution.py:439
  11.7 2.9 %collective-permute-start.4 = (bf16[128,512]{1,0:T(8,128)(2,1)S(1)}, bf16[128,512]{1,0:T(8,128)(2,1)S(1)}, u32[]{:S(2)}, u32[]{:S(2)}) collective-permute-start(bf16[128,512]{1,0:T(8,128)(2,1)S(1)} %shard_map.80.done), channel_id=1, source_target_pairs={{0,1},{1,0},{2,3},{3,2},{4,5},{5,4},{6,7},{7,6},{8,9},{9,8},{10,11... | collective-permute-start | bytes 393224 | tf_op jit(solution)/shard_map/ppermute | solution.py:432
  12.3 2.3 %collective-permute-start.5 = (bf16[128,512]{1,0:T(8,128)(2,1)S(1)}, bf16[128,512]{1,0:T(8,128)(2,1)S(1)}, u32[]{:S(2)}, u32[]{:S(2)}) collective-permute-start(bf16[128,512]{1,0:T(8,128)(2,1)S(1)} %get-tuple-element.40), channel_id=1, source_target_pairs={{0,1},{1,0},{2,3},{3,2},{4,5},{5,4},{6,7},{7,6},{8,9},{9,8},{10,11... | collective-permute-start | bytes 393224 | tf_op jit(solution)/shard_map/ppermute | solution.py:435
  12.5 5.0 %collective-permute-start.8 = (bf16[128,512]{1,0:T(8,128)(2,1)S(1)}, bf16[128,512]{1,0:T(8,128)(2,1)S(1)}, u32[]{:S(2)}, u32[]{:S(2)}) collective-permute-start(bf16[128,512]{1,0:T(8,128)(2,1)S(1)} %get-tuple-element.40), channel_id=1, source_target_pairs={{0,4},{1,3},{2,0},{3,7},{4,8},{5,1},{6,2},{7,11},{8,12},{9,5},{10,... | collective-permute-start | bytes 393224 | tf_op jit(solution)/shard_map/ppermute | solution.py:442
  14.7 6.4 %collective-permute-start.11 = (bf16[256,512]{1,0:T(8,128)(2,1)S(1)}, bf16[256,512]{1,0:T(8,128)(2,1)S(1)}, u32[]{:S(2)}, u32[]{:S(2)}) collective-permute-start(bf16[256,512]{1,0:T(8,128)(2,1)S(1)} %shard_map.87.refs_2_), channel_id=1, source_target_pairs={{0,4},{1,3},{2,0},{3,7},{4,8},{5,1},{6,2},{7,11},{8,12},{9,5},{10,... | collective-permute-start | bytes 786440 | tf_op jit(solution)/shard_map/ppermute | solution.py:445
  17.5 6.4 %collective-permute-start.9 = (bf16[256,512]{1,0:T(8,128)(2,1)S(1)}, bf16[256,512]{1,0:T(8,128)(2,1)S(1)}, u32[]{:S(2)}, u32[]{:S(2)}) collective-permute-start(bf16[256,512]{1,0:T(8,128)(2,1)S(1)} %shard_map.91.refs_0_), channel_id=1, source_target_pairs={{0,4},{1,3},{2,0},{3,7},{4,8},{5,1},{6,2},{7,11},{8,12},{9,5},{10,... | collective-permute-start | bytes 786440 | tf_op jit(solution)/shard_map/ppermute | solution.py:444
  19.6 6.4 %collective-permute-start.17 = (bf16[256,512]{1,0:T(8,128)(2,1)S(1)}, bf16[256,512]{1,0:T(8,128)(2,1)S(1)}, u32[]{:S(2)}, u32[]{:S(2)}) collective-permute-start(bf16[256,512]{1,0:T(8,128)(2,1)S(1)} %shard_map.91.refs_0_), channel_id=1, source_target_pairs={{0,1},{1,0},{2,3},{3,2},{4,5},{5,4},{6,7},{7,6},{8,9},{9,8},{10,11... | collective-permute-start | bytes 786440 | tf_op jit(solution)/shard_map/ppermute | solution.py:446
  21.1 6.4 %collective-permute-start.12 = (bf16[256,512]{1,0:T(8,128)(2,1)S(1)}, bf16[256,512]{1,0:T(8,128)(2,1)S(1)}, u32[]{:S(2)}, u32[]{:S(2)}) collective-permute-start(bf16[256,512]{1,0:T(8,128)(2,1)S(1)} %collective-permute-done.11.refs_1_), channel_id=1, source_target_pairs={{0,4},{1,3},{2,0},{3,7},{4,8},{5,1},{6,2},{7,11},{8,12},{9,5},{10,... | collective-permute-start | bytes 786440 | tf_op jit(solution)/shard_map/ppermute | solution.py:445
  23.9 3.6 %collective-permute-start.19 = (bf16[256,512]{1,0:T(8,128)(2,1)S(1)}, bf16[256,512]{1,0:T(8,128)(2,1)S(1)}, u32[]{:S(2)}, u32[]{:S(2)}) collective-permute-start(bf16[256,512]{1,0:T(8,128)(2,1)S(1)} %collective-permute-done.9.refs_4_), channel_id=1, source_target_pairs={{0,1},{1,0},{2,3},{3,2},{4,5},{5,4},{6,7},{7,6},{8,9},{9,8},{10,11... | collective-permute-start | bytes 786440 | tf_op jit(solution)/shard_map/ppermute | solution.py:446
  24.0 6.4 %collective-permute-start.10 = (bf16[256,512]{1,0:T(8,128)(2,1)S(1)}, bf16[256,512]{1,0:T(8,128)(2,1)S(1)}, u32[]{:S(2)}, u32[]{:S(2)}) collective-permute-start(bf16[256,512]{1,0:T(8,128)(2,1)S(1)} %collective-permute-done.9.refs_4_), channel_id=1, source_target_pairs={{0,4},{1,3},{2,0},{3,7},{4,8},{5,1},{6,2},{7,11},{8,12},{9,5},{10,... | collective-permute-start | bytes 786440 | tf_op jit(solution)/shard_map/ppermute | solution.py:444
  26.0 6.4 %collective-permute-start.18 = (bf16[256,512]{1,0:T(8,128)(2,1)S(1)}, bf16[256,512]{1,0:T(8,128)(2,1)S(1)}, u32[]{:S(2)}, u32[]{:S(2)}) collective-permute-start(bf16[256,512]{1,0:T(8,128)(2,1)S(1)} %collective-permute-done.11.refs_1_), channel_id=1, source_target_pairs={{0,1},{1,0},{2,3},{3,2},{4,5},{5,4},{6,7},{7,6},{8,9},{9,8},{10,11... | collective-permute-start | bytes 786440 | tf_op jit(solution)/shard_map/ppermute | solution.py:446
  27.5 6.4 %collective-permute-start.20 = (bf16[256,512]{1,0:T(8,128)(2,1)S(1)}, bf16[256,512]{1,0:T(8,128)(2,1)S(1)}, u32[]{:S(2)}, u32[]{:S(2)}) collective-permute-start(bf16[256,512]{1,0:T(8,128)(2,1)S(1)} %collective-permute-done.12.refs_5_), channel_id=1, source_target_pairs={{0,1},{1,0},{2,3},{3,2},{4,5},{5,4},{6,7},{7,6},{8,9},{9,8},{10,11... | collective-permute-start | bytes 786440 | tf_op jit(solution)/shard_map/ppermute | solution.py:446
  27.5 6.4 %collective-permute-start.13 = (bf16[256,512]{1,0:T(8,128)(2,1)S(1)}, bf16[256,512]{1,0:T(8,128)(2,1)S(1)}, u32[]{:S(2)}, u32[]{:S(2)}) collective-permute-start(bf16[256,512]{1,0:T(8,128)(2,1)S(1)} %collective-permute-done.12.refs_5_), channel_id=1, source_target_pairs={{0,4},{1,3},{2,0},{3,7},{4,8},{5,1},{6,2},{7,11},{8,12},{9,5},{10,... | collective-permute-start | bytes 786440 | tf_op jit(solution)/shard_map/ppermute | solution.py:445
  30.3 6.4 %collective-permute-start.16 = (bf16[256,512]{1,0:T(8,128)(2,1)S(1)}, bf16[256,512]{1,0:T(8,128)(2,1)S(1)}, u32[]{:S(2)}, u32[]{:S(2)}) collective-permute-start(bf16[256,512]{1,0:T(8,128)(2,1)S(1)} %collective-permute-done.10.refs_0_), channel_id=1, source_target_pairs={{0,4},{1,3},{2,0},{3,7},{4,8},{5,1},{6,2},{7,11},{8,12},{9,5},{10,... | collective-permute-start | bytes 786440 | tf_op jit(solution)/shard_map/ppermute | solution.py:447
  32.4 5.0 %collective-permute-start.3 = (bf16[2,128,256]{2,1,0:T(8,128)(2,1)S(1)}, bf16[2,128,256]{2,1,0:T(8,128)(2,1)S(1)}, u32[]{:S(2)}, u32[]{:S(2)}) collective-permute-start(bf16[2,128,256]{2,1,0:T(8,128)(2,1)S(1)} %get-tuple-element.39), channel_id=1, source_target_pairs={{0,16},{16,0},{1,17},{17,1},{2,18},{18,2},{3,19},{19,3},{4,20},{20... | collective-permute-start | bytes 393224 | tf_op jit(solution)/shard_map/ppermute | solution.py:428
  33.9 4.2 %collective-permute-start.14 = (bf16[256,512]{1,0:T(8,128)(2,1)S(1)}, bf16[256,512]{1,0:T(8,128)(2,1)S(1)}, u32[]{:S(2)}, u32[]{:S(2)}) collective-permute-start(bf16[256,512]{1,0:T(8,128)(2,1)S(1)} %collective-permute-done.10.refs_0_), channel_id=1, source_target_pairs={{0,1},{1,0},{2,3},{3,2},{4,5},{5,4},{6,7},{7,6},{8,9},{9,8},{10,11... | collective-permute-start | bytes 786440 | tf_op jit(solution)/shard_map/ppermute | solution.py:446
  33.9 4.2 %collective-permute-start.15 = (bf16[256,512]{1,0:T(8,128)(2,1)S(1)}, bf16[256,512]{1,0:T(8,128)(2,1)S(1)}, u32[]{:S(2)}, u32[]{:S(2)}) collective-permute-start(bf16[256,512]{1,0:T(8,128)(2,1)S(1)} %collective-permute-done.13.refs_1_), channel_id=1, source_target_pairs={{0,1},{1,0},{2,3},{3,2},{4,5},{5,4},{6,7},{7,6},{8,9},{9,8},{10,11... | collective-permute-start | bytes 786440 | tf_op jit(solution)/shard_map/ppermute | solution.py:446
  36.7 1.9 %collective-permute-start.21 = (bf16[256,512]{1,0:T(8,128)(2,1)S(1)}, bf16[256,512]{1,0:T(8,128)(2,1)S(1)}, u32[]{:S(2)}, u32[]{:S(2)}) collective-permute-start(bf16[256,512]{1,0:T(8,128)(2,1)S(1)} %collective-permute-done.16.refs_0_), channel_id=1, source_target_pairs={{0,1},{1,0},{2,3},{3,2},{4,5},{5,4},{6,7},{7,6},{8,9},{9,8},{10,11... | collective-permute-start | bytes 786440 | tf_op jit(solution)/shard_map/ppermute | solution.py:451
  38.0 5.1 %collective-permute-start.6 = (bf16[256,512]{1,0:T(8,128)(2,1)S(1)}, bf16[256,512]{1,0:T(8,128)(2,1)S(1)}, u32[]{:S(2)}, u32[]{:S(2)}) collective-permute-start(bf16[256,512]{1,0:T(8,128)(2,1)S(1)} %shard_map.84.refs_1_), channel_id=1, source_target_pairs={{0,1},{1,0},{2,3},{3,2},{4,5},{5,4},{6,7},{7,6},{8,9},{9,8},{10,11... | collective-permute-start | bytes 786440 | tf_op jit(solution)/shard_map/ppermute | solution.py:456
  38.9 5.9 %collective-permute-start.22 = (bf16[128,512]{1,0:T(8,128)(2,1)S(1)}, bf16[128,512]{1,0:T(8,128)(2,1)S(1)}, u32[]{:S(2)}, u32[]{:S(2)}) collective-permute-start(bf16[128,512]{1,0:T(8,128)(2,1)S(1)} %get-tuple-element.45), channel_id=1, source_target_pairs={{0,16},{16,0},{1,17},{17,1},{2,18},{18,2},{3,19},{19,3},{4,20},{20... | collective-permute-start | bytes 393224 | tf_op jit(solution)/shard_map/ppermute | solution.py:460
